TPU v7x, 128 devices: a whole 4x4x4 slice. The times are simulated.
128 devices in a mesh: blk: 16 (over y_lo, z, core), col: 8 (over y_hi, x).
Axes of the slice: x: 4, y: 4 (y_hi: 2, y_lo: 2; y = y_hi * 2 + y_lo), z: 4, core: 2. Of those that a mesh axis runs over, the one named last changes fastest.
Arguments:
- features: bfloat16 [384, 256, 256], P('blk', 'col'), may hold values from -6 to 6
- cotangent: bfloat16 [384, 256, 256], P('blk', 'col'), may hold values from -6 to 6
- w_self: bfloat16 [256, 256], replicated, may hold values from -0.375 to 0.375
- w_neigh: bfloat16 [256, 256], replicated, may hold values from -0.375 to 0.375
- tile_row: int32 [2048], P('blk'), may hold values from 0 to 23
- tile_owner: int32 [2048, 1], P('blk'), may hold values from 0 to 15; in each aligned block of 128 rows (0 to 127, 128 to 255, ...) at most 12 rows name the same one
- tile_col: int32 [2048], P('blk'), may hold values from 0 to 23
- tile_count: int32 [16], P('blk'), may hold values from 96 to 128, as said below
- edge_dst: int32 [2048, 640], P('blk'), may hold values from 0 to 255
- edge_src: int32 [2048, 640], P('blk'), may hold values from 0 to 255
Outputs:
- hidden: bfloat16 [384, 256, 256], P('blk', 'col')
- input_grad: bfloat16 [384, 256, 256], P('blk', 'col')
- self_grad: float32 [256, 256], P('col')
- neigh_grad: float32 [256, 256], P('col')
Inputs may be any that keep to these rules, and one draw needn't show every extreme that they name: `tile_owner`: among the 128 slots of one index of blk, no owner is named more than 12 times. `tile_count`: every index of blk keeps all 128 or three quarters of its slots live, always the first ones; some index keeps all.
All inputs are finite; a program needn't handle non-finite values.
Results may differ from a plain program's by a relative error of at most 0.007.
Values may be sent and summed in bfloat16 or wider, within the bound.
No kernel may reach another device: no remote copies, remote signals or barrier semaphores. Data moves between devices by JAX's collectives and lax.ppermute only.
A program may use at most 128 MiB of HBM per device.

v0:
```python
import math

import jax
import jax.numpy as jnp
from jax import lax
from jax.sharding import PartitionSpec as P

highest = lax.Precision.HIGHEST


def edge_tables(src_ids, dst_ids, tile_alive, tile_width):
    lane_index = jnp.arange(tile_width, dtype=jnp.int32)
    spread = (src_ids[..., None] == lane_index).astype(jnp.bfloat16)
    collect = ((dst_ids[..., None] == lane_index) & tile_alive[:, None, None]).astype(jnp.bfloat16)
    return (spread, collect)


def local(
    features,
    cotangent,
    w_self,
    w_neigh,
    tile_row,
    tile_owner,
    tile_col,
    tile_count,
    edge_dst,
    edge_src,
):
    blocks, feat_cols, tile_width = features.shape
    cycle_size = lax.axis_size("blk")
    col_first = lax.axis_index("col") * feat_cols
    slot_total = tile_row.shape[0]
    edge_count = edge_dst.shape[1]
    tile_groups = slot_total // 8
    tile_alive = jnp.arange(slot_total) < tile_count[0]
    source = tile_owner[:, 0] * blocks + tile_col
    shard_piece = lax.all_gather(features, "blk", axis=0, tiled=True)
    piece_rows = shard_piece.shape[0]
    inside = (source >= 0) & (source < piece_rows)
    taken = jnp.take(shard_piece, jnp.clip(source, 0, piece_rows - 1), axis=0)
    chosen = jnp.where(inside[:, None, None], taken, jnp.zeros_like(taken))
    grouped_src = edge_src.reshape(tile_groups, 8, edge_count)
    grouped_dst = edge_dst.reshape(tile_groups, 8, edge_count)
    grouped_alive = tile_alive.reshape(tile_groups, 8)

    def forward_tiles(tile_args):
        tile_feats, src_ids, dst_ids, alive_now = tile_args
        spread, collect = edge_tables(src_ids, dst_ids, alive_now, tile_width)
        picked = jnp.einsum(
            "tfm,tem->tfe", tile_feats, spread, preferred_element_type=jnp.float32
        ).astype(jnp.bfloat16)
        flows = jnp.einsum("tfe,tek->tfk", picked, collect, preferred_element_type=jnp.float32)
        counts = jnp.sum(collect, axis=1, dtype=jnp.float32)
        return (flows, counts)

    flows, counts = lax.map(
        forward_tiles,
        (
            chosen.reshape(tile_groups, 8, feat_cols, tile_width),
            grouped_src,
            grouped_dst,
            grouped_alive,
        ),
    )
    flows = flows.reshape(slot_total, feat_cols, tile_width)
    counts = counts.reshape(slot_total, tile_width)
    row_hot = (tile_row[None, :] == jnp.arange(blocks)[:, None]).astype(jnp.float32)
    summed = jnp.einsum("rt,tfk->rfk", row_hot, flows, precision=highest)
    degree = jnp.dot(row_hot, counts, precision=highest)
    inverse = 1.0 / jnp.maximum(degree, 1.0)
    neighbor_mean = (summed * inverse[:, None, :]).astype(jnp.bfloat16)
    whole_feats, whole_mean = (
        lax.all_gather(features, "col", axis=1, tiled=True),
        lax.all_gather(neighbor_mean, "col", axis=1, tiled=True),
    )
    self_cols = lax.dynamic_slice_in_dim(w_self, col_first, feat_cols, 1)
    neigh_cols = lax.dynamic_slice_in_dim(w_neigh, col_first, feat_cols, 1)
    preact = jnp.einsum("bfk,fg->bgk", whole_feats, self_cols, preferred_element_type=jnp.float32)
    preact = preact + jnp.einsum(
        "bfk,fg->bgk", whole_mean, neigh_cols, preferred_element_type=jnp.float32
    )
    gate_value = jax.nn.sigmoid(preact)
    hidden = (preact * gate_value).astype(jnp.bfloat16)
    out_grad = (
        cotangent.astype(jnp.float32) * gate_value * (1.0 + preact * (1.0 - gate_value))
    ).astype(jnp.bfloat16)
    self_full = jnp.einsum("bgk,fg->bfk", out_grad, self_cols, preferred_element_type=jnp.float32)
    neigh_full = jnp.einsum("bgk,fg->bfk", out_grad, neigh_cols, preferred_element_type=jnp.float32)
    self_term, pre_sum = (
        lax.psum_scatter(self_full, "col", scatter_dimension=1, tiled=True),
        lax.psum_scatter(neigh_full, "col", scatter_dimension=1, tiled=True),
    )
    part_self = jnp.einsum("bfk,bgk->fg", whole_feats, out_grad, preferred_element_type=jnp.float32)
    part_neigh = jnp.einsum("bfk,bgk->fg", whole_mean, out_grad, preferred_element_type=jnp.float32)
    part_self, part_neigh = (
        lax.all_to_all(part_self, "col", split_axis=0, concat_axis=1, tiled=True),
        lax.all_to_all(part_neigh, "col", split_axis=0, concat_axis=1, tiled=True),
    )
    self_grad, neigh_grad = lax.psum((part_self, part_neigh), "blk")
    grad_scale = 1.0 / math.sqrt(blocks * tile_width * cycle_size)
    pre_grad = (pre_sum * inverse[:, None, :]).astype(jnp.bfloat16)
    dst_rows = jnp.take(pre_grad, tile_row, axis=0)

    def backward_tiles(tile_args):
        tile_grads, src_ids, dst_ids, alive_now = tile_args
        spread, collect = edge_tables(src_ids, dst_ids, alive_now, tile_width)
        picked = jnp.einsum(
            "tfk,tek->tfe", tile_grads, collect, preferred_element_type=jnp.float32
        ).astype(jnp.bfloat16)
        return jnp.einsum(
            "tfe,tem->tfm", picked, spread, preferred_element_type=jnp.float32
        ).astype(jnp.bfloat16)

    partials = lax.map(
        backward_tiles,
        (
            dst_rows.reshape(tile_groups, 8, feat_cols, tile_width),
            grouped_src,
            grouped_dst,
            grouped_alive,
        ),
    )
    partials = partials.reshape(slot_total, feat_cols, tile_width)
    hot = (source[None, :] == jnp.arange(blocks * lax.axis_size("blk"))[:, None]).astype(
        jnp.bfloat16
    )
    returned = lax.psum_scatter(
        jnp.einsum("ct,tfm->cfm", hot, partials, preferred_element_type=jnp.float32).astype(
            jnp.bfloat16
        ),
        "blk",
        scatter_dimension=0,
        tiled=True,
    ).astype(jnp.float32)
    input_grad = (self_term + returned).astype(jnp.bfloat16)
    return (hidden, input_grad, self_grad * grad_scale, neigh_grad * grad_scale)


def solution(mesh):
    placed = (
        P("blk", "col", None),
        P("blk", "col", None),
        P(),
        P(),
        P("blk"),
        P("blk", None),
        P("blk"),
        P("blk"),
        P("blk", None),
        P("blk", None),
    )
    return jax.shard_map(
        local,
        mesh=mesh,
        in_specs=placed,
        out_specs=(P("blk", "col", None), P("blk", "col", None), P("col", None), P("col", None)),
        check_vma=False,
    )
```

profile of v0, /device:TPU:0, one launch (start us, length us, event | category | flops | bytes accessed | tf_op | source)
XLA Modules:
  0.0 625.6 jit_solution(13560252776539541166)
XLA Ops:
  10.3 44.3 %all-gather.6.cloned.1.call-done = bf16[384,32,256]{2,1,0:T(8,128)(2,1)} async-done(((bf16[24,32,256]{2,1,0:T(8,128)(2,1)}), bf16[384,32,256]{2,1,0:T(8,128)(2,1)}) %all-gather.6.cloned.1.call-update) | async-done | bytes 6291472 | tf_op jit(solution)/shard_map/all_gather | solution.py:38
  54.7 3.5 gather_fusion
  58.1 1.6 select_select_fusion
  59.8 91.6 %while.24 = (s32[]{:T(128)}, f32[16,8,32,256]{3,2,1,0:T(8,128)}, f32[16,8,256]{2,1,0:T(8,128)S(1)}, bf16[16,8,32,256]{3,2,1,0:T(8,128)(2,1)}, s32[16,8,640]{2,1,...) while((s32[]{:T(128)}, f32[16,8,32,256]{3,2,1,0:T(8,128)}, ...), condition=%wide.region_2.3_spmd.clone, body=%wide.region_0.2_spmd.sunk.clone | while | flops 178419712 | bytes 562297 | solution.py:57
  60.5 3.7 fusion.114
  66.2 3.7 fusion.114
  70.0 1.2 convert_reduce_fusion.3
  72.0 3.7 fusion.114
  75.7 1.2 convert_reduce_fusion.3
  77.7 3.7 fusion.114
  81.4 1.2 convert_reduce_fusion.3
  83.4 3.7 fusion.114
  87.1 1.2 convert_reduce_fusion.3
  89.2 3.7 fusion.114
  92.9 1.2 convert_reduce_fusion.3
  94.9 3.7 fusion.114
  98.6 1.2 convert_reduce_fusion.3
  100.6 3.7 fusion.114
  106.4 3.7 fusion.114
  112.1 3.7 fusion.114
  117.8 3.7 fusion.114
  123.5 3.7 fusion.114
  129.3 3.7 fusion.114
  135.0 3.7 fusion.114
  140.7 3.7 fusion.114
  146.5 3.7 fusion.114
  151.6 6.6 %fusion.65 = bf16[24,32,256]{2,0,1:T(8,128)(2,1)} fusion(f32[128,32,256]{2,1,0:T(8,128)} %bitcast.133, f32[24,256]{1,0:T(8,128)S(1)} %fusion.71, s32[128]{0:T(128)S(1)} %copy-done.6), kind=kOutput, calls=%fused_computation.56 | convolution fusion | flops 302386176 | bytes 4612608 | tf_op jit(solution)/shard_map/rt,tfk->rfk/dot_general | solution.py:69
  158.5 2.6 fusion.80
  161.1 61.1 %all-gather.8.cloned.1.call-done = bf16[24,256,256]{2,0,1:T(8,128)(2,1)} async-done(((bf16[24,32,256]{2,0,1:T(8,128)(2,1)}), bf16[24,256,256]{2,0,1:T(8,128)(2,1)}) %all-gather.8.cloned.1.call-update) | async-done | bytes 3145744 | tf_op jit(solution)/shard_map/all_gather | solution.py:75
  222.2 3.7 multiply_convert_fusion.1
  227.6 6.3 %copy.76 = f32[256,24,256]{2,1,0:T(8,128)} copy(f32[256,24,256]{2,0,1:T(8,128)S(1)} %fusion.76) | data formatting | bytes 12582912 | tf_op jit(solution)/shard_map/bgk,fg->bfk/dot_general | solution.py:89
  234.0 3.1 fusion.68
  238.0 3.3 all-to-all-start.1
  241.3 2.2 convolution_bitcast_fusion.1
  244.4 4.8 all-to-all-done.1
  249.2 3.3 all-to-all-start
  254.7 5.8 all-to-all-done
  262.0 4.7 convolution_bitcast_fusion
  267.1 65.6 %reduce-scatter.6.cloned.1.call-done = f32[24,32,256]{2,0,1:T(8,128)} async-done(((f32[24,256,256]{2,0,1:T(8,128)}), f32[24,32,256]{2,0,1:T(8,128)}) %reduce-scatter.6.cloned.1.call-update) | async-done | bytes 786448 | tf_op jit(solution)/shard_map/reduce_scatter | solution.py:92
  334.7 1.6 broadcast_select_fusion
  336.3 70.9 %while.25 = (s32[]{:T(128)}, bf16[16,8,32,256]{3,2,1,0:T(8,128)(2,1)}, bf16[16,8,32,256]{3,2,1,0:T(8,128)(2,1)}, s32[16,8,640]{2,1,0:T(8,128)}, pred[16,8]{1,0:T(8,128)(4,1)S(1)}, /*index=5*/s32[16,8,640]{2,1,0:T(8,128)}) while((s32[]{:T(128)}, bf16[16,8,32,256]{3,2,1,0:T(8,128)(2,1)}, bf16[16,8,32,256]{3,2,1,0:T(8,128)(2,1)}, ...), condition=%wide.region_6.7_spmd.clone, body=%wide.region_5.6_spmd.sunk.clone | while | flops 171933696 | bytes 386149 | solution.py:115
  337.0 3.7 fusion.117
  341.4 3.7 fusion.117
  345.9 3.7 fusion.117
  350.3 3.7 fusion.117
  354.7 3.7 fusion.117
  359.2 3.7 fusion.117
  363.6 3.7 fusion.117
  368.1 3.7 fusion.117
  372.5 3.7 fusion.117
  376.9 3.7 fusion.117
  381.4 3.7 fusion.117
  385.8 3.7 fusion.117
  390.2 3.7 fusion.117
  394.6 3.7 fusion.117
  399.1 3.7 fusion.117
  403.5 3.7 fusion.117
  407.2 3.5 fusion.54
  410.7 6.4 %copy.71 = bf16[384,32,256]{2,1,0:T(8,128)(2,1)} copy(bf16[384,32,256]{2,0,1:T(8,128)(2,1)S(1)} %fusion.54) | data formatting | bytes 12582912 | tf_op jit(solution)/shard_map/ct,tfm->cfm/dot_general | solution.py:129
  417.1 23.1 %all-reduce.3.cloned.1.call-done = (f32[32,256]{1,0:T(8,128)}, f32[32,256]{1,0:T(8,128)}) async-done(((f32[32,256]{1,0:T(8,128)}, f32[32,256]{1,0:T(8,128)}), (f32[32,256]{1,0:T(8,128)}, f32[32,256]{1,0:T(8,128)})) %all-reduce.3.cloned.1.call-update) | async-done | bytes 65552 | tf_op jit(solution)/shard_map/psum | solution.py:100
  440.2 1.4 broadcast_multiply_fusion
  441.6 103.0 %reduce-scatter.4.cloned.1.call-done = f32[24,32,256]{2,1,0:T(8,128)} async-done(((f32[24,256,256]{2,1,0:T(8,128)}), f32[24,32,256]{2,1,0:T(8,128)}) %reduce-scatter.4.cloned.1.call-update) | async-done | bytes 786448 | tf_op jit(solution)/shard_map/reduce_scatter | solution.py:91
  544.6 72.0 %reduce-scatter.8.cloned.1.call-done = bf16[24,32,256]{2,1,0:T(8,128)(2,1)} async-done(((bf16[384,32,256]{2,1,0:T(8,128)(2,1)}), bf16[24,32,256]{2,1,0:T(8,128)(2,1)}) %reduce-scatter.8.cloned.1.call-update) | async-done | bytes 393232 | tf_op jit(solution)/shard_map/reduce_scatter | solution.py:128
  616.6 2.1 add_convert_fusion
  (152 shorter events, 48.9 us)
Async XLA Ops:
  7.2 215.0 %copy-start = (bf16[256,256]{1,0:T(8,128)(2,1)S(1)}, bf16[256,256]{1,0:T(8,128)(2,1)}, u32[]{:S(2)}) copy-start(bf16[256,256]{1,0:T(8,128)(2,1)} %param.17) | copy-start | bytes 393220
  7.2 47.5 %all-gather.6.cloned.1.call-start = ((), (), s32[]{:S(2)}) async-start(), calls=%async_computation.6 | async-start | bytes 6684672 | tf_op jit(solution)/shard_map/all_gather | solution.py:38
  7.9 150.6 %all-gather.4.cloned.1.call-start = ((), (), s32[]{:S(2)}) async-start(), calls=%async_computation.5 | async-start | bytes 3538944 | tf_op jit(solution)/shard_map/all_gather | solution.py:74
  8.7 213.5 %all-gather.8.cloned.1.call-start = ((), (), s32[]{:S(2)}) async-start(), calls=%async_computation.7 | async-start | bytes 3538944 | tf_op jit(solution)/shard_map/all_gather | solution.py:75
  59.8 91.7 %copy-start.6 = (s32[128]{0:T(128)S(1)}, s32[128]{0:T(128)}, u32[]{:S(2)}) copy-start(s32[128]{0:T(128)} %param.18) | copy-start | bytes 1540
  151.6 6.9 %copy-start.4 = (bf16[256,256]{1,0:T(8,128)(2,1)S(1)}, bf16[256,256]{1,0:T(8,128)(2,1)}, u32[]{:S(2)}) copy-start(bf16[256,256]{1,0:T(8,128)(2,1)} %param.16) | copy-start | bytes 393220
  158.2 64.0 %copy-start.7 = (bf16[24,32,256]{2,1,0:T(8,128)(2,1)S(1)}, bf16[24,32,256]{2,1,0:T(8,128)(2,1)}, u32[]{:S(2)}) copy-start(bf16[24,32,256]{2,1,0:T(8,128)(2,1)} %param.15) | copy-start | bytes 1179652
  158.2 174.5 %reduce-scatter.6.cloned.1.call-start = ((), (), s32[]{:S(2)}) async-start(), calls=%async_computation.9 | async-start | bytes 7077888 | tf_op jit(solution)/shard_map/reduce_scatter | solution.py:92
  225.9 0.7 copy-start.3
  234.0 7.3 %copy-start.2 = (bf16[24,256,256]{2,1,0:T(8,128)(2,1)S(1)}, bf16[24,256,256]{2,1,0:T(8,128)(2,1)}, u32[]{:S(2)}) copy-start(bf16[24,256,256]{2,1,0:T(8,128)(2,1)} %all-gather.4.cloned.1.call-done) | copy-start | bytes 9437188
  238.0 11.2 %all-to-all-start.1 = ((f32[8,1,1024]{2,1,0:T(1,128)}), f32[8,1,1024]{2,1,0:T(1,128)S(1)}, u32[]{:S(2)}, u32[]{:S(2)}) async-start(f32[8,1,1024]{2,1,0:T(1,128)} %reshape.100), calls=%async_computation.4 | async-start | bytes 65536 | tf_op jit(solution)/shard_map/all_to_all | solution.py:98
  241.3 20.7 %copy-start.5 = (bf16[256,256]{1,0:T(8,128)(2,1)S(1)}, bf16[256,256]{1,0:T(8,128)(2,1)}, u32[]{:S(2)}) copy-start(bf16[256,256]{1,0:T(8,128)(2,1)} %param.16) | copy-start | bytes 393220
  249.2 11.3 %all-to-all-start = ((f32[8,1,1024]{2,1,0:T(1,128)}), f32[8,1,1024]{2,1,0:T(1,128)S(1)}, u32[]{:S(2)}, u32[]{:S(2)}) async-start(f32[8,1,1024]{2,1,0:T(1,128)} %reshape.98), calls=%async_computation.3 | async-start | bytes 65536 | tf_op jit(solution)/shard_map/all_to_all | solution.py:97
  252.5 187.7 %all-reduce.3.cloned.1.call-start = ((), (), s32[]{:S(2)}) async-start(), calls=%async_computation.11 | async-start | bytes 131072 | tf_op jit(solution)/shard_map/psum | solution.py:100
  262.0 282.6 %reduce-scatter.4.cloned.1.call-start = ((), (), s32[]{:S(2)}) async-start(), calls=%async_computation.8 | async-start | bytes 7077888 | tf_op jit(solution)/shard_map/reduce_scatter | solution.py:91
  266.7 349.9 %reduce-scatter.8.cloned.1.call-start = ((), (), s32[]{:S(2)}) async-start(), calls=%async_computation.10 | async-start | bytes 6684672 | tf_op jit(solution)/shard_map/reduce_scatter | solution.py:128
  417.1 201.6 %copy-start.1 = (bf16[256,256]{1,0:T(8,128)(2,1)S(1)}, bf16[256,256]{1,0:T(8,128)(2,1)}, u32[]{:S(2)}) copy-start(bf16[256,256]{1,0:T(8,128)(2,1)} %param.17) | copy-start | bytes 393220
Sparse Core Ops, SparseCore 0:
  9.7 44.8 all-gather.5
  57.0 63.8 all-gather.3
  158.3 63.8 all-gather.7
  234.1 98.5 reduce-scatter.5
  335.9 104.3 all-reduce.2
  444.0 100.5 reduce-scatter.3
  547.1 69.4 reduce-scatter.7
where the time goes:
time: 629 us; the launch traced here: 626 us
  waiting for transfers between devices  381 us (61%)
  matrix products  146 us (23%)
  local copies, waits for them, and re-layouts  46.3 us (7%)
  other arithmetic  29.3 us (5%)
  between operations  15.1 us (2%)
  starting transfers between devices  7.37 us (1%)
    reduce_scatter x1, waiting for transfers between devices, local(): lax.psum_scatter(self_full, 'col', scatter_dimension=1, tiled=True)  103 us
    reduce_scatter x1, waiting for transfers between devices, local(): lax.psum_scatter(jnp.einsum('ct,tfm->cfm', hot, partials, preferred_eleme...  72 us
    reduce_scatter x1, waiting for transfers between devices, local(): lax.psum_scatter(neigh_full, 'col', scatter_dimension=1, tiled=True)  65.6 us
    all_gather x1, waiting for transfers between devices, local(): lax.all_gather(neighbor_mean, 'col', axis=1, tiled=True)  61.1 us
    dot_general x16, matrix products, forward_tiles(): jnp.einsum('tfe,tek->tfk', picked, collect, preferred_element_type=jnp.fl...  59.5 us
    dot_general x16, matrix products, backward_tiles(): jnp.einsum('tfe,tem->tfm', picked, spread, preferred_element_type=jnp.flo...  58.8 us
    all_gather x1, waiting for transfers between devices, local(): shard_piece = lax.all_gather(features, 'blk', axis=0, tiled=True)  44.3 us
    psum x1, waiting for transfers between devices, local(): self_grad, neigh_grad = lax.psum((part_self, part_neigh), 'blk')  23.1 us
  transfers between devices with their start and end apart: 9, of which 8 were waited for; matrix products, arithmetic and copies ran while one was open for 33% of the time, Pallas kernels for 0%

commit v1 on v0

v1 whole, which is shorter than its diff:
```python
import functools
import math

import jax
import jax.numpy as jnp
from jax import lax
from jax.experimental import pallas as pl
from jax.experimental.pallas import tpu as pltpu
from jax.sharding import PartitionSpec as P

GROUP = 8
VMEM_BYTES = 48 * 1024 * 1024


def adjacency_kernel(row_ref, count_ref, src_ref, dst_ref, adj_ref, inv_ref, deg_ref):
    step = pl.program_id(0)
    width = adj_ref.shape[1]
    edges = src_ref.shape[1]

    @pl.when(step == 0)
    def _():
        deg_ref[...] = jnp.zeros_like(deg_ref)

    lane_index = lax.broadcasted_iota(jnp.int32, (width, edges), 0)
    for j in range(GROUP):
        slot = step * GROUP + j
        alive = slot < count_ref[0]
        src = src_ref[j : j + 1, :]
        dst = jnp.where(alive, dst_ref[j : j + 1, :], -1)
        spread = jnp.where(lane_index == src, 1.0, 0.0).astype(jnp.bfloat16)
        collect = jnp.where(lane_index == dst, 1.0, 0.0).astype(jnp.bfloat16)
        adj = lax.dot_general(
            spread, collect, (((1,), (1,)), ((), ())), preferred_element_type=jnp.float32
        )
        adj_ref[j] = adj.astype(jnp.bfloat16)
        row = row_ref[slot]
        deg_ref[row] += jnp.sum(adj.reshape(width // 8, 8, width), axis=0)

    @pl.when(step == pl.num_programs(0) - 1)
    def _():
        degree = jnp.sum(deg_ref[...], axis=1, keepdims=True)
        inv_ref[...] = 1.0 / jnp.maximum(degree, 1.0)


def build_adjacency(tile_row, tile_count, edge_src, edge_dst, blocks, width):
    slots, edges = edge_src.shape
    return pl.pallas_call(
        adjacency_kernel,
        grid_spec=pltpu.PrefetchScalarGridSpec(
            num_scalar_prefetch=2,
            grid=(slots // GROUP,),
            in_specs=[
                pl.BlockSpec((GROUP, edges), lambda i, *_: (i, 0)),
                pl.BlockSpec((GROUP, edges), lambda i, *_: (i, 0)),
            ],
            out_specs=[
                pl.BlockSpec((GROUP, width, width), lambda i, *_: (i, 0, 0)),
                pl.BlockSpec((blocks, 1, width), lambda i, *_: (0, 0, 0)),
            ],
            scratch_shapes=[pltpu.VMEM((blocks, 8, width), jnp.float32)],
        ),
        out_shape=[
            jax.ShapeDtypeStruct((slots, width, width), jnp.bfloat16),
            jax.ShapeDtypeStruct((blocks, 1, width), jnp.float32),
        ],
        compiler_params=pltpu.CompilerParams(vmem_limit_bytes=VMEM_BYTES),
        cost_estimate=pl.CostEstimate(
            flops=2 * slots * edges * width * width,
            bytes_accessed=slots * width * width * 2,
            transcendentals=0,
        ),
        name="adjacency",
    )(tile_row, tile_count, edge_src, edge_dst)


def mean_kernel(row_ref, source_ref, feats_ref, adj_ref, inv_ref, mean_ref, sum_ref):
    step = pl.program_id(0)

    @pl.when(step == 0)
    def _():
        sum_ref[...] = jnp.zeros_like(sum_ref)

    for j in range(GROUP):
        slot = step * GROUP + j
        flow = jnp.dot(
            feats_ref[source_ref[slot]], adj_ref[j], preferred_element_type=jnp.float32
        )
        sum_ref[row_ref[slot]] += flow

    @pl.when(step == pl.num_programs(0) - 1)
    def _():
        mean_ref[...] = (sum_ref[...] * inv_ref[...]).astype(jnp.bfloat16)


def neighbor_mean(tile_row, source, feats, adj, inverse):
    slots, width, _ = adj.shape
    nodes, cols, _ = feats.shape
    blocks = inverse.shape[0]
    whole = pl.BlockSpec(memory_space=pltpu.VMEM)
    return pl.pallas_call(
        mean_kernel,
        grid_spec=pltpu.PrefetchScalarGridSpec(
            num_scalar_prefetch=2,
            grid=(slots // GROUP,),
            in_specs=[
                whole,
                pl.BlockSpec((GROUP, width, width), lambda i, *_: (i, 0, 0)),
                whole,
            ],
            out_specs=whole,
            scratch_shapes=[pltpu.VMEM((blocks, cols, width), jnp.float32)],
        ),
        out_shape=jax.ShapeDtypeStruct((blocks, cols, width), jnp.bfloat16),
        compiler_params=pltpu.CompilerParams(vmem_limit_bytes=VMEM_BYTES),
        name="neighbor_mean",
    )(tile_row, source, feats, adj, inverse)


def dense_kernel(
    x_ref, mean_ref, cot_ref, ws_ref, wn_ref, wst_ref, wnt_ref, inv_ref,
    hidden_ref, self_ref, pre_ref, gs_ref, gn_ref,
):
    step = pl.program_id(0)
    parts, _, cols, width = x_ref.shape
    feats = parts * cols
    x = x_ref[...].reshape(feats, width)
    mean = mean_ref[...].reshape(feats, width)
    cot = cot_ref[...].reshape(feats, width).astype(jnp.float32)
    preact = jnp.dot(wst_ref[...], x, preferred_element_type=jnp.float32)
    preact = preact + jnp.dot(wnt_ref[...], mean, preferred_element_type=jnp.float32)
    gate = jax.nn.sigmoid(preact)
    hidden_ref[...] = (preact * gate).astype(jnp.bfloat16).reshape(parts, 1, cols, width)
    out_grad = (cot * gate * (1.0 + preact * (1.0 - gate))).astype(jnp.bfloat16)
    self_term = jnp.dot(ws_ref[...], out_grad, preferred_element_type=jnp.float32)
    self_ref[...] = self_term.astype(self_ref.dtype).reshape(parts, 1, cols, width)
    pre = jnp.dot(wn_ref[...], out_grad, preferred_element_type=jnp.float32) * inv_ref[0]
    pre_ref[...] = pre.astype(jnp.bfloat16).reshape(parts, 1, cols, width)

    @pl.when(step == 0)
    def _():
        gs_ref[...] = jnp.zeros_like(gs_ref)
        gn_ref[...] = jnp.zeros_like(gn_ref)

    nt = (((1,), (1,)), ((), ()))
    gs_ref[...] += lax.dot_general(x, out_grad, nt, preferred_element_type=jnp.float32)
    gn_ref[...] += lax.dot_general(mean, out_grad, nt, preferred_element_type=jnp.float32)


def dense(x, mean, cot, w_self, w_neigh, inverse):
    parts, rows, cols, width = x.shape
    feats = parts * cols
    part = pl.BlockSpec((parts, 1, cols, width), lambda i: (0, i, 0, 0))
    weight = pl.BlockSpec((feats, feats), lambda i: (0, 0))
    moved = jax.ShapeDtypeStruct(x.shape, jnp.bfloat16)
    grad = jax.ShapeDtypeStruct((feats, feats), jnp.float32)
    return pl.pallas_call(
        dense_kernel,
        grid=(rows,),
        in_specs=[part, part, part, weight, weight, weight, weight,
                  pl.BlockSpec((1, 1, width), lambda i: (i, 0, 0))],
        out_specs=[part, part, part, weight, weight],
        out_shape=[moved, moved, moved, grad, grad],
        compiler_params=pltpu.CompilerParams(vmem_limit_bytes=VMEM_BYTES),
        name="dense",
    )(x, mean, cot, w_self, w_neigh, w_self.T, w_neigh.T, inverse)


def back_kernel(row_ref, source_ref, grads_ref, adj_ref, out_ref, sum_ref):
    step = pl.program_id(0)

    @pl.when(step == 0)
    def _():
        sum_ref[...] = jnp.zeros_like(sum_ref)

    for j in range(GROUP):
        slot = step * GROUP + j
        back = lax.dot_general(
            grads_ref[row_ref[slot]], adj_ref[j], (((1,), (1,)), ((), ())),
            preferred_element_type=jnp.float32,
        )
        sum_ref[source_ref[slot]] += back.astype(jnp.bfloat16).astype(jnp.float32)

    @pl.when(step == pl.num_programs(0) - 1)
    def _():
        out_ref[...] = sum_ref[...].astype(jnp.bfloat16)


def transposed_sums(tile_row, source, grads, adj, nodes):
    slots, width, _ = adj.shape
    _, cols, _ = grads.shape
    whole = pl.BlockSpec(memory_space=pltpu.VMEM)
    return pl.pallas_call(
        back_kernel,
        grid_spec=pltpu.PrefetchScalarGridSpec(
            num_scalar_prefetch=2,
            grid=(slots // GROUP,),
            in_specs=[whole, pl.BlockSpec((GROUP, width, width), lambda i, *_: (i, 0, 0))],
            out_specs=whole,
            scratch_shapes=[pltpu.VMEM((nodes, cols, width), jnp.float32)],
        ),
        out_shape=jax.ShapeDtypeStruct((nodes, cols, width), jnp.bfloat16),
        compiler_params=pltpu.CompilerParams(vmem_limit_bytes=VMEM_BYTES),
        name="transposed_sums",
    )(tile_row, source, grads, adj)


def local(
    features, cotangent, w_self, w_neigh, tile_row, tile_owner, tile_col, tile_count,
    edge_dst, edge_src,
):
    blocks, cols, width = features.shape
    n_blk, n_col = lax.axis_size("blk"), lax.axis_size("col")
    per = blocks // n_col
    source = tile_owner[:, 0] * blocks + tile_col

    def to_nodes(a):
        return lax.all_to_all(a.reshape(n_col, per, cols, width), "col", 0, 0)

    def to_feats(a):
        return lax.all_to_all(a, "col", 0, 0).reshape(blocks, cols, width)

    gathered = lax.all_gather(features, "blk", axis=0, tiled=True)
    adj, inverse = build_adjacency(tile_row, tile_count, edge_src, edge_dst, blocks, width)
    x_nodes, cot_nodes = to_nodes(features), to_nodes(cotangent)
    mean = neighbor_mean(tile_row, source, gathered, adj, inverse)
    mean_nodes = to_nodes(mean)
    own_inverse = lax.dynamic_slice_in_dim(inverse, lax.axis_index("col") * per, per, 0)
    hidden, self_term, pre_grad, self_part, neigh_part = dense(
        x_nodes, mean_nodes, cot_nodes, w_self, w_neigh, own_inverse
    )
    pre_feats = to_feats(pre_grad)
    back = transposed_sums(tile_row, source, pre_feats, adj, blocks * n_blk)
    returned = lax.psum_scatter(back, "blk", scatter_dimension=0, tiled=True)
    input_grad = (
        to_feats(self_term).astype(jnp.float32) + returned.astype(jnp.float32)
    ).astype(jnp.bfloat16)

    feats = n_col * cols
    parts = jnp.stack([self_part, neigh_part]).reshape(2, n_col, cols, feats)
    total = jnp.sum(lax.all_to_all(parts, "col", 1, 1), axis=1)
    for bit in range(n_blk.bit_length() - 1):
        total = total + lax.ppermute(
            total, "blk", [(i, i ^ (1 << bit)) for i in range(n_blk)]
        )
    total = total * (1.0 / math.sqrt(blocks * width * n_blk))
    return (to_feats(hidden), input_grad, total[0], total[1])


def solution(mesh):
    placed = (
        P("blk", "col", None),
        P("blk", "col", None),
        P(),
        P(),
        P("blk"),
        P("blk", None),
        P("blk"),
        P("blk"),
        P("blk", None),
        P("blk", None),
    )
    return jax.shard_map(
        local,
        mesh=mesh,
        in_specs=placed,
        out_specs=(P("blk", "col", None), P("blk", "col", None), P("col", None), P("col", None)),
        check_vma=False,
    )
```

time: 629 us -> 213 us (0.34)
  waiting for transfers between devices: 381 us -> 69.8 us
  matrix products: 146 us -> 0 us
  Pallas kernels: 0 us -> 60.7 us
  local copies, waits for them, and re-layouts: 46.3 us -> 4.2 us
  other arithmetic: 29.3 us -> 1.99 us
  blocking collectives: 0 us -> 26.3 us
  starting transfers between devices: 7.37 us -> 32.8 us
    reduce_scatter x3 -> x1, waiting for transfers between devices: 241 us -> 26.1 us  [local(): returned = lax.psum_scatter(back, 'blk', scatter_dimension=0, tiled=True)]
    dot_general x41 -> x0, matrix products: 146 us -> none  [the longest x16 59.5 us: forward_tiles(): jnp.einsum('tfe,tek->tfk', picked, collect, preferred_element_type=jnp.fl...]
    all_gather x3 -> x1, waiting for transfers between devices: 105 us -> 5.44 us  [local(): gathered = lax.all_gather(features, 'blk', axis=0, tiled=True)]
    pallas_call x0 -> x4, Pallas kernels: none -> 60.7 us  [the longest x1 22.1 us: build_adjacency(): pl.pallas_call(adjacency_kernel, grid_spec=pltpu.PrefetchScalarGridSpec(n...]
    all_to_all x0 -> x2, blocking collectives: none -> 26.3 us  [the longest x1 13.5 us: local(): total = jnp.sum(lax.all_to_all(parts, 'col', 1, 1), axis=1)]
    eq x32 -> x0, local copies, waits for them, and re-layouts: 24 us -> none  [the longest x16 12.1 us: edge_tables(): dst_ids[..., None] == lane_index]
    psum x1 -> x0, waiting for transfers between devices: 23.1 us -> none  [local(): self_grad, neigh_grad = lax.psum((part_self, part_neigh), 'blk')]
    all_to_all x2 -> x5, starting transfers between devices: 6.68 us -> 27.9 us  [the longest x3 16.8 us: to_nodes(): return lax.all_to_all(a.reshape(n_col, per, cols, width), 'col', 0, 0)]
  transfers between devices with their start and end apart: 9 -> 11, of which waited for: 8 -> 8; matrix products, arithmetic and copies ran while one was open for 33% -> 0% of each run, Pallas kernels for 0% -> 18%
where the time goes in v1:
time: 213 us; the launch traced here: 211 us
  waiting for transfers between devices  69.8 us (33%)
  Pallas kernels  60.7 us (28%)
  starting transfers between devices  32.8 us (15%)
  blocking collectives  26.3 us (12%)
  between operations  14.8 us (7%)
  local copies, waits for them, and re-layouts  4.2 us (2%)
    reduce_scatter x1, waiting for transfers between devices, local(): returned = lax.psum_scatter(back, 'blk', scatter_dimension=0, tiled=True)  26.1 us
    pallas_call x1, Pallas kernels, build_adjacency(): pl.pallas_call(adjacency_kernel, grid_spec=pltpu.PrefetchScalarGridSpec(n...  22.1 us
    all_to_all x3, waiting for transfers between devices, to_nodes(): return lax.all_to_all(a.reshape(n_col, per, cols, width), 'col', 0, 0)  19.9 us
    pallas_call x1, Pallas kernels, transposed_sums(): pl.pallas_call(back_kernel, grid_spec=pltpu.PrefetchScalarGridSpec(num_sc...  18.9 us
    all_to_all x3, starting transfers between devices, to_nodes(): return lax.all_to_all(a.reshape(n_col, per, cols, width), 'col', 0, 0)  16.8 us
    pallas_call x1, Pallas kernels, neighbor_mean(): pl.pallas_call(mean_kernel, grid_spec=pltpu.PrefetchScalarGridSpec(num_sc...  16.4 us
    all_to_all x1, blocking collectives, local(): total = jnp.sum(lax.all_to_all(parts, 'col', 1, 1), axis=1)  13.5 us
    all_to_all x1, blocking collectives, to_feats(): return lax.all_to_all(a, 'col', 0, 0).reshape(blocks, cols, width)  12.7 us
  transfers between devices with their start and end apart: 11, of which 8 were waited for; matrix products, arithmetic and copies ran while one was open for 0% of the time, Pallas kernels for 18%

profile of v1, /device:TPU:0, one launch (start us, length us, event | category | flops | bytes accessed | tf_op | source)
XLA Modules:
  0.0 210.5 jit_solution(15437406089593474128)
XLA Ops:
  7.2 0.0 all-gather.2.cloned.1.call-start
  7.2 0.7 all-gather.2.cloned.1.call-update
  7.9 7.0 %all-to-all-start = ((bf16[8,3,32,256]{3,2,1,0:T(8,128)(2,1)}), bf16[8,3,32,256]{3,2,1,0:T(8,128)(2,1)S(1)}, u32[]{:S(2)}, u32[]{:S(2)}) async-start(bf16[8,3,32,256]{3,2,1,0:T(8,128)(2,1)} %bitcast.27), calls=%async_computation | async-start | bytes 786432 | tf_op jit(solution)/shard_map/all_to_all | solution.py:217
  15.6 9.6 %all-to-all-done.x_ref = bf16[8,3,32,256]{3,2,1,0:T(8,128)(2,1)S(1)} async-done(((bf16[8,3,32,256]{3,2,1,0:T(8,128)(2,1)}), bf16[8,3,32,256]{3,2,1,0:T(8,128)(2,1)S(1)}, u32[]{:S(2)}, u32[]{:S(2)}) %all-to-all-start) | async-done | bytes 393248 | tf_op jit(solution)/shard_map/all_to_all | solution.py:217
  25.1 3.5 %all-to-all-start.2 = ((bf16[8,3,32,256]{3,2,1,0:T(8,128)(2,1)}), bf16[8,3,32,256]{3,2,1,0:T(8,128)(2,1)S(1)}, u32[]{:S(2)}, u32[]{:S(2)}) async-start(bf16[8,3,32,256]{3,2,1,0:T(8,128)(2,1)} %bitcast.29), calls=%async_computation.2 | async-start | bytes 786432 | tf_op jit(solution)/shard_map/all_to_all | solution.py:217
  28.6 0.0 copy-start.2
  28.6 0.6 copy-done.2
  29.3 0.0 copy-start.4
  29.3 1.0 copy-done.4
  30.2 0.0 copy-start.5
  30.2 1.0 copy-done.5
  31.2 0.0 copy-start.6
  31.2 0.0 copy-start.7
  31.2 0.0 copy-start.3
  31.2 22.1 %adjacency.1 = (bf16[128,256,256]{2,1,0:T(8,128)(2,1)}, f32[24,1,256]{2,1,0:T(1,128)S(1)}) custom-call(s32[128]{0:T(128)S(1)} %copy-done.2, s32[1]{0:T(128)S(6)} %copy.21.count_ref, s32[128,640]{1,0:T(8,128)S(1)} %copy-done.4, s32[128,640]{1,0:T(8,128)S(1)} %copy-done.5), custom_call_target="tpu_custom_call" | custom-call | flops 10737418240 | bytes 16777216 | tf_op jit(solution)/shard_map/adjacency/pallas_call | solution.py:47
  53.3 0.0 copy-done.6
  53.3 0.0 copy-done.7
  53.3 5.4 %all-gather.2.cloned.1.call-done.feats_ref = bf16[384,32,256]{2,1,0:T(8,128)(2,1)} async-done(((bf16[24,32,256]{2,1,0:T(8,128)(2,1)}), bf16[384,32,256]{2,1,0:T(8,128)(2,1)}) %all-gather.2.cloned.1.call-update) | async-done | bytes 6291472 | tf_op jit(solution)/shard_map/all_gather | solution.py:222
  58.8 0.0 copy-done.3
  58.8 0.0 copy-start
  58.8 0.0 copy-start.1
  58.8 16.4 %neighbor_mean.1 = bf16[24,32,256]{2,1,0:T(8,128)(2,1)} custom-call(s32[128]{0:T(128)S(1)} %copy-done.3, s32[128]{0:T(128)S(1)} %bitcast_add_fusion.source_ref, bf16[384,32,256]{2,1,0:T(8,128)(2,1)} %all-gather.2.cloned.1.call-done.feats_ref, bf16[128,256,256]{2,1,0:T(8,128)(2,1)} %get-tuple-element.11.adj_ref, f32[24,1,256]{2,1,0:T(1,128)S(1)} %get-tuple-element.12.inv_ref), custom_call_target="tpu_custom_call" | custom-call | tf_op jit(solution)/shard_map/neighbor_mean/pallas_call | solution.py:100
  75.1 0.0 all-to-all-done.2.cot_ref
  75.1 6.3 %all-to-all-start.1 = ((bf16[8,3,32,256]{3,2,1,0:T(8,128)(2,1)}), bf16[8,3,32,256]{3,2,1,0:T(8,128)(2,1)S(1)}, u32[]{:S(2)}, u32[]{:S(2)}) async-start(bf16[8,3,32,256]{3,2,1,0:T(8,128)(2,1)} %bitcast.2), calls=%async_computation.1 | async-start | bytes 786432 | tf_op jit(solution)/shard_map/all_to_all | solution.py:217
  81.4 0.0 reduce-scatter.2.cloned.1.call-start
  81.5 0.0 copy-done
  81.5 0.1 copy.16
  81.6 0.0 copy-done.1
  81.6 0.1 copy.17
  81.7 10.3 %all-to-all-done.1.mean_ref = bf16[8,3,32,256]{3,2,1,0:T(8,128)(2,1)S(1)} async-done(((bf16[8,3,32,256]{3,2,1,0:T(8,128)(2,1)}), bf16[8,3,32,256]{3,2,1,0:T(8,128)(2,1)S(1)}, u32[]{:S(2)}, u32[]{:S(2)}) %all-to-all-start.1) | async-done | bytes 393248 | tf_op jit(solution)/shard_map/all_to_all | solution.py:217
  92.0 3.4 %dense.1 = (bf16[8,3,32,256]{3,2,1,0:T(8,128)(2,1)}, bf16[8,3,32,256]{3,2,1,0:T(8,128)(2,1)}, bf16[8,3,32,256]{3,2,1,0:T(8,128)(2,1)S(1)}, f32[256,256]{1,0:T(8,128)S(1)}, f32[256,256]{1,0:T(8,128)S(1)}) custom-call(bf16[8,3,32,256]{3,2,1,0:T(8,128)(2,1)S(1)} %all-to-all-done.x_ref, bf16[8,3,32,256]{3,2,1,0:T(8,128)(2,1)S(1)} %all-to-all-done.1.mean_ref, ...), custom_call_target="tpu_custom_call" | custom-call | tf_op jit(solution)/shard_map/dense/pallas_call | solution.py:156
  95.4 12.7 %all_to_all.35 = bf16[8,3,32,256]{3,2,1,0:T(8,128)(2,1)S(1)} all-to-all(bf16[8,3,32,256]{3,2,1,0:T(8,128)(2,1)S(1)} %get-tuple-element.15), channel_id=1, replica_groups=mesh['blk'=16,'col'=8] {'col'}, dimensions={0} | all-to-all | bytes 786432 | tf_op jit(solution)/shard_map/all_to_all | solution.py:220
  108.2 18.9 %transposed_sums.1 = bf16[384,32,256]{2,1,0:T(8,128)(2,1)} custom-call(s32[128]{0:T(128)S(1)} %copy-done.3, s32[128]{0:T(128)S(1)} %bitcast_add_fusion.source_ref, bf16[24,32,256]{2,1,0:T(8,128)(2,1)S(1)} %bitcast.22, bf16[128,256,256]{2,1,0:T(8,128)(2,1)} %get-tuple-element.11.adj_ref), custom_call_target="tpu_custom_call" | custom-call | tf_op jit(solution)/shard_map/transposed_sums/pallas_call | solution.py:192
  127.1 0.0 reduce-scatter.2.cloned.1.call-update
  127.1 13.5 %all_to_all.36 = f32[2,8,32,256]{3,2,0,1:T(8,128)S(1)} all-to-all(f32[2,8,32,256]{3,2,0,1:T(8,128)S(1)} %pad_maximum_fusion), channel_id=1, replica_groups=mesh['blk'=16,'col'=8] {'col'}, dimensions={1} | all-to-all | bytes 1048576 | tf_op jit(solution)/shard_map/all_to_all | solution.py:240
  140.7 3.5 %all-to-all-start.3 = ((bf16[8,3,32,256]{3,2,1,0:T(8,128)(2,1)}), bf16[8,3,32,256]{3,2,1,0:T(8,128)(2,1)S(1)}, u32[]{:S(2)}, u32[]{:S(2)}) async-start(bf16[8,3,32,256]{3,2,1,0:T(8,128)(2,1)} %get-tuple-element.13), calls=%async_computation.3 | async-start | bytes 786432 | tf_op jit(solution)/shard_map/all_to_all | solution.py:220
  144.2 0.1 collective-permute-start
  144.3 1.2 collective-permute-done
  145.5 1.5 collective-permute-start.1
  147.0 3.8 %collective-permute-done.1 = f32[2,32,256]{2,1,0:T(8,128)S(1)} collective-permute-done((f32[2,32,256]{2,1,0:T(8,128)S(1)}, f32[2,32,256]{2,1,0:T(8,128)S(1)}, u32[]{:S(2)}, u32[]{:S(2)}) %collective-permute-start.1) | collective-permute-done | bytes 65568 | tf_op jit(solution)/shard_map/ppermute | solution.py:242
  150.8 2.8 %collective-permute-start.2 = (f32[2,32,256]{2,1,0:T(8,128)S(1)}, f32[2,32,256]{2,1,0:T(8,128)S(1)}, u32[]{:S(2)}, u32[]{:S(2)}) collective-permute-start(f32[2,32,256]{2,1,0:T(8,128)S(1)} %add.27), channel_id=1, source_target_pairs={{0,32},{8,40},{16,48},{24,56},{32,0},{40,8},{48,16},{56,24},{64,96... | collective-permute-start | bytes 196616 | tf_op jit(solution)/shard_map/ppermute | solution.py:242
  153.6 3.8 %collective-permute-done.2 = f32[2,32,256]{2,1,0:T(8,128)S(1)} collective-permute-done((f32[2,32,256]{2,1,0:T(8,128)S(1)}, f32[2,32,256]{2,1,0:T(8,128)S(1)}, u32[]{:S(2)}, u32[]{:S(2)}) %collective-permute-start.2) | collective-permute-done | bytes 65568 | tf_op jit(solution)/shard_map/ppermute | solution.py:242
  157.4 0.4 collective-permute-start.3
  157.8 0.0 all-to-all-done.3
  157.8 7.7 %all-to-all-start.4 = ((bf16[8,3,32,256]{3,2,1,0:T(8,128)(2,1)}), bf16[8,3,32,256]{3,2,1,0:T(8,128)(2,1)S(1)}, u32[]{:S(2)}, u32[]{:S(2)}) async-start(bf16[8,3,32,256]{3,2,1,0:T(8,128)(2,1)} %get-tuple-element.14), calls=%async_computation.4 | async-start | bytes 786432 | tf_op jit(solution)/shard_map/all_to_all | solution.py:220
  165.5 0.0 collective-permute-done.3
  165.5 0.6 slice_bitcast_fusion
  166.1 8.8 %all-to-all-done.4 = bf16[8,3,32,256]{3,2,1,0:T(8,128)(2,1)S(1)} async-done(((bf16[8,3,32,256]{3,2,1,0:T(8,128)(2,1)}), bf16[8,3,32,256]{3,2,1,0:T(8,128)(2,1)S(1)}, u32[]{:S(2)}, u32[]{:S(2)}) %all-to-all-start.4) | async-done | bytes 393248 | tf_op jit(solution)/shard_map/all_to_all | solution.py:220
  175.0 26.1 %reduce-scatter.2.cloned.1.call-done = bf16[24,32,256]{2,1,0:T(8,128)(2,1)} async-done(((bf16[384,32,256]{2,1,0:T(8,128)(2,1)}), bf16[24,32,256]{2,1,0:T(8,128)(2,1)}) %reduce-scatter.2.cloned.1.call-update) | async-done | bytes 393232 | tf_op jit(solution)/shard_map/reduce_scatter | solution.py:233
  201.1 1.9 fusion
  203.0 0.7 copy.22
  (8 shorter events, 0.1 us)
Async XLA Ops:
  7.2 51.6 %all-gather.2.cloned.1.call-start = ((), (), s32[]{:S(2)}) async-start(), calls=%async_computation.8 | async-start | bytes 6684672 | tf_op jit(solution)/shard_map/all_gather | solution.py:222
  7.9 17.2 %all-to-all-start = ((bf16[8,3,32,256]{3,2,1,0:T(8,128)(2,1)}), bf16[8,3,32,256]{3,2,1,0:T(8,128)(2,1)S(1)}, u32[]{:S(2)}, u32[]{:S(2)}) async-start(bf16[8,3,32,256]{3,2,1,0:T(8,128)(2,1)} %bitcast.27), calls=%async_computation | async-start | bytes 786432 | tf_op jit(solution)/shard_map/all_to_all | solution.py:217
  25.1 50.0 %all-to-all-start.2 = ((bf16[8,3,32,256]{3,2,1,0:T(8,128)(2,1)}), bf16[8,3,32,256]{3,2,1,0:T(8,128)(2,1)S(1)}, u32[]{:S(2)}, u32[]{:S(2)}) async-start(bf16[8,3,32,256]{3,2,1,0:T(8,128)(2,1)} %bitcast.29), calls=%async_computation.2 | async-start | bytes 786432 | tf_op jit(solution)/shard_map/all_to_all | solution.py:217
  28.6 0.7 copy-start.2
  29.3 1.0 copy-start.4
  30.2 1.0 copy-start.5
  31.2 22.1 %copy-start.6 = (s32[128]{0:T(128)S(1)}, s32[128]{0:T(128)}, u32[]{:S(2)}) copy-start(s32[128]{0:T(128)} %param.16) | copy-start | bytes 1540
  31.2 22.1 %copy-start.7 = (s32[128,1]{0,1:T(1,128)S(1)}, s32[128,1]{0,1:T(1,128)}, u32[]{:S(2)}) copy-start(s32[128,1]{0,1:T(1,128)} %param.15) | copy-start | bytes 1540
  31.2 27.5 %copy-start.3 = (s32[128]{0:T(128)S(1)}, s32[128]{0:T(128)}, u32[]{:S(2)}) copy-start(s32[128]{0:T(128)} %row_ref.5) | copy-start | bytes 1540
  58.8 22.7 %copy-start = (bf16[256,256]{1,0:T(8,128)(2,1)S(1)}, bf16[256,256]{1,0:T(8,128)(2,1)}, u32[]{:S(2)}) copy-start(bf16[256,256]{1,0:T(8,128)(2,1)} %ws_ref.1) | copy-start | bytes 393220
  58.8 22.8 %copy-start.1 = (bf16[256,256]{1,0:T(8,128)(2,1)S(1)}, bf16[256,256]{1,0:T(8,128)(2,1)}, u32[]{:S(2)}) copy-start(bf16[256,256]{1,0:T(8,128)(2,1)} %wn_ref.1) | copy-start | bytes 393220
  75.1 16.9 %all-to-all-start.1 = ((bf16[8,3,32,256]{3,2,1,0:T(8,128)(2,1)}), bf16[8,3,32,256]{3,2,1,0:T(8,128)(2,1)S(1)}, u32[]{:S(2)}, u32[]{:S(2)}) async-start(bf16[8,3,32,256]{3,2,1,0:T(8,128)(2,1)} %bitcast.2), calls=%async_computation.1 | async-start | bytes 786432 | tf_op jit(solution)/shard_map/all_to_all | solution.py:217
  81.4 119.6 %reduce-scatter.2.cloned.1.call-start = ((), (), s32[]{:S(2)}) async-start(), calls=%async_computation.9 | async-start | bytes 6684672 | tf_op jit(solution)/shard_map/reduce_scatter | solution.py:233
  140.7 17.1 %all-to-all-start.3 = ((bf16[8,3,32,256]{3,2,1,0:T(8,128)(2,1)}), bf16[8,3,32,256]{3,2,1,0:T(8,128)(2,1)S(1)}, u32[]{:S(2)}, u32[]{:S(2)}) async-start(bf16[8,3,32,256]{3,2,1,0:T(8,128)(2,1)} %get-tuple-element.13), calls=%async_computation.3 | async-start | bytes 786432 | tf_op jit(solution)/shard_map/all_to_all | solution.py:220
  144.2 1.3 collective-permute-start
  145.5 5.3 %collective-permute-start.1 = (f32[2,32,256]{2,1,0:T(8,128)S(1)}, f32[2,32,256]{2,1,0:T(8,128)S(1)}, u32[]{:S(2)}, u32[]{:S(2)}) collective-permute-start(f32[2,32,256]{2,1,0:T(8,128)S(1)} %add.26), channel_id=1, source_target_pairs={{0,16},{8,24},{16,0},{24,8},{32,48},{40,56},{48,32},{56,40},{64,80... | collective-permute-start | bytes 196616 | tf_op jit(solution)/shard_map/ppermute | solution.py:242
  150.8 6.5 %collective-permute-start.2 = (f32[2,32,256]{2,1,0:T(8,128)S(1)}, f32[2,32,256]{2,1,0:T(8,128)S(1)}, u32[]{:S(2)}, u32[]{:S(2)}) collective-permute-start(f32[2,32,256]{2,1,0:T(8,128)S(1)} %add.27), channel_id=1, source_target_pairs={{0,32},{8,40},{16,48},{24,56},{32,0},{40,8},{48,16},{56,24},{64,96... | collective-permute-start | bytes 196616 | tf_op jit(solution)/shard_map/ppermute | solution.py:242
  157.4 8.1 %collective-permute-start.3 = (f32[2,32,256]{2,1,0:T(8,128)S(1)}, f32[2,32,256]{2,1,0:T(8,128)S(1)}, u32[]{:S(2)}, u32[]{:S(2)}) collective-permute-start(f32[2,32,256]{2,1,0:T(8,128)S(1)} %add.28), channel_id=1, source_target_pairs={{0,64},{8,72},{16,80},{24,88},{32,96},{40,104},{48,112},{56,120},{... | collective-permute-start | bytes 196616 | tf_op jit(solution)/shard_map/ppermute | solution.py:242
  157.8 17.2 %all-to-all-start.4 = ((bf16[8,3,32,256]{3,2,1,0:T(8,128)(2,1)}), bf16[8,3,32,256]{3,2,1,0:T(8,128)(2,1)S(1)}, u32[]{:S(2)}, u32[]{:S(2)}) async-start(bf16[8,3,32,256]{3,2,1,0:T(8,128)(2,1)} %get-tuple-element.14), calls=%async_computation.4 | async-start | bytes 786432 | tf_op jit(solution)/shard_map/all_to_all | solution.py:220
Sparse Core Ops, SparseCore 0:
  9.7 49.0 all-gather.1
  127.2 73.8 reduce-scatter.1

commit v2 on v0

v2 whole, which is shorter than its diff:
```python
import functools
import math

import jax
import jax.numpy as jnp
from jax import lax
from jax.experimental import pallas as pl
from jax.experimental.pallas import tpu as pltpu
from jax.sharding import PartitionSpec as P

UNROLL = 8
HERE = 160
ROWS = 168
CUTS = (0, 8, 16)
VMEM_BYTES = 14 * 1024 * 1024
NT = (((1,), (1,)), ((), ()))
WHOLE = pl.BlockSpec(memory_space=pltpu.VMEM)
IDLE = pl.BlockSpec(memory_space=pl.ANY)
SCALARS = pl.BlockSpec(memory_space=pltpu.SMEM)

VIEW = (0, 2, 6, 1, 3, 4, 7, 5)


def turned(i, dz):
    y, z, core = i >> 3, (i >> 1) & 3, i & 1
    return (y << 3) | (((z + dz) % 4) << 1) | core


ROUTES = {
    "up": [(i, turned(i, 1)) for i in range(16)],
    "down": [(i, turned(i, -1)) for i in range(16)],
    "over": [(i, i ^ 8) for i in range(16)],
    "core": [(i, i ^ 1) for i in range(16)],
}


def send(value, route):
    return lax.ppermute(value, "blk", ROUTES[route])


def call(
    kernel, out_shape, operands, scalars=(), scratch=(), aliases=None, flops=0, name=None,
    idle=(), idle_out=0,
):
    out_specs = [WHOLE] * (len(out_shape) - idle_out) + [IDLE] * idle_out
    return pl.pallas_call(
        kernel,
        in_specs=[SCALARS] * len(scalars) + [WHOLE] * len(operands) + [IDLE] * len(idle),
        out_specs=out_specs,
        out_shape=out_shape,
        scratch_shapes=list(scratch),
        input_output_aliases=aliases or {},
        compiler_params=pltpu.CompilerParams(vmem_limit_bytes=VMEM_BYTES),
        cost_estimate=pl.CostEstimate(flops=flops, bytes_accessed=0, transcendentals=0),
        name=name,
    )(*scalars, *operands, *idle)


def one_hot(ids, lanes):
    hit = jnp.where(
        lanes == ids.astype(jnp.bfloat16), jnp.ones((), jnp.bfloat16), jnp.zeros((), jnp.bfloat16)
    )
    return hit.astype(jnp.float8_e4m3fn)


def adjacency_kernel(first, last, fresh, final, plan_ref, edge_ref, *refs):
    if fresh:
        weight_ref, refs = refs[0], refs[1:]
    else:
        refs = refs[2:]
    adj_ref, deg_ref, refs = refs[0], refs[1], refs[2:]
    width = adj_ref.shape[1]
    edges = edge_ref.shape[1]
    if fresh:
        deg_ref[...] = jnp.zeros_like(deg_ref)
        turn_ref = refs[0]
        for k in range(2):
            turn_ref[k] = weight_ref[k]
            turn_ref[2 + k] = weight_ref[k].T
    lanes = lax.broadcasted_iota(jnp.int32, (width, edges), 0).astype(jnp.bfloat16)

    def body(i, carry):
        base = pl.multiple_of(i * 8, 8)
        both = edge_ref[pl.ds(base, 8), :]
        src, dst = both & 255, both >> 8
        for j in range(8):
            spread, collect = one_hot(src[j : j + 1], lanes), one_hot(dst[j : j + 1], lanes)
            adj = lax.dot_general(spread, collect, NT, preferred_element_type=jnp.float32)
            adj_ref[base + j] = adj.astype(jnp.bfloat16)
            deg_ref[plan_ref[ROWS + base + j]] += jnp.sum(adj.reshape(width // 8, 8, width), axis=0)
        return carry

    lax.fori_loop(first, last, body, 0)
    if final:
        inv_ref = refs[0]
        blocks = inv_ref.shape[0]
        degree = jnp.sum(deg_ref[:blocks], axis=1, keepdims=True)
        inv_ref[...] = 1.0 / jnp.maximum(degree, 1.0)


def adjacency(k, plan, edges, blocks, width, weights=None, state=()):
    slots, count = edges.shape
    fresh, final = k == 0, k == len(CUTS) - 2
    outs = [
        jax.ShapeDtypeStruct((slots, width, width), jnp.bfloat16),
        jax.ShapeDtypeStruct((blocks + 1, 8, width), jnp.float32),
    ]
    if fresh:
        outs.append(jax.ShapeDtypeStruct((4,) + weights.shape[1:], jnp.bfloat16))
    if final:
        outs.append(jax.ShapeDtypeStruct((blocks, 1, width), jnp.float32))
    return call(
        functools.partial(adjacency_kernel, CUTS[k], CUTS[k + 1], fresh, final),
        outs,
        (edges, *((weights,) if fresh else state)),
        (plan,),
        aliases=None if fresh else {2: 0, 3: 1},
        flops=2 * 8 * (CUTS[k + 1] - CUTS[k]) * count * width * width,
        name="adjacency",
    )


def near_kernel(own_ref, less_ref, more_ref, over_ref, kept_ref, deg_ref, near_ref, one_ref, two_ref):
    rows = own_ref.shape[0]
    for k, ref in enumerate((own_ref, less_ref, more_ref, over_ref)):
        near_ref[k * rows : (k + 1) * rows] = ref[...]
    one_ref[...] = more_ref[...]
    two_ref[...] = over_ref[...]


def join_near(pieces, deg):
    rows, cols, width = pieces[0].shape
    return call(
        near_kernel,
        [jax.ShapeDtypeStruct(deg.shape, deg.dtype)]
        + [jax.ShapeDtypeStruct((n, cols, width), jnp.bfloat16) for n in (4 * rows, rows, rows)],
        (*pieces, deg),
        aliases={4: 0},
        name="join",
    )


def mid_kernel(more_ref, less_ref, two_ref, kept_ref, inv_ref, mid_ref, *outs):
    rows = more_ref.shape[0]
    third = rows // 3
    for k, ref in enumerate((more_ref, less_ref, two_ref)):
        mid_ref[k * rows : (k + 1) * rows] = ref[...]
    outs[0][...] = two_ref[:third]
    outs[1][...] = less_ref[third : 2 * third]
    outs[2][...] = more_ref[2 * third :]


def join_mid(pieces, inverse):
    rows, cols, width = pieces[0].shape
    sizes = (3 * rows,) + (rows // 3,) * 3
    return call(
        mid_kernel,
        [jax.ShapeDtypeStruct(inverse.shape, inverse.dtype)]
        + [jax.ShapeDtypeStruct((n, cols, width), jnp.bfloat16) for n in sizes],
        (*pieces, inverse),
        aliases={3: 0},
        name="join",
    )


def far_kernel(one_ref, two_ref, three_ref, kept_ref, sum_ref, far_ref):
    rows = one_ref.shape[0]
    for k, ref in enumerate((one_ref, two_ref, three_ref)):
        far_ref[k * rows : (k + 1) * rows] = ref[...]


def join_far(pieces, sums):
    rows, cols, width = pieces[0].shape
    return call(
        far_kernel,
        [
            jax.ShapeDtypeStruct(sums.shape, sums.dtype),
            jax.ShapeDtypeStruct((3 * rows, cols, width), jnp.bfloat16),
        ],
        (*pieces, sums),
        aliases={3: 0},
        name="join",
    )


def ranged(start, stop, body):
    def step(i, carry):
        for j in range(UNROLL):
            spot = start + i * UNROLL + j
            body(jnp.minimum(spot, stop - 1), spot < stop)
        return carry

    lax.fori_loop(0, (stop - start + UNROLL - 1) // UNROLL, step, 0)


def fields(item):
    return item & 127, (item >> 7) & 31, (item >> 12) & 31, (item >> 17) & 15, item >> 21


def mean_kernel(low, high, fresh, final, idle, plan_ref, adj_ref, here_ref, swap_ref, *refs):
    if not fresh:
        refs = refs[1:]
    if final:
        inv_ref, x_ref, cot_ref, refs = *refs[:3], refs[3:]
    refs = refs[idle:]
    sum_ref = refs[0]
    blocks = sum_ref.shape[0] - 1
    slots = adj_ref.shape[0]
    if fresh:
        sum_ref[...] = jnp.zeros_like(sum_ref)
    if final:
        out_ref = refs[1]
        parts, rows, cols, width = out_ref.shape
        rows = rows // 3
        out_ref[:, rows : 2 * rows] = x_ref[...].reshape(parts, rows, cols, width)
        out_ref[:, 2 * rows :] = cot_ref[...].reshape(parts, rows, cols, width)

    for core, feats_ref in enumerate((here_ref, swap_ref)):
        def add(spot, valid):
            slot, row, col, key, _ = fields(plan_ref[spot])
            place = (key - low - 8 * core) * blocks + col
            flow = jnp.dot(feats_ref[place], adj_ref[slot], preferred_element_type=jnp.float32)
            sum_ref[jnp.where(valid, row, blocks)] += flow

        ranged(plan_ref[slots + low + 8 * core], plan_ref[slots + high + 8 * core], add)
    if final:
        mean = (sum_ref[:blocks] * inv_ref[...]).astype(jnp.bfloat16)
        out_ref[:, :rows] = mean.reshape(parts, rows, cols, width)


def mean_stage(plan, adj, low, high, pieces, before=None, last=(), parts=0, idle=()):
    rows, cols, width = pieces[0].shape
    blocks = rows // (high - low)
    fresh, final = before is None, len(last) > 0
    outs = [jax.ShapeDtypeStruct((blocks + 1, cols, width), jnp.float32)]
    if final:
        outs.append(jax.ShapeDtypeStruct((parts, 3 * blocks // parts, cols, width), jnp.bfloat16))
    return call(
        functools.partial(mean_kernel, low, high, fresh, final, len(idle)),
        outs,
        [adj, *pieces] + ([] if fresh else [before]) + list(last),
        (plan,),
        aliases=None if fresh else {4: 0},
        flops=2 * (high - low) * 16 * width**3,
        idle=idle,
        name="neighbor_mean",
    )[-1]


def dense_kernel(plan_ref, in_ref, turn_ref, inv_ref, adj_ref, out_ref, kept_ref, gs_ref, gn_ref):
    parts, rows, cols, width = in_ref.shape
    rows = rows // 3
    feats = parts * cols
    here = plan_ref[HERE]
    for i in range(rows):
        mean = in_ref[:, i].reshape(feats, width)
        x = in_ref[:, rows + i].reshape(feats, width)
        cot = in_ref[:, 2 * rows + i].reshape(feats, width).astype(jnp.float32)
        preact = jnp.dot(turn_ref[2], x, preferred_element_type=jnp.float32)
        preact = preact + jnp.dot(turn_ref[3], mean, preferred_element_type=jnp.float32)
        gate = jax.nn.sigmoid(preact)
        hidden = (preact * gate).astype(jnp.bfloat16)
        out_ref[:, rows + i] = hidden.reshape(parts, cols, width)
        out_grad = (cot * gate * (1.0 + preact * (1.0 - gate))).astype(jnp.bfloat16)
        self_term = jnp.dot(turn_ref[0], out_grad, preferred_element_type=jnp.float32)
        out_ref[:, 2 * rows + i] = self_term.astype(jnp.bfloat16).reshape(parts, cols, width)
        pre = jnp.dot(turn_ref[1], out_grad, preferred_element_type=jnp.float32)
        pre = pre * inv_ref[here * rows + i]
        out_ref[:, i] = pre.astype(jnp.bfloat16).reshape(parts, cols, width)
        for ref, left in ((gs_ref, x), (gn_ref, mean)):
            term = lax.dot_general(left, out_grad, NT, preferred_element_type=jnp.float32)
            ref[...] = ref[...] + term if i else term
    for k, ref in enumerate((gs_ref, gn_ref)):
        out_ref[:, 3 * rows + k] = ref[...].astype(jnp.bfloat16).reshape(parts, cols, width)


def dense(plan, packed, turn, inverse, adj):
    parts, rows, cols, width = packed.shape
    feats = parts * cols
    grad = pltpu.VMEM((feats, feats), jnp.float32)
    return call(
        dense_kernel,
        [
            jax.ShapeDtypeStruct((parts, rows + 2, cols, width), jnp.bfloat16),
            jax.ShapeDtypeStruct(adj.shape, adj.dtype),
        ],
        (packed, turn, inverse, adj),
        (plan,),
        [grad, grad],
        aliases={4: 1},
        flops=4 * rows * width * feats * feats,
        name="dense",
    )


def back_kernel(
    low, high, adds, takes, cuts, tail, idle, plan_ref, grads_ref, adj_ref, *refs
):
    received, refs = refs[: len(adds)], refs[len(adds) :]
    tails, refs = refs[: len(takes)], refs[len(takes) :]
    outs, sum_ref = refs[idle + 1 :], refs[-1]
    slots = adj_ref.shape[0]
    total = sum_ref.shape[0] - 1
    blocks = total // (high - low)
    sum_ref[...] = jnp.zeros_like(sum_ref)
    for (at, rows, skip), ref in zip(adds, received):
        sum_ref[at : at + rows] += ref[skip : skip + rows].astype(jnp.float32)

    def add(spot, valid):
        slot, _, col, key, place = fields(plan_ref[spot])
        back = lax.dot_general(
            grads_ref[place], adj_ref[slot], NT, preferred_element_type=jnp.float32
        )
        spot = jnp.where(valid, (key - (low & 7)) * blocks + col - (low & 8) * blocks, total)
        sum_ref[spot] += back.astype(jnp.bfloat16).astype(jnp.float32)

    ranged(plan_ref[slots + low], plan_ref[slots + high], add)
    at = 0
    for (rows, with_tail), out in zip(cuts, outs):
        out[:rows] = sum_ref[at : at + rows].astype(out.dtype)
        at += rows
    if tail:
        if len(tails) == 1 and not takes[0]:
            chunks = tails[0]
            value = sum(
                chunks[k, -2:].astype(jnp.float32) for k in range(chunks.shape[0])
            )
        else:
            value = sum(
                ref[at : at + 2].astype(jnp.float32) for at, ref in zip(takes, tails)
            )
        value = value.astype(jnp.bfloat16)
        outs[len(cuts)][...] = value
        for (rows, with_tail), out in zip(cuts, outs):
            if with_tail:
                out[rows:] = value


def back_stage(plan, grads, adj, low, high, cuts, received=(), tails=(), idle=()):
    slots, width, _ = adj.shape
    cols = grads.shape[1]
    blocks = sum(rows for rows, _, _ in cuts) // (high - low)
    shapes = [
        jax.ShapeDtypeStruct((rows + (2 if with_tail else 0), cols, width), dtype)
        for rows, dtype, with_tail in cuts
    ]
    if tails:
        shapes.append(jax.ShapeDtypeStruct((2, cols, width), jnp.bfloat16))
    kept = jax.ShapeDtypeStruct(adj.shape, adj.dtype)
    count = 3 + len(received) + len(tails)
    return call(
        functools.partial(
            back_kernel,
            low,
            high,
            tuple((at, rows, sum(skip)) for at, rows, _, *skip in received),
            tuple(at for at, _ in tails),
            tuple((rows, with_tail) for rows, _, with_tail in cuts),
            len(tails) > 0,
            len(idle),
        ),
        [kept] + shapes + [jax.ShapeDtypeStruct(v.shape, v.dtype) for v in idle],
        (grads, adj, *[entry[2] for entry in received], *[v for _, v in tails]),
        (plan,),
        [pltpu.VMEM(((high - low) * blocks + 1, cols, width), jnp.float32)],
        aliases={2: 0, **{count + i: 1 + len(shapes) + i for i in range(len(idle))}},
        flops=2 * (high - low) * 8 * width**3,
        name="transposed_sums",
        idle=idle,
        idle_out=len(idle),
    )


def relay_kernel(
    z_more_ref, y_own_ref, y_more_ref, y_less_ref, z_two_ref, own_ref, rest_ref,
    up_ref, over_ref, sum_ref,
):
    rows, cols, width = y_own_ref.shape
    full = jnp.float32
    up = z_more_ref[...] + y_more_ref[...].astype(full)
    up_ref[:rows] = (up + z_two_ref[:rows].astype(full)).astype(jnp.bfloat16)
    up_ref[rows:] = z_two_ref[rows:]
    over_ref[...] = (y_own_ref[...] + y_less_ref[:rows].astype(full)).astype(jnp.bfloat16)
    per = rows // rest_ref.shape[0]
    term = rest_ref[:, 2 * per : 3 * per].reshape(rows, cols, width).astype(full)
    sum_ref[...] = own_ref[...] + term


def relay(*values):
    rows, cols, width = values[0].shape
    sizes = ((rows + 2, jnp.bfloat16), (rows, jnp.bfloat16), (rows, jnp.float32))
    shapes = [jax.ShapeDtypeStruct((n, cols, width), dtype) for n, dtype in sizes]
    return call(relay_kernel, shapes, values, name="relay")


def finish_kernel(
    scale, own_ref, less_ref, more_ref, over_ref, g_ref, down_ref, up_ref, input_ref, gs_ref, gn_ref
):
    blocks = own_ref.shape[0]
    full = jnp.float32
    back = own_ref[...] + less_ref[...].astype(full)
    back = back + more_ref[:blocks].astype(full) + over_ref[...].astype(full)
    input_ref[...] = back.astype(jnp.bfloat16)
    total = g_ref[...].astype(full) + more_ref[blocks:].astype(full)
    total = total + (down_ref[blocks:].astype(full) + up_ref[blocks:].astype(full))
    total = total * scale
    gs_ref[...] = total[0]
    gn_ref[...] = total[1]


def finish(scale, *values):
    blocks, cols, width = values[0].shape
    moved = jax.ShapeDtypeStruct((blocks, cols, width), jnp.bfloat16)
    grad = jax.ShapeDtypeStruct((cols, width), jnp.float32)
    return call(
        functools.partial(finish_kernel, scale), [moved, grad, grad], values, name="finish"
    )


def make_plan(tile_row, tile_owner, tile_col, tile_count, blocks):
    slots = tile_row.shape[0]
    ids = jnp.arange(slots, dtype=jnp.int32)
    me = lax.axis_index("blk").astype(jnp.int32)
    owner = tile_owner[:, 0]
    code = ((owner ^ me) >> 3) * 4 + (((owner >> 1) - (me >> 1)) & 3)
    view = sum(jnp.where(code == k, VIEW[k], 0) for k in range(8))
    key = view + 8 * ((owner ^ me) & 1)
    key = jnp.where(ids < tile_count[0], key, 16)
    moved = tile_row + 8 * (tile_row // 3)
    item = ids + (tile_row << 7) + (tile_col << 12) + ((key & 15) << 17) + (moved << 21)
    full = key * slots + ids
    rank = jnp.sum((full[None, :] < full[:, None]).astype(jnp.int32), axis=1)
    ordered = jnp.sum(jnp.where(rank[None, :] == ids[:, None], item[None, :], 0), axis=1)
    starts = jnp.sum((key[None, :] < jnp.arange(32, dtype=jnp.int32)[:, None]).astype(jnp.int32), axis=1)
    here = jnp.full((8,), lax.axis_index("col"), jnp.int32)
    rows = jnp.where(ids < tile_count[0], tile_row, blocks)
    return jnp.concatenate([ordered, starts, here, rows])


def local(
    features, cotangent, w_self, w_neigh, tile_row, tile_owner, tile_col, tile_count,
    edge_dst, edge_src,
):
    blocks, cols, width = features.shape
    n_blk, n_col = lax.axis_size("blk"), lax.axis_size("col")
    per = blocks // n_col
    third = blocks // 3

    def over_col(a, rows):
        moved = lax.all_to_all(a.reshape(n_col, rows * cols, width), "col", 0, 0)
        return moved.reshape(n_col, rows, cols, width)

    own = features
    z_less, z_more, y_own = send(own, "up"), send(own, "down"), send(own, "over")
    plan = make_plan(tile_row, tile_owner, tile_col, tile_count, blocks)
    build = functools.partial(
        adjacency, plan=plan, edges=edge_src + (edge_dst << 8), blocks=blocks, width=width
    )
    adj, deg, turn = build(0, weights=jnp.stack([w_self, w_neigh]))
    deg, near, z_more, y_own = join_near((own, z_less, z_more, y_own), deg)
    y_more, y_less, z_two = send(z_more, "over"), send(y_own, "up"), send(z_more, "down")
    near_swap = send(near, "core")
    adj, deg, inverse = build(1, state=(adj, deg))
    inverse, mid, *cut = join_mid((y_more, y_less, z_two), inverse)
    cut = [send(cut[0], "over"), send(cut[1], "up"), send(cut[2], "down")]
    mid_swap = send(mid, "core")
    sums = mean_stage(plan, adj, 0, 4, [near, near_swap], idle=(mid,))
    sums, y_two = join_far(cut, sums)
    y_swap = send(y_two, "core")
    sums = mean_stage(plan, adj, 4, 7, [mid, mid_swap], sums)
    packed = mean_stage(
        plan, adj, 7, 8, [y_two, y_swap], sums, (inverse, own, cotangent), n_col
    )

    out, adj = dense(plan, over_col(packed, 3 * per), turn, inverse, adj)
    moved = over_col(out, 3 * per + 2)
    hidden = moved[:, per : 2 * per].reshape(blocks, cols, width)
    grads = moved.reshape(n_col * (3 * per + 2), cols, width)

    half, full = jnp.bfloat16, jnp.float32
    back = functools.partial(back_stage, plan, grads)
    adj, far, g = back(adj, 12, 16, [(4 * blocks, half, True)], tails=[(0, moved)])
    far = send(far, "core")
    adj, near = back(adj, 8, 12, [(4 * blocks, half, False)])
    near = send(near, "core")
    adj, *cut, g = back(
        adj, 7, 8, [(third, half, True), (third, half, False), (third, half, False)],
        [(0, blocks, far, 3 * blocks)], [(0, g), (4 * blocks, far)],
    )
    cut = [send(cut[0], "over"), send(cut[1], "down"), send(cut[2], "up")]
    adj, own, z_less, z_more, y_own = back(
        adj, 0, 4,
        [(blocks, full, False), (blocks, half, False), (blocks, full, False), (blocks, full, False)],
        [(0, 4 * blocks, near)],
    )
    z_less = send(z_less, "down")
    adj, y_more, y_less, z_two, g = back(
        adj, 4, 7, [(blocks, half, False), (blocks, half, True), (blocks, half, True)],
        [(0, 3 * blocks, far), (2 * blocks, third, cut[0]), (blocks + third, third, cut[1]),
         (2 * third, third, cut[2])],
        [(0, g), (third, cut[0])],
    )
    y_more, y_less, z_two = send(y_more, "over"), send(y_less, "down"), send(z_two, "up")
    z_more, y_own, own = relay(z_more, y_own, y_more, y_less, z_two, own, moved)
    z_more, y_own = send(z_more, "up"), send(y_own, "over")
    scale = 1.0 / math.sqrt(blocks * width * n_blk)
    return (hidden, *finish(scale, own, z_less, z_more, y_own, g, y_less, z_two))


def solution(mesh):
    placed = (
        P("blk", "col", None),
        P("blk", "col", None),
        P(),
        P(),
        P("blk"),
        P("blk", None),
        P("blk"),
        P("blk"),
        P("blk", None),
        P("blk", None),
    )
    return jax.shard_map(
        local,
        mesh=mesh,
        in_specs=placed,
        out_specs=(P("blk", "col", None), P("blk", "col", None), P("col", None), P("col", None)),
        check_vma=False,
    )
```

time: 629 us -> 141 us (0.22)
  waiting for transfers between devices: 381 us -> 25.8 us
  matrix products: 146 us -> 0 us
  blocking collectives: 0 us -> 49.4 us
  local copies, waits for them, and re-layouts: 46.3 us -> 0.79 us
  Pallas kernels: 0 us -> 34.3 us
  other arithmetic: 29.3 us -> 3.95 us
  starting transfers between devices: 7.37 us -> 25 us
  between operations: 15.1 us -> 1.53 us
    reduce_scatter x3 -> x0, waiting for transfers between devices: 241 us -> none  [the longest x1 103 us: local(): lax.psum_scatter(self_full, 'col', scatter_dimension=1, tiled=True)]
    dot_general x41 -> x0, matrix products: 146 us -> none  [the longest x16 59.5 us: forward_tiles(): jnp.einsum('tfe,tek->tfk', picked, collect, preferred_element_type=jnp.fl...]
    all_gather x3 -> x0, waiting for transfers between devices: 105 us -> none  [the longest x1 61.1 us: local(): lax.all_gather(neighbor_mean, 'col', axis=1, tiled=True)]
    all_to_all x0 -> x2, blocking collectives: none -> 49.4 us  [over_col(): moved = lax.all_to_all(a.reshape(n_col, rows * cols, width), 'col', 0, 0)]
    pallas_call x0 -> x16, Pallas kernels: none -> 34.3 us  [call(): pl.pallas_call(kernel, in_specs=[SCALARS] * len(scalars) + [WHOLE] * len(...]
    ppermute x0 -> x23, waiting for transfers between devices: none -> 25.8 us  [send(): return lax.ppermute(value, 'blk', ROUTES[route])]
    ppermute x0 -> x23, starting transfers between devices: none -> 25 us  [send(): return lax.ppermute(value, 'blk', ROUTES[route])]
    eq x32 -> x0, local copies, waits for them, and re-layouts: 24 us -> none  [the longest x16 12.1 us: edge_tables(): dst_ids[..., None] == lane_index]
  transfers between devices with their start and end apart: 9 -> 23, of which waited for: 8 -> 10; matrix products, arithmetic and copies ran while one was open for 33% -> 3% of each run, Pallas kernels for 0% -> 17%
where the time goes in v2:
time: 141 us
  blocking collectives  49.4 us (35%)
  Pallas kernels  34.3 us (24%)
  waiting for transfers between devices  25.8 us (18%)
  starting transfers between devices  25 us (18%)
  other arithmetic  3.95 us (3%)
  between operations  1.53 us (1%)
    all_to_all x2, blocking collectives, over_col(): moved = lax.all_to_all(a.reshape(n_col, rows * cols, width), 'col', 0, 0)  49.4 us
    pallas_call x16, Pallas kernels, call(): pl.pallas_call(kernel, in_specs=[SCALARS] * len(scalars) + [WHOLE] * len(...  34.3 us
    ppermute x23, waiting for transfers between devices, send(): return lax.ppermute(value, 'blk', ROUTES[route])  25.8 us
    ppermute x23, starting transfers between devices, send(): return lax.ppermute(value, 'blk', ROUTES[route])  25 us
  transfers between devices with their start and end apart: 23, of which 10 were waited for; matrix products, arithmetic and copies ran while one was open for 3% of the time, Pallas kernels for 17%

profile of v2, /device:TPU:0, one launch (start us, length us, event | category | flops | bytes accessed | tf_op | source)
XLA Modules:
  0.0 140.8 jit_solution(17872472499254201919)
XLA Ops:
  0.6 2.1 %collective-permute-start = (bf16[24,32,256]{2,1,0:T(8,128)(2,1)}, bf16[24,32,256]{2,1,0:T(8,128)(2,1)S(1)}, u32[]{:S(2)}, u32[]{:S(2)}) collective-permute-start(bf16[24,32,256]{2,1,0:T(8,128)(2,1)} %refs_2_.1), channel_id=1, source_target_pairs={{0,16},{8,24},{16,32},{24,40},{32,48},{40,56},{48,0},{56,8},{64,80... | collective-permute-start | bytes 1179656 | tf_op jit(solution)/shard_map/ppermute | solution.py:38
  2.7 2.2 %collective-permute-start.1 = (bf16[24,32,256]{2,1,0:T(8,128)(2,1)}, bf16[24,32,256]{2,1,0:T(8,128)(2,1)S(1)}, u32[]{:S(2)}, u32[]{:S(2)}) collective-permute-start(bf16[24,32,256]{2,1,0:T(8,128)(2,1)} %refs_2_.1), channel_id=1, source_target_pairs={{0,48},{8,56},{16,0},{24,8},{32,16},{40,24},{48,32},{56,40},{64,11... | collective-permute-start | bytes 1179656 | tf_op jit(solution)/shard_map/ppermute | solution.py:38
  4.9 1.6 %collective-permute-start.2 = (bf16[24,32,256]{2,1,0:T(8,128)(2,1)}, bf16[24,32,256]{2,1,0:T(8,128)(2,1)S(1)}, u32[]{:S(2)}, u32[]{:S(2)}) collective-permute-start(bf16[24,32,256]{2,1,0:T(8,128)(2,1)} %refs_2_.1), channel_id=1, source_target_pairs={{0,64},{8,72},{16,80},{24,88},{32,96},{40,104},{48,112},{56,120},{... | collective-permute-start | bytes 1179656 | tf_op jit(solution)/shard_map/ppermute | solution.py:38
  7.1 0.7 fusion.9
  7.8 0.1 convert_reduce_fusion.1
  7.9 0.2 convert_reduce_fusion
  8.1 0.7 shift-left_add_fusion.1
  8.8 0.1 select_reduce_fusion
  8.9 1.1 shift-left_add_fusion.edge_ref
  10.0 1.0 pad_maximum_fusion.refs_0_
  11.0 0.1 pad_add_fusion.plan_ref
  11.1 5.8 %adjacency.2 = (bf16[128,256,256]{2,1,0:T(8,128)(2,1)S(1)}, f32[25,8,256]{2,1,0:T(8,128)S(1)}, bf16[4,256,256]{2,1,0:T(8,128)(2,1)S(1)}) custom-call(s32[296]{0:T(512)S(1)} %pad_add_fusion.plan_ref, s32[128,640]{1,0:T(8,128)S(1)} %shift-left_add_fusion.edge_ref, bf16[2,256,256]{2,1,0:T(8,128)(2,1)S(1)} %pad_maximum_fusion.refs_0_), custom_call_target="tpu_custom_call" | custom-call | flops 5368709120 | tf_op jit(solution)/shard_map/adjacency/pallas_call | solution.py:46
  17.0 0.0 collective-permute-done.1.more_ref
  17.0 0.0 collective-permute-done.2.over_ref
  17.0 0.2 join.3
  17.2 0.1 collective-permute-start.9
  17.3 0.5 collective-permute-start.3
  17.8 1.9 %collective-permute-start.5 = (bf16[24,32,256]{2,1,0:T(8,128)(2,1)S(1)}, bf16[24,32,256]{2,1,0:T(8,128)(2,1)S(1)}, u32[]{:S(2)}, u32[]{:S(2)}) collective-permute-start(bf16[24,32,256]{2,1,0:T(8,128)(2,1)S(1)} %get-tuple-element.52), channel_id=1, source_target_pairs={{0,48},{8,56},{16,0},{24,8},{32,16},{40,24},{48,32},{56,40},{64,11... | collective-permute-start | bytes 1179656 | tf_op jit(solution)/shard_map/ppermute | solution.py:38
  19.7 0.1 collective-permute-start.4
  19.8 5.8 %adjacency.3 = (bf16[128,256,256]{2,1,0:T(8,128)(2,1)S(1)}, f32[25,8,256]{2,1,0:T(8,128)S(1)}, f32[24,1,256]{2,1,0:T(1,128)S(1)}) custom-call(s32[296]{0:T(512)S(1)} %pad_add_fusion.plan_ref, s32[128,640]{1,0:T(8,128)S(1)} %shift-left_add_fusion.edge_ref, ...), custom_call_target="tpu_custom_call", output_to_operand_aliasing={{0}: (2, {}), {1}: (3, {})} | custom-call | flops 5368709120 | tf_op jit(solution)/shard_map/adjacency/pallas_call | solution.py:46
  25.6 3.2 %collective-permute-done.3.more_ref = bf16[24,32,256]{2,1,0:T(8,128)(2,1)S(1)} collective-permute-done((bf16[24,32,256]{2,1,0:T(8,128)(2,1)S(1)}, bf16[24,32,256]{2,1,0:T(8,128)(2,1)S(1)}, u32[]{:S(2)}, u32[]{:S(2)}) %collective-permute-start.3) | collective-permute-done | bytes 393248 | tf_op jit(solution)/shard_map/ppermute | solution.py:38
  28.8 0.2 collective-permute-done.5.two_ref
  29.0 2.9 %collective-permute-done.4.less_ref = bf16[24,32,256]{2,1,0:T(8,128)(2,1)S(1)} collective-permute-done((bf16[24,32,256]{2,1,0:T(8,128)(2,1)S(1)}, bf16[24,32,256]{2,1,0:T(8,128)(2,1)S(1)}, u32[]{:S(2)}, u32[]{:S(2)}) %collective-permute-start.4) | collective-permute-done | bytes 393248 | tf_op jit(solution)/shard_map/ppermute | solution.py:38
  31.8 0.1 join.4
  31.9 0.1 collective-permute-start.11
  32.0 1.7 %collective-permute-start.6 = (bf16[8,32,256]{2,1,0:T(8,128)(2,1)S(1)}, bf16[8,32,256]{2,1,0:T(8,128)(2,1)S(1)}, u32[]{:S(2)}, u32[]{:S(2)}) collective-permute-start(bf16[8,32,256]{2,1,0:T(8,128)(2,1)S(1)} %get-tuple-element.55), channel_id=1, source_target_pairs={{0,64},{8,72},{16,80},{24,88},{32,96},{40,104},{48,112},{56,120},{... | collective-permute-start | bytes 393224 | tf_op jit(solution)/shard_map/ppermute | solution.py:38
  33.7 0.0 collective-permute-start.7
  33.7 3.2 %collective-permute-start.8 = (bf16[8,32,256]{2,1,0:T(8,128)(2,1)S(1)}, bf16[8,32,256]{2,1,0:T(8,128)(2,1)S(1)}, u32[]{:S(2)}, u32[]{:S(2)}) collective-permute-start(bf16[8,32,256]{2,1,0:T(8,128)(2,1)S(1)} %get-tuple-element.57), channel_id=1, source_target_pairs={{0,48},{8,56},{16,0},{24,8},{32,16},{40,24},{48,32},{56,40},{64,11... | collective-permute-start | bytes 393224 | tf_op jit(solution)/shard_map/ppermute | solution.py:38
  36.9 0.0 collective-permute-done.9.swap_ref
  36.9 3.3 %neighbor_mean.3.kept_ref = f32[25,32,256]{2,1,0:T(8,128)S(1)} custom-call(s32[296]{0:T(512)S(1)} %pad_add_fusion.plan_ref, bf16[128,256,256]{2,1,0:T(8,128)(2,1)S(1)} %get-tuple-element.51.adj_ref, bf16[96,32,256]{2,1,0:T(8,128)(2,1)S(1)} %get-tuple-element.58.here_ref, bf16[96,32,256]{2,1,0:T(8,128)(2,1)S(1)} %collective-permute-done.9.swap_ref, ...), custom_call_target="tpu_custom_call" | custom-call | flops 2147483648 | tf_op jit(solution)/shard_map/neighbor_mean/pallas_call | solution.py:46
  40.2 0.0 collective-permute-done.6.one_ref
  40.3 0.2 collective-permute-done.7.two_ref
  40.5 0.1 collective-permute-start.10
  40.6 0.0 copy-start.1
  40.6 2.4 %neighbor_mean.4.refs_0_ = f32[25,32,256]{2,1,0:T(8,128)S(1)} custom-call(s32[296]{0:T(512)S(1)} %pad_add_fusion.plan_ref, bf16[128,256,256]{2,1,0:T(8,128)(2,1)S(1)} %get-tuple-element.51.adj_ref, bf16[72,32,256]{2,1,0:T(8,128)(2,1)S(1)} %get-tuple-element.59.refs_0_.here_ref, ...), custom_call_target="tpu_custom_call", output_to_operand_aliasing={{}: (4, {})} | custom-call | flops 1610612736 | tf_op jit(solution)/shard_map/neighbor_mean/pallas_call | solution.py:46
  43.0 1.6 %neighbor_mean.5 = (f32[25,32,256]{2,1,0:T(8,128)S(1)}, bf16[8,9,32,256]{3,2,1,0:T(8,128)(2,1)S(1)}) custom-call(s32[296]{0:T(512)S(1)} %pad_add_fusion.plan_ref, bf16[128,256,256]{2,1,0:T(8,128)(2,1)S(1)} %get-tuple-element.51.adj_ref, bf16[24,32,256]{2,1,0:T(8,128)(2,1)S(1)} %get-tuple-element.60.here_ref, ...), custom_call_target="tpu_custom_call", output_to_operand_aliasing={{0}: (4, {})} | custom-call | flops 536870912 | tf_op jit(solution)/shard_map/neighbor_mean/pallas_call | solution.py:46
  44.6 25.7 %all_to_all.10 = bf16[8,288,256]{2,1,0:T(8,128)(2,1)S(1)} all-to-all(bf16[8,288,256]{2,1,0:T(8,128)(2,1)S(1)} %bitcast.27), channel_id=1, replica_groups=mesh['blk'=16,'col'=8] {'col'}, dimensions={0} | all-to-all | bytes 2359296 | tf_op jit(solution)/shard_map/all_to_all | solution.py:450
  70.3 2.0 %dense.1 = (bf16[8,11,32,256]{3,2,1,0:T(8,128)(2,1)S(1)}, bf16[128,256,256]{2,1,0:T(8,128)(2,1)S(1)}) custom-call(s32[296]{0:T(512)S(1)} %pad_add_fusion.plan_ref, bf16[8,9,32,256]{3,2,1,0:T(8,128)(2,1)S(1)} %bitcast.25, bf16[4,256,256]{2,1,0:T(8,128)(2,1)S(1)} %get-tuple-element.64.turn_ref, ...), custom_call_target="tpu_custom_call", output_to_operand_aliasing={{1}: (4, {})} | custom-call | flops 603979776 | tf_op jit(solution)/shard_map/dense/pallas_call | solution.py:46
  72.3 23.7 %all_to_all.11 = bf16[8,352,256]{2,1,0:T(8,128)(2,1)S(1)} all-to-all(bf16[8,352,256]{2,1,0:T(8,128)(2,1)S(1)} %bitcast.26), channel_id=1, replica_groups=mesh['blk'=16,'col'=8] {'col'}, dimensions={0} | all-to-all | bytes 2883584 | tf_op jit(solution)/shard_map/all_to_all | solution.py:450
  96.0 3.1 %transposed_sums.5 = (bf16[128,256,256]{2,1,0:T(8,128)(2,1)S(1)}, bf16[98,32,256]{2,1,0:T(8,128)(2,1)S(1)}, bf16[2,32,256]{2,1,0:T(8,128)(2,1)S(1)}) custom-call(s32[296]{0:T(512)S(1)} %pad_add_fusion.plan_ref, bf16[88,32,256]{2,1,0:T(8,128)(2,1)S(1)} %bitcast.18, ...), custom_call_target="tpu_custom_call", output_to_operand_aliasing={{0}: (2, {})} | custom-call | flops 1073741824 | tf_op jit(solution)/shard_map/transposed_sums/pallas_call | solution.py:46
  99.1 0.1 collective-permute-start.12
  99.2 2.7 %transposed_sums.6 = (bf16[128,256,256]{2,1,0:T(8,128)(2,1)S(1)}, bf16[96,32,256]{2,1,0:T(8,128)(2,1)S(1)}) custom-call(s32[296]{0:T(512)S(1)} %pad_add_fusion.plan_ref, bf16[88,32,256]{2,1,0:T(8,128)(2,1)S(1)} %bitcast.19, bf16[128,256,256]{2,1,0:T(8,128)(2,1)S(1)} %get-tuple-element.67.adj_ref), custom_call_target="tpu_custom_call", output_to_operand_aliasing={{0}: (2, {})} | custom-call | flops 1073741824 | tf_op jit(solution)/shard_map/transposed_sums/pallas_call | solution.py:46
  101.8 1.0 collective-permute-start.13
  102.8 1.1 transposed_sums.7
  104.0 0.1 collective-permute-start.14
  104.1 1.8 %collective-permute-start.15 = (bf16[8,32,256]{2,1,0:T(8,128)(2,1)S(1)}, bf16[8,32,256]{2,1,0:T(8,128)(2,1)S(1)}, u32[]{:S(2)}, u32[]{:S(2)}) collective-permute-start(bf16[8,32,256]{2,1,0:T(8,128)(2,1)S(1)} %get-tuple-element.77), channel_id=1, source_target_pairs={{0,48},{8,56},{16,0},{24,8},{32,16},{40,24},{48,32},{56,40},{64,11... | collective-permute-start | bytes 393224 | tf_op jit(solution)/shard_map/ppermute | solution.py:38
  105.8 0.3 collective-permute-start.16
  106.2 3.2 %transposed_sums.8 = (bf16[128,256,256]{2,1,0:T(8,128)(2,1)S(1)}, f32[24,32,256]{2,1,0:T(8,128)S(1)}, bf16[24,32,256]{2,1,0:T(8,128)(2,1)S(1)}, f32[24,32,256]{2,1,0:T(8,128)S(1)}, f32[24,32,256]{2,1,0:T(8,128)S(1)}) custom-call(s32[296]{0:T(512)S(1)} %pad_add_fusion.plan_ref, bf16[88,32,256]{2,1,0:T(8,128)(2,1)S(1)} %bitcast.21, ...), custom_call_target="tpu_custom_call", output_to_operand_aliasing={{0}: (2, {})} | custom-call | flops 1073741824 | tf_op jit(solution)/shard_map/transposed_sums/pallas_call | solution.py:46
  109.4 0.6 collective-permute-done.15.refs_2_
  110.0 2.3 %collective-permute-done.16.refs_3_ = bf16[8,32,256]{2,1,0:T(8,128)(2,1)S(1)} collective-permute-done((bf16[8,32,256]{2,1,0:T(8,128)(2,1)S(1)}, bf16[8,32,256]{2,1,0:T(8,128)(2,1)S(1)}, u32[]{:S(2)}, u32[]{:S(2)}) %collective-permute-start.16) | collective-permute-done | bytes 131104 | tf_op jit(solution)/shard_map/ppermute | solution.py:38
  112.3 1.8 %transposed_sums.9 = (bf16[128,256,256]{2,1,0:T(8,128)(2,1)S(1)}, bf16[24,32,256]{2,1,0:T(8,128)(2,1)S(1)}, bf16[26,32,256]{2,1,0:T(8,128)(2,1)S(1)}, bf16[26,32...) custom-call(s32[296]{0:T(512)S(1)} %pad_add_fusion.plan_ref, ...), custom_call_target="tpu_custom_call", output_to_operand_aliasing={{0}: (2, {})} | custom-call | flops 805306368 | tf_op jit(solution)/shard_map/transposed_sums/pallas_call | solution.py:46
  114.2 0.4 collective-permute-start.18
  114.5 1.7 %collective-permute-start.19 = (bf16[26,32,256]{2,1,0:T(8,128)(2,1)S(1)}, bf16[26,32,256]{2,1,0:T(8,128)(2,1)S(1)}, u32[]{:S(2)}, u32[]{:S(2)}) collective-permute-start(bf16[26,32,256]{2,1,0:T(8,128)(2,1)S(1)} %get-tuple-element.82), channel_id=1, source_target_pairs={{0,16},{8,24},{16,32},{24,40},{32,48},{40,56},{48,0},{56,8},{64,80... | collective-permute-start | bytes 1277960 | tf_op jit(solution)/shard_map/ppermute | solution.py:38
  116.3 2.1 %collective-permute-start.17 = (bf16[24,32,256]{2,1,0:T(8,128)(2,1)S(1)}, bf16[24,32,256]{2,1,0:T(8,128)(2,1)S(1)}, u32[]{:S(2)}, u32[]{:S(2)}) collective-permute-start(bf16[24,32,256]{2,1,0:T(8,128)(2,1)S(1)} %get-tuple-element.80), channel_id=1, source_target_pairs={{0,64},{8,72},{16,80},{24,88},{32,96},{40,104},{48,112},{56,120},{... | collective-permute-start | bytes 1179656 | tf_op jit(solution)/shard_map/ppermute | solution.py:38
  118.4 8.2 %collective-permute-done.17.y_more_ref = bf16[24,32,256]{2,1,0:T(8,128)(2,1)S(1)} collective-permute-done((bf16[24,32,256]{2,1,0:T(8,128)(2,1)S(1)}, bf16[24,32,256]{2,1,0:T(8,128)(2,1)S(1)}, u32[]{:S(2)}, u32[]{:S(2)}) %collective-permute-start.17) | collective-permute-done | bytes 393248 | tf_op jit(solution)/shard_map/ppermute | solution.py:38
  126.6 0.5 collective-permute-done.19.z_two_ref.up_ref
  127.1 0.3 relay.1
  127.4 0.5 collective-permute-start.21
  127.9 2.8 %collective-permute-start.20 = (bf16[24,32,256]{2,1,0:T(8,128)(2,1)S(1)}, bf16[24,32,256]{2,1,0:T(8,128)(2,1)S(1)}, u32[]{:S(2)}, u32[]{:S(2)}) collective-permute-start(bf16[24,32,256]{2,1,0:T(8,128)(2,1)S(1)} %get-tuple-element.85), channel_id=1, source_target_pairs={{0,48},{8,56},{16,0},{24,8},{32,16},{40,24},{48,32},{56,40},{64,11... | collective-permute-start | bytes 1179656 | tf_op jit(solution)/shard_map/ppermute | solution.py:38
  130.7 0.7 collective-permute-start.22
  131.4 0.8 slice.4
  132.2 5.5 %collective-permute-done.20.less_ref = bf16[24,32,256]{2,1,0:T(8,128)(2,1)S(1)} collective-permute-done((bf16[24,32,256]{2,1,0:T(8,128)(2,1)S(1)}, bf16[24,32,256]{2,1,0:T(8,128)(2,1)S(1)}, u32[]{:S(2)}, u32[]{:S(2)}) %collective-permute-start.20) | collective-permute-done | bytes 393248 | tf_op jit(solution)/shard_map/ppermute | solution.py:38
  137.7 2.2 %collective-permute-done.22.over_ref = bf16[24,32,256]{2,1,0:T(8,128)(2,1)S(1)} collective-permute-done((bf16[24,32,256]{2,1,0:T(8,128)(2,1)S(1)}, bf16[24,32,256]{2,1,0:T(8,128)(2,1)S(1)}, u32[]{:S(2)}, u32[]{:S(2)}) %collective-permute-start.22) | collective-permute-done | bytes 393248 | tf_op jit(solution)/shard_map/ppermute | solution.py:38
  139.9 0.9 finish.1
  (15 shorter events, 0.1 us)
Async XLA Ops:
  0.6 16.3 %collective-permute-start = (bf16[24,32,256]{2,1,0:T(8,128)(2,1)}, bf16[24,32,256]{2,1,0:T(8,128)(2,1)S(1)}, u32[]{:S(2)}, u32[]{:S(2)}) collective-permute-start(bf16[24,32,256]{2,1,0:T(8,128)(2,1)} %refs_2_.1), channel_id=1, source_target_pairs={{0,16},{8,24},{16,32},{24,40},{32,48},{40,56},{48,0},{56,8},{64,80... | collective-permute-start | bytes 1179656 | tf_op jit(solution)/shard_map/ppermute | solution.py:38
  2.7 14.3 %collective-permute-start.1 = (bf16[24,32,256]{2,1,0:T(8,128)(2,1)}, bf16[24,32,256]{2,1,0:T(8,128)(2,1)S(1)}, u32[]{:S(2)}, u32[]{:S(2)}) collective-permute-start(bf16[24,32,256]{2,1,0:T(8,128)(2,1)} %refs_2_.1), channel_id=1, source_target_pairs={{0,48},{8,56},{16,0},{24,8},{32,16},{40,24},{48,32},{56,40},{64,11... | collective-permute-start | bytes 1179656 | tf_op jit(solution)/shard_map/ppermute | solution.py:38
  4.9 12.1 %collective-permute-start.2 = (bf16[24,32,256]{2,1,0:T(8,128)(2,1)}, bf16[24,32,256]{2,1,0:T(8,128)(2,1)S(1)}, u32[]{:S(2)}, u32[]{:S(2)}) collective-permute-start(bf16[24,32,256]{2,1,0:T(8,128)(2,1)} %refs_2_.1), channel_id=1, source_target_pairs={{0,64},{8,72},{16,80},{24,88},{32,96},{40,104},{48,112},{56,120},{... | collective-permute-start | bytes 1179656 | tf_op jit(solution)/shard_map/ppermute | solution.py:38
  11.1 5.9 %copy-start = (bf16[24,32,256]{2,1,0:T(8,128)(2,1)S(1)}, bf16[24,32,256]{2,1,0:T(8,128)(2,1)}, u32[]{:S(2)}) copy-start(bf16[24,32,256]{2,1,0:T(8,128)(2,1)} %refs_2_.1) | copy-start | bytes 1179652
  17.2 19.8 %collective-permute-start.9 = (bf16[96,32,256]{2,1,0:T(8,128)(2,1)S(1)}, bf16[96,32,256]{2,1,0:T(8,128)(2,1)S(1)}, u32[]{:S(2)}, u32[]{:S(2)}) collective-permute-start(bf16[96,32,256]{2,1,0:T(8,128)(2,1)S(1)} %get-tuple-element.58.here_ref), channel_id=1, source_target_pairs={{0,8},{8,0},{16,24},{24,16},{32,40},{40,32},{48,56},{56,48},{64,72... | collective-permute-start | bytes 4718600 | tf_op jit(solution)/shard_map/ppermute | solution.py:38
  17.3 11.5 %collective-permute-start.3 = (bf16[24,32,256]{2,1,0:T(8,128)(2,1)S(1)}, bf16[24,32,256]{2,1,0:T(8,128)(2,1)S(1)}, u32[]{:S(2)}, u32[]{:S(2)}) collective-permute-start(bf16[24,32,256]{2,1,0:T(8,128)(2,1)S(1)} %get-tuple-element.52), channel_id=1, source_target_pairs={{0,64},{8,72},{16,80},{24,88},{32,96},{40,104},{48,112},{56,120},{... | collective-permute-start | bytes 1179656 | tf_op jit(solution)/shard_map/ppermute | solution.py:38
  17.8 11.2 %collective-permute-start.5 = (bf16[24,32,256]{2,1,0:T(8,128)(2,1)S(1)}, bf16[24,32,256]{2,1,0:T(8,128)(2,1)S(1)}, u32[]{:S(2)}, u32[]{:S(2)}) collective-permute-start(bf16[24,32,256]{2,1,0:T(8,128)(2,1)S(1)} %get-tuple-element.52), channel_id=1, source_target_pairs={{0,48},{8,56},{16,0},{24,8},{32,16},{40,24},{48,32},{56,40},{64,11... | collective-permute-start | bytes 1179656 | tf_op jit(solution)/shard_map/ppermute | solution.py:38
  19.7 12.1 %collective-permute-start.4 = (bf16[24,32,256]{2,1,0:T(8,128)(2,1)S(1)}, bf16[24,32,256]{2,1,0:T(8,128)(2,1)S(1)}, u32[]{:S(2)}, u32[]{:S(2)}) collective-permute-start(bf16[24,32,256]{2,1,0:T(8,128)(2,1)S(1)} %get-tuple-element.53), channel_id=1, source_target_pairs={{0,16},{8,24},{16,32},{24,40},{32,48},{40,56},{48,0},{56,8},{64,80... | collective-permute-start | bytes 1179656 | tf_op jit(solution)/shard_map/ppermute | solution.py:38
  31.9 8.6 %collective-permute-start.11 = (bf16[72,32,256]{2,1,0:T(8,128)(2,1)S(1)}, bf16[72,32,256]{2,1,0:T(8,128)(2,1)S(1)}, u32[]{:S(2)}, u32[]{:S(2)}) collective-permute-start(bf16[72,32,256]{2,1,0:T(8,128)(2,1)S(1)} %get-tuple-element.59.refs_0_.here_ref), channel_id=1, source_target_pairs={{0,8},{8,0},{16,24},{24,16},{32,40},{40,32},{48,56},{56,48},{64,72... | collective-permute-start | bytes 3538952 | tf_op jit(solution)/shard_map/ppermute | solution.py:38
  32.0 8.2 %collective-permute-start.6 = (bf16[8,32,256]{2,1,0:T(8,128)(2,1)S(1)}, bf16[8,32,256]{2,1,0:T(8,128)(2,1)S(1)}, u32[]{:S(2)}, u32[]{:S(2)}) collective-permute-start(bf16[8,32,256]{2,1,0:T(8,128)(2,1)S(1)} %get-tuple-element.55), channel_id=1, source_target_pairs={{0,64},{8,72},{16,80},{24,88},{32,96},{40,104},{48,112},{56,120},{... | collective-permute-start | bytes 393224 | tf_op jit(solution)/shard_map/ppermute | solution.py:38
  33.7 6.8 %collective-permute-start.7 = (bf16[8,32,256]{2,1,0:T(8,128)(2,1)S(1)}, bf16[8,32,256]{2,1,0:T(8,128)(2,1)S(1)}, u32[]{:S(2)}, u32[]{:S(2)}) collective-permute-start(bf16[8,32,256]{2,1,0:T(8,128)(2,1)S(1)} %get-tuple-element.56), channel_id=1, source_target_pairs={{0,16},{8,24},{16,32},{24,40},{32,48},{40,56},{48,0},{56,8},{64,80... | collective-permute-start | bytes 393224 | tf_op jit(solution)/shard_map/ppermute | solution.py:38
  33.7 6.8 %collective-permute-start.8 = (bf16[8,32,256]{2,1,0:T(8,128)(2,1)S(1)}, bf16[8,32,256]{2,1,0:T(8,128)(2,1)S(1)}, u32[]{:S(2)}, u32[]{:S(2)}) collective-permute-start(bf16[8,32,256]{2,1,0:T(8,128)(2,1)S(1)} %get-tuple-element.57), channel_id=1, source_target_pairs={{0,48},{8,56},{16,0},{24,8},{32,16},{40,24},{48,32},{56,40},{64,11... | collective-permute-start | bytes 393224 | tf_op jit(solution)/shard_map/ppermute | solution.py:38
  40.5 2.5 %collective-permute-start.10 = (bf16[24,32,256]{2,1,0:T(8,128)(2,1)S(1)}, bf16[24,32,256]{2,1,0:T(8,128)(2,1)S(1)}, u32[]{:S(2)}, u32[]{:S(2)}) collective-permute-start(bf16[24,32,256]{2,1,0:T(8,128)(2,1)S(1)} %get-tuple-element.60.here_ref), channel_id=1, source_target_pairs={{0,8},{8,0},{16,24},{24,16},{32,40},{40,32},{48,56},{56,48},{64,72... | collective-permute-start | bytes 1179656 | tf_op jit(solution)/shard_map/ppermute | solution.py:38
  40.6 2.4 %copy-start.1 = (bf16[24,32,256]{2,1,0:T(8,128)(2,1)S(1)}, bf16[24,32,256]{2,1,0:T(8,128)(2,1)}, u32[]{:S(2)}) copy-start(bf16[24,32,256]{2,1,0:T(8,128)(2,1)} %refs_3_.1) | copy-start | bytes 1179652
  99.1 3.8 %collective-permute-start.12 = (bf16[98,32,256]{2,1,0:T(8,128)(2,1)S(1)}, bf16[98,32,256]{2,1,0:T(8,128)(2,1)S(1)}, u32[]{:S(2)}, u32[]{:S(2)}) collective-permute-start(bf16[98,32,256]{2,1,0:T(8,128)(2,1)S(1)} %get-tuple-element.69), channel_id=1, source_target_pairs={{0,8},{8,0},{16,24},{24,16},{32,40},{40,32},{48,56},{56,48},{64,72... | collective-permute-start | bytes 4816904 | tf_op jit(solution)/shard_map/ppermute | solution.py:38
  101.8 4.3 %collective-permute-start.13 = (bf16[96,32,256]{2,1,0:T(8,128)(2,1)S(1)}, bf16[96,32,256]{2,1,0:T(8,128)(2,1)S(1)}, u32[]{:S(2)}, u32[]{:S(2)}) collective-permute-start(bf16[96,32,256]{2,1,0:T(8,128)(2,1)S(1)} %get-tuple-element.72), channel_id=1, source_target_pairs={{0,8},{8,0},{16,24},{24,16},{32,40},{40,32},{48,56},{56,48},{64,72... | collective-permute-start | bytes 4718600 | tf_op jit(solution)/shard_map/ppermute | solution.py:38
  104.0 8.3 %collective-permute-start.14 = (bf16[10,32,256]{2,1,0:T(8,128)(2,1)S(1)}, bf16[10,32,256]{2,1,0:T(8,128)(2,1)S(1)}, u32[]{:S(2)}, u32[]{:S(2)}) collective-permute-start(bf16[10,32,256]{2,1,0:T(8,128)(2,1)S(1)} %get-tuple-element.76), channel_id=1, source_target_pairs={{0,64},{8,72},{16,80},{24,88},{32,96},{40,104},{48,112},{56,120},{... | collective-permute-start | bytes 491528 | tf_op jit(solution)/shard_map/ppermute | solution.py:38
  104.1 5.9 %collective-permute-start.15 = (bf16[8,32,256]{2,1,0:T(8,128)(2,1)S(1)}, bf16[8,32,256]{2,1,0:T(8,128)(2,1)S(1)}, u32[]{:S(2)}, u32[]{:S(2)}) collective-permute-start(bf16[8,32,256]{2,1,0:T(8,128)(2,1)S(1)} %get-tuple-element.77), channel_id=1, source_target_pairs={{0,48},{8,56},{16,0},{24,8},{32,16},{40,24},{48,32},{56,40},{64,11... | collective-permute-start | bytes 393224 | tf_op jit(solution)/shard_map/ppermute | solution.py:38
  105.8 6.5 %collective-permute-start.16 = (bf16[8,32,256]{2,1,0:T(8,128)(2,1)S(1)}, bf16[8,32,256]{2,1,0:T(8,128)(2,1)S(1)}, u32[]{:S(2)}, u32[]{:S(2)}) collective-permute-start(bf16[8,32,256]{2,1,0:T(8,128)(2,1)S(1)} %get-tuple-element.78), channel_id=1, source_target_pairs={{0,16},{8,24},{16,32},{24,40},{32,48},{40,56},{48,0},{56,8},{64,80... | collective-permute-start | bytes 393224 | tf_op jit(solution)/shard_map/ppermute | solution.py:38
  114.2 12.4 %collective-permute-start.18 = (bf16[26,32,256]{2,1,0:T(8,128)(2,1)S(1)}, bf16[26,32,256]{2,1,0:T(8,128)(2,1)S(1)}, u32[]{:S(2)}, u32[]{:S(2)}) collective-permute-start(bf16[26,32,256]{2,1,0:T(8,128)(2,1)S(1)} %get-tuple-element.81), channel_id=1, source_target_pairs={{0,48},{8,56},{16,0},{24,8},{32,16},{40,24},{48,32},{56,40},{64,11... | collective-permute-start | bytes 1277960 | tf_op jit(solution)/shard_map/ppermute | solution.py:38
  114.5 12.6 %collective-permute-start.19 = (bf16[26,32,256]{2,1,0:T(8,128)(2,1)S(1)}, bf16[26,32,256]{2,1,0:T(8,128)(2,1)S(1)}, u32[]{:S(2)}, u32[]{:S(2)}) collective-permute-start(bf16[26,32,256]{2,1,0:T(8,128)(2,1)S(1)} %get-tuple-element.82), channel_id=1, source_target_pairs={{0,16},{8,24},{16,32},{24,40},{32,48},{40,56},{48,0},{56,8},{64,80... | collective-permute-start | bytes 1277960 | tf_op jit(solution)/shard_map/ppermute | solution.py:38
  116.3 10.3 %collective-permute-start.17 = (bf16[24,32,256]{2,1,0:T(8,128)(2,1)S(1)}, bf16[24,32,256]{2,1,0:T(8,128)(2,1)S(1)}, u32[]{:S(2)}, u32[]{:S(2)}) collective-permute-start(bf16[24,32,256]{2,1,0:T(8,128)(2,1)S(1)} %get-tuple-element.80), channel_id=1, source_target_pairs={{0,64},{8,72},{16,80},{24,88},{32,96},{40,104},{48,112},{56,120},{... | collective-permute-start | bytes 1179656 | tf_op jit(solution)/shard_map/ppermute | solution.py:38
  127.4 12.5 %collective-permute-start.21 = (bf16[26,32,256]{2,1,0:T(8,128)(2,1)S(1)}, bf16[26,32,256]{2,1,0:T(8,128)(2,1)S(1)}, u32[]{:S(2)}, u32[]{:S(2)}) collective-permute-start(bf16[26,32,256]{2,1,0:T(8,128)(2,1)S(1)} %get-tuple-element.86), channel_id=1, source_target_pairs={{0,16},{8,24},{16,32},{24,40},{32,48},{40,56},{48,0},{56,8},{64,80... | collective-permute-start | bytes 1277960 | tf_op jit(solution)/shard_map/ppermute | solution.py:38
  127.9 9.8 %collective-permute-start.20 = (bf16[24,32,256]{2,1,0:T(8,128)(2,1)S(1)}, bf16[24,32,256]{2,1,0:T(8,128)(2,1)S(1)}, u32[]{:S(2)}, u32[]{:S(2)}) collective-permute-start(bf16[24,32,256]{2,1,0:T(8,128)(2,1)S(1)} %get-tuple-element.85), channel_id=1, source_target_pairs={{0,48},{8,56},{16,0},{24,8},{32,16},{40,24},{48,32},{56,40},{64,11... | collective-permute-start | bytes 1179656 | tf_op jit(solution)/shard_map/ppermute | solution.py:38
  130.7 9.2 %collective-permute-start.22 = (bf16[24,32,256]{2,1,0:T(8,128)(2,1)S(1)}, bf16[24,32,256]{2,1,0:T(8,128)(2,1)S(1)}, u32[]{:S(2)}, u32[]{:S(2)}) collective-permute-start(bf16[24,32,256]{2,1,0:T(8,128)(2,1)S(1)} %get-tuple-element.87), channel_id=1, source_target_pairs={{0,64},{8,72},{16,80},{24,88},{32,96},{40,104},{48,112},{56,120},{... | collective-permute-start | bytes 1179656 | tf_op jit(solution)/shard_map/ppermute | solution.py:38

commit v3 on v2

--- a/solution.py
+++ b/solution.py
@@ -8,15 +8,14 @@
 from jax.experimental.pallas import tpu as pltpu
 from jax.sharding import PartitionSpec as P
 
-UNROLL = 8
+UNROLL = 12
 HERE = 160
 ROWS = 168
-CUTS = (0, 8, 16)
+CUTS = (0, 4, 16)
 VMEM_BYTES = 14 * 1024 * 1024
 NT = (((1,), (1,)), ((), ()))
 WHOLE = pl.BlockSpec(memory_space=pltpu.VMEM)
 IDLE = pl.BlockSpec(memory_space=pl.ANY)
-SCALARS = pl.BlockSpec(memory_space=pltpu.SMEM)
 
 VIEW = (0, 2, 6, 1, 3, 4, 7, 5)
 
@@ -38,51 +37,53 @@
     return lax.ppermute(value, "blk", ROUTES[route])
 
 
+def with_plan(kernel, plan_ref, *refs):
+    *refs, held_ref, sem = refs
+    copy = pltpu.make_async_copy(plan_ref, held_ref, sem)
+    copy.start()
+    kernel(held_ref, copy.wait, *refs)
+
+
 def call(
-    kernel, out_shape, operands, scalars=(), scratch=(), aliases=None, flops=0, name=None,
-    idle=(), idle_out=0,
+    kernel, out_shape, operands, plan=None, scratch=(), aliases=None, name=None, idle=(), idle_out=0
 ):
-    out_specs = [WHOLE] * (len(out_shape) - idle_out) + [IDLE] * idle_out
+    scratch = list(scratch)
+    if plan is not None:
+        kernel = functools.partial(with_plan, kernel)
+        scratch += [pltpu.SMEM(plan.shape, plan.dtype), pltpu.SemaphoreType.DMA]
+    lead = [] if plan is None else [plan]
     return pl.pallas_call(
         kernel,
-        in_specs=[SCALARS] * len(scalars) + [WHOLE] * len(operands) + [IDLE] * len(idle),
-        out_specs=out_specs,
+        in_specs=[IDLE] * len(lead) + [WHOLE] * len(operands) + [IDLE] * len(idle),
+        out_specs=[WHOLE] * (len(out_shape) - idle_out) + [IDLE] * idle_out,
         out_shape=out_shape,
-        scratch_shapes=list(scratch),
+        scratch_shapes=scratch,
         input_output_aliases=aliases or {},
         compiler_params=pltpu.CompilerParams(vmem_limit_bytes=VMEM_BYTES),
-        cost_estimate=pl.CostEstimate(flops=flops, bytes_accessed=0, transcendentals=0),
         name=name,
-    )(*scalars, *operands, *idle)
+    )(*lead, *operands, *idle)
 
 
 def one_hot(ids, lanes):
-    hit = jnp.where(
-        lanes == ids.astype(jnp.bfloat16), jnp.ones((), jnp.bfloat16), jnp.zeros((), jnp.bfloat16)
-    )
-    return hit.astype(jnp.float8_e4m3fn)
-
-
-def adjacency_kernel(first, last, fresh, final, plan_ref, edge_ref, *refs):
-    if fresh:
-        weight_ref, refs = refs[0], refs[1:]
-    else:
+    one, zero = jnp.ones((), jnp.float8_e4m3fn), jnp.zeros((), jnp.float8_e4m3fn)
+    return jnp.where(lanes == ids, one, zero)
+
+
+def adjacency_kernel(first, last, fresh, final, plan_ref, ready, edge_ref, *refs):
+    if not fresh:
         refs = refs[2:]
     adj_ref, deg_ref, refs = refs[0], refs[1], refs[2:]
     width = adj_ref.shape[1]
     edges = edge_ref.shape[1]
     if fresh:
         deg_ref[...] = jnp.zeros_like(deg_ref)
-        turn_ref = refs[0]
-        for k in range(2):
-            turn_ref[k] = weight_ref[k]
-            turn_ref[2 + k] = weight_ref[k].T
-    lanes = lax.broadcasted_iota(jnp.int32, (width, edges), 0).astype(jnp.bfloat16)
+    lanes = lax.broadcasted_iota(jnp.int32, (width, edges), 0).astype(jnp.int8)
+    ready()
 
     def body(i, carry):
         base = pl.multiple_of(i * 8, 8)
         both = edge_ref[pl.ds(base, 8), :]
-        src, dst = both & 255, both >> 8
+        src, dst = (both & 255).astype(jnp.int8), (both >> 8).astype(jnp.int8)
         for j in range(8):
             spread, collect = one_hot(src[j : j + 1], lanes), one_hot(dst[j : j + 1], lanes)
             adj = lax.dot_general(spread, collect, NT, preferred_element_type=jnp.float32)
@@ -98,24 +99,21 @@
         inv_ref[...] = 1.0 / jnp.maximum(degree, 1.0)
 
 
-def adjacency(k, plan, edges, blocks, width, weights=None, state=()):
+def adjacency(k, plan, edges, blocks, width, state=()):
     slots, count = edges.shape
     fresh, final = k == 0, k == len(CUTS) - 2
     outs = [
         jax.ShapeDtypeStruct((slots, width, width), jnp.bfloat16),
         jax.ShapeDtypeStruct((blocks + 1, 8, width), jnp.float32),
     ]
-    if fresh:
-        outs.append(jax.ShapeDtypeStruct((4,) + weights.shape[1:], jnp.bfloat16))
     if final:
         outs.append(jax.ShapeDtypeStruct((blocks, 1, width), jnp.float32))
     return call(
         functools.partial(adjacency_kernel, CUTS[k], CUTS[k + 1], fresh, final),
         outs,
-        (edges, *((weights,) if fresh else state)),
-        (plan,),
+        (edges, *state),
+        plan,
         aliases=None if fresh else {2: 0, 3: 1},
-        flops=2 * 8 * (CUTS[k + 1] - CUTS[k]) * count * width * width,
         name="adjacency",
     )
 
@@ -140,7 +138,7 @@
     )
 
 
-def mid_kernel(more_ref, less_ref, two_ref, kept_ref, inv_ref, mid_ref, *outs):
+def mid_kernel(more_ref, less_ref, two_ref, kept_ref, sum_ref, mid_ref, *outs):
     rows = more_ref.shape[0]
     third = rows // 3
     for k, ref in enumerate((more_ref, less_ref, two_ref)):
@@ -150,14 +148,14 @@
     outs[2][...] = more_ref[2 * third :]
 
 
-def join_mid(pieces, inverse):
+def join_mid(pieces, kept):
     rows, cols, width = pieces[0].shape
     sizes = (3 * rows,) + (rows // 3,) * 3
     return call(
         mid_kernel,
-        [jax.ShapeDtypeStruct(inverse.shape, inverse.dtype)]
+        [jax.ShapeDtypeStruct(kept.shape, kept.dtype)]
         + [jax.ShapeDtypeStruct((n, cols, width), jnp.bfloat16) for n in sizes],
-        (*pieces, inverse),
+        (*pieces, kept),
         aliases={3: 0},
         name="join",
     )
@@ -197,12 +195,16 @@
     return item & 127, (item >> 7) & 31, (item >> 12) & 31, (item >> 17) & 15, item >> 21
 
 
-def mean_kernel(low, high, fresh, final, idle, plan_ref, adj_ref, here_ref, swap_ref, *refs):
+def mean_kernel(low, high, fresh, final, turns, idle, plan_ref, ready, adj_ref, here_ref, swap_ref, *refs):
     if not fresh:
         refs = refs[1:]
     if final:
         inv_ref, x_ref, cot_ref, refs = *refs[:3], refs[3:]
-    refs = refs[idle:]
+    if turns:
+        weight_ref, refs = refs[0], refs[1 + idle :]
+        for k in range(2):
+            refs[1][k] = weight_ref[k]
+            refs[1][2 + k] = weight_ref[k].T
     sum_ref = refs[0]
     blocks = sum_ref.shape[0] - 1
     slots = adj_ref.shape[0]
@@ -214,6 +216,7 @@
         rows = rows // 3
         out_ref[:, rows : 2 * rows] = x_ref[...].reshape(parts, rows, cols, width)
         out_ref[:, 2 * rows :] = cot_ref[...].reshape(parts, rows, cols, width)
+    ready()
 
     for core, feats_ref in enumerate((here_ref, swap_ref)):
         def add(spot, valid):
@@ -228,29 +231,32 @@
         out_ref[:, :rows] = mean.reshape(parts, rows, cols, width)
 
 
-def mean_stage(plan, adj, low, high, pieces, before=None, last=(), parts=0, idle=()):
+def mean_stage(plan, adj, low, high, pieces, before=None, last=(), parts=0, weights=None, idle=()):
     rows, cols, width = pieces[0].shape
     blocks = rows // (high - low)
     fresh, final = before is None, len(last) > 0
     outs = [jax.ShapeDtypeStruct((blocks + 1, cols, width), jnp.float32)]
     if final:
         outs.append(jax.ShapeDtypeStruct((parts, 3 * blocks // parts, cols, width), jnp.bfloat16))
-    return call(
-        functools.partial(mean_kernel, low, high, fresh, final, len(idle)),
+    turns = weights is not None
+    if turns:
+        outs.append(jax.ShapeDtypeStruct((4,) + weights.shape[1:], jnp.bfloat16))
+    return call(
+        functools.partial(mean_kernel, low, high, fresh, final, turns, len(idle)),
         outs,
-        [adj, *pieces] + ([] if fresh else [before]) + list(last),
-        (plan,),
+        [adj, *pieces] + ([] if fresh else [before]) + list(last) + ([weights] if turns else []),
+        plan,
         aliases=None if fresh else {4: 0},
-        flops=2 * (high - low) * 16 * width**3,
         idle=idle,
         name="neighbor_mean",
-    )[-1]
-
-
-def dense_kernel(plan_ref, in_ref, turn_ref, inv_ref, adj_ref, out_ref, kept_ref, gs_ref, gn_ref):
+    )
+
+
+def dense_kernel(plan_ref, ready, in_ref, turn_ref, inv_ref, adj_ref, out_ref, kept_ref, gs_ref, gn_ref):
     parts, rows, cols, width = in_ref.shape
     rows = rows // 3
     feats = parts * cols
+    ready()
     here = plan_ref[HERE]
     for i in range(rows):
         mean = in_ref[:, i].reshape(feats, width)
@@ -285,16 +291,15 @@
             jax.ShapeDtypeStruct(adj.shape, adj.dtype),
         ],
         (packed, turn, inverse, adj),
-        (plan,),
+        plan,
         [grad, grad],
         aliases={4: 1},
-        flops=4 * rows * width * feats * feats,
         name="dense",
     )
 
 
 def back_kernel(
-    low, high, adds, takes, cuts, tail, idle, plan_ref, grads_ref, adj_ref, *refs
+    low, high, adds, takes, cuts, tail, idle, plan_ref, ready, grads_ref, adj_ref, *refs
 ):
     received, refs = refs[: len(adds)], refs[len(adds) :]
     tails, refs = refs[: len(takes)], refs[len(takes) :]
@@ -305,6 +310,8 @@
     sum_ref[...] = jnp.zeros_like(sum_ref)
     for (at, rows, skip), ref in zip(adds, received):
         sum_ref[at : at + rows] += ref[skip : skip + rows].astype(jnp.float32)
+
+    ready()
 
     def add(spot, valid):
         slot, _, col, key, place = fields(plan_ref[spot])
@@ -336,7 +343,7 @@
                 out[rows:] = value
 
 
-def back_stage(plan, grads, adj, low, high, cuts, received=(), tails=(), idle=()):
+def back_stage(plan, grads, adj, low, high, cuts, received=(), tails=(), idle=(), name=None):
     slots, width, _ = adj.shape
     cols = grads.shape[1]
     blocks = sum(rows for rows, _, _ in cuts) // (high - low)
@@ -361,11 +368,10 @@
         ),
         [kept] + shapes + [jax.ShapeDtypeStruct(v.shape, v.dtype) for v in idle],
         (grads, adj, *[entry[2] for entry in received], *[v for _, v in tails]),
-        (plan,),
+        plan,
         [pltpu.VMEM(((high - low) * blocks + 1, cols, width), jnp.float32)],
         aliases={2: 0, **{count + i: 1 + len(shapes) + i for i in range(len(idle))}},
-        flops=2 * (high - low) * 8 * width**3,
-        name="transposed_sums",
+        name=name,
         idle=idle,
         idle_out=len(idle),
     )
@@ -456,7 +462,7 @@
     build = functools.partial(
         adjacency, plan=plan, edges=edge_src + (edge_dst << 8), blocks=blocks, width=width
     )
-    adj, deg, turn = build(0, weights=jnp.stack([w_self, w_neigh]))
+    adj, deg = build(0)
     deg, near, z_more, y_own = join_near((own, z_less, z_more, y_own), deg)
     y_more, y_less, z_two = send(z_more, "over"), send(y_own, "up"), send(z_more, "down")
     near_swap = send(near, "core")
@@ -464,11 +470,13 @@
     inverse, mid, *cut = join_mid((y_more, y_less, z_two), inverse)
     cut = [send(cut[0], "over"), send(cut[1], "up"), send(cut[2], "down")]
     mid_swap = send(mid, "core")
-    sums = mean_stage(plan, adj, 0, 4, [near, near_swap], idle=(mid,))
+    sums, turn = mean_stage(
+        plan, adj, 0, 4, [near, near_swap], weights=jnp.stack([w_self, w_neigh]), idle=(mid,)
+    )
     sums, y_two = join_far(cut, sums)
     y_swap = send(y_two, "core")
-    sums = mean_stage(plan, adj, 4, 7, [mid, mid_swap], sums)
-    packed = mean_stage(
+    (sums,) = mean_stage(plan, adj, 4, 7, [mid, mid_swap], sums)
+    _, packed = mean_stage(
         plan, adj, 7, 8, [y_two, y_swap], sums, (inverse, own, cotangent), n_col
     )
 
@@ -479,28 +487,30 @@
 
     half, full = jnp.bfloat16, jnp.float32
     back = functools.partial(back_stage, plan, grads)
-    adj, far, g = back(adj, 12, 16, [(4 * blocks, half, True)], tails=[(0, moved)])
+    adj, far, g = back(adj, 15, 16, name="sums_far_swap", cuts=[(blocks, half, True)], tails=[(0, moved)])
     far = send(far, "core")
-    adj, near = back(adj, 8, 12, [(4 * blocks, half, False)])
+    adj, mid = back(adj, 12, 15, name="sums_mid_swap", cuts=[(3 * blocks, half, False)])
+    adj, *cut, g, mid = back(
+        adj, 7, 8, name="sums_far_own", cuts=[(third, half, True), (third, half, False), (third, half, False)],
+        received=[(0, blocks, far)], tails=[(0, g), (blocks, far)], idle=(mid,),
+    )
+    mid = send(mid, "core")
+    cut = [send(cut[0], "over"), send(cut[1], "down"), send(cut[2], "up")]
+    adj, near = back(adj, 8, 12, name="sums_near_swap", cuts=[(4 * blocks, half, False)])
+    adj, y_more, y_less, z_two, g, near = back(
+        adj, 4, 7, name="sums_mid_own", cuts=[(blocks, half, False), (blocks, half, True), (blocks, half, True)],
+        received=[(0, 3 * blocks, mid), (2 * blocks, third, cut[0]), (blocks + third, third, cut[1]),
+         (2 * third, third, cut[2])],
+        tails=[(0, g), (third, cut[0])], idle=(near,),
+    )
     near = send(near, "core")
-    adj, *cut, g = back(
-        adj, 7, 8, [(third, half, True), (third, half, False), (third, half, False)],
-        [(0, blocks, far, 3 * blocks)], [(0, g), (4 * blocks, far)],
-    )
-    cut = [send(cut[0], "over"), send(cut[1], "down"), send(cut[2], "up")]
+    y_more, y_less, z_two = send(y_more, "over"), send(y_less, "down"), send(z_two, "up")
     adj, own, z_less, z_more, y_own = back(
-        adj, 0, 4,
+        adj, 0, 4, name="sums_near_own", cuts=
         [(blocks, full, False), (blocks, half, False), (blocks, full, False), (blocks, full, False)],
-        [(0, 4 * blocks, near)],
+        received=[(0, 4 * blocks, near)],
     )
     z_less = send(z_less, "down")
-    adj, y_more, y_less, z_two, g = back(
-        adj, 4, 7, [(blocks, half, False), (blocks, half, True), (blocks, half, True)],
-        [(0, 3 * blocks, far), (2 * blocks, third, cut[0]), (blocks + third, third, cut[1]),
-         (2 * third, third, cut[2])],
-        [(0, g), (third, cut[0])],
-    )
-    y_more, y_less, z_two = send(y_more, "over"), send(y_less, "down"), send(z_two, "up")
     z_more, y_own, own = relay(z_more, y_own, y_more, y_less, z_two, own, moved)
     z_more, y_own = send(z_more, "up"), send(y_own, "over")
     scale = 1.0 / math.sqrt(blocks * width * n_blk)

time: 141 us -> 140 us (level)
    ppermute x23 -> x24, waiting for transfers between devices: 25.8 us -> 26.8 us  [send(): return lax.ppermute(value, 'blk', ROUTES[route])]
    ppermute x23 -> x24, starting transfers between devices: 25 us -> 24.3 us  [send(): return lax.ppermute(value, 'blk', ROUTES[route])]
    pallas_call x16 -> x17, Pallas kernels: 34.3 us -> 33.8 us  [call(): pl.pallas_call(kernel, in_specs=[IDLE] * len(lead) + [WHOLE] * len(operan...]
  transfers between devices with their start and end apart: 23 -> 24, of which waited for: 10 -> 14; matrix products, arithmetic and copies ran while one was open for 3% -> 3% of each run, Pallas kernels for 17% -> 17%
where the time goes in v3:
time: 140 us
  blocking collectives  49.7 us (36%)
  Pallas kernels  33.8 us (24%)
  waiting for transfers between devices  26.8 us (19%)
  starting transfers between devices  24.3 us (17%)
  other arithmetic  2.97 us (2%)
  between operations  1.57 us (1%)
    all_to_all x2, blocking collectives, over_col(): moved = lax.all_to_all(a.reshape(n_col, rows * cols, width), 'col', 0, 0)  49.7 us
    pallas_call x17, Pallas kernels, call(): pl.pallas_call(kernel, in_specs=[IDLE] * len(lead) + [WHOLE] * len(operan...  33.8 us
    ppermute x24, waiting for transfers between devices, send(): return lax.ppermute(value, 'blk', ROUTES[route])  26.8 us
    ppermute x24, starting transfers between devices, send(): return lax.ppermute(value, 'blk', ROUTES[route])  24.3 us
  transfers between devices with their start and end apart: 24, of which 14 were waited for; matrix products, arithmetic and copies ran while one was open for 3% of the time, Pallas kernels for 17%

profile of v3, /device:TPU:0, one launch (start us, length us, event | category | flops | bytes accessed | tf_op | source)
XLA Modules:
  0.0 139.9 jit_solution(12236038133789544769)
XLA Ops:
  0.6 2.1 %collective-permute-start = (bf16[24,32,256]{2,1,0:T(8,128)(2,1)}, bf16[24,32,256]{2,1,0:T(8,128)(2,1)S(1)}, u32[]{:S(2)}, u32[]{:S(2)}) collective-permute-start(bf16[24,32,256]{2,1,0:T(8,128)(2,1)} %refs_5_.1), channel_id=1, source_target_pairs={{0,16},{8,24},{16,32},{24,40},{32,48},{40,56},{48,0},{56,8},{64,80... | collective-permute-start | bytes 1179656 | tf_op jit(solution)/shard_map/ppermute | solution.py:37
  2.7 2.2 %collective-permute-start.1 = (bf16[24,32,256]{2,1,0:T(8,128)(2,1)}, bf16[24,32,256]{2,1,0:T(8,128)(2,1)S(1)}, u32[]{:S(2)}, u32[]{:S(2)}) collective-permute-start(bf16[24,32,256]{2,1,0:T(8,128)(2,1)} %refs_5_.1), channel_id=1, source_target_pairs={{0,48},{8,56},{16,0},{24,8},{32,16},{40,24},{48,32},{56,40},{64,11... | collective-permute-start | bytes 1179656 | tf_op jit(solution)/shard_map/ppermute | solution.py:37
  4.9 1.6 %collective-permute-start.2 = (bf16[24,32,256]{2,1,0:T(8,128)(2,1)}, bf16[24,32,256]{2,1,0:T(8,128)(2,1)S(1)}, u32[]{:S(2)}, u32[]{:S(2)}) collective-permute-start(bf16[24,32,256]{2,1,0:T(8,128)(2,1)} %refs_5_.1), channel_id=1, source_target_pairs={{0,64},{8,72},{16,80},{24,88},{32,96},{40,104},{48,112},{56,120},{... | collective-permute-start | bytes 1179656 | tf_op jit(solution)/shard_map/ppermute | solution.py:37
  7.1 0.7 fusion.9
  7.8 0.2 convert_reduce_fusion
  8.0 0.7 shift-left_add_fusion.1
  8.7 0.1 select_reduce_fusion
  8.8 0.1 convert_reduce_fusion.1
  8.9 0.1 pad_add_fusion.plan_ref
  9.0 1.1 shift-left_add_fusion.refs_0_
  10.1 2.9 %adjacency.2 = (bf16[128,256,256]{2,1,0:T(8,128)(2,1)S(1)}, f32[25,8,256]{2,1,0:T(8,128)S(1)}) custom-call(s32[296]{0:T(512)S(1)} %pad_add_fusion.plan_ref, s32[128,640]{1,0:T(8,128)S(1)} %shift-left_add_fusion.refs_0_), custom_call_target="tpu_custom_call" | custom-call | tf_op jit(solution)/shard_map/adjacency/pallas_call | solution.py:55
  13.0 1.1 collective-permute-done.less_ref
  14.2 1.5 %collective-permute-done.2.over_ref = bf16[24,32,256]{2,1,0:T(8,128)(2,1)S(1)} collective-permute-done((bf16[24,32,256]{2,1,0:T(8,128)(2,1)}, bf16[24,32,256]{2,1,0:T(8,128)(2,1)S(1)}, u32[]{:S(2)}, u32[]{:S(2)}) %collective-permute-start.2) | collective-permute-done | bytes 393248 | tf_op jit(solution)/shard_map/ppermute | solution.py:37
  15.7 0.2 join.3
  15.9 0.1 collective-permute-start.9
  15.9 1.7 %collective-permute-start.3 = (bf16[24,32,256]{2,1,0:T(8,128)(2,1)S(1)}, bf16[24,32,256]{2,1,0:T(8,128)(2,1)S(1)}, u32[]{:S(2)}, u32[]{:S(2)}) collective-permute-start(bf16[24,32,256]{2,1,0:T(8,128)(2,1)S(1)} %get-tuple-element.57), channel_id=1, source_target_pairs={{0,64},{8,72},{16,80},{24,88},{32,96},{40,104},{48,112},{56,120},{... | collective-permute-start | bytes 1179656 | tf_op jit(solution)/shard_map/ppermute | solution.py:37
  17.6 1.7 %collective-permute-start.5 = (bf16[24,32,256]{2,1,0:T(8,128)(2,1)S(1)}, bf16[24,32,256]{2,1,0:T(8,128)(2,1)S(1)}, u32[]{:S(2)}, u32[]{:S(2)}) collective-permute-start(bf16[24,32,256]{2,1,0:T(8,128)(2,1)S(1)} %get-tuple-element.57), channel_id=1, source_target_pairs={{0,48},{8,56},{16,0},{24,8},{32,16},{40,24},{48,32},{56,40},{64,11... | collective-permute-start | bytes 1179656 | tf_op jit(solution)/shard_map/ppermute | solution.py:37
  19.3 0.4 collective-permute-start.4
  19.6 7.6 %adjacency.3 = (bf16[128,256,256]{2,1,0:T(8,128)(2,1)S(1)}, f32[25,8,256]{2,1,0:T(8,128)S(1)}, f32[24,1,256]{2,1,0:T(1,128)S(1)}) custom-call(s32[296]{0:T(512)S(1)} %pad_add_fusion.plan_ref, s32[128,640]{1,0:T(8,128)S(1)} %shift-left_add_fusion.refs_0_, ...), custom_call_target="tpu_custom_call", output_to_operand_aliasing={{0}: (2, {}), {1}: (3, {})} | custom-call | tf_op jit(solution)/shard_map/adjacency/pallas_call | solution.py:55
  27.2 0.2 collective-permute-done.3.more_ref
  27.5 1.3 collective-permute-done.5.two_ref
  28.8 2.6 %collective-permute-done.4.less_ref = bf16[24,32,256]{2,1,0:T(8,128)(2,1)S(1)} collective-permute-done((bf16[24,32,256]{2,1,0:T(8,128)(2,1)S(1)}, bf16[24,32,256]{2,1,0:T(8,128)(2,1)S(1)}, u32[]{:S(2)}, u32[]{:S(2)}) %collective-permute-start.4) | collective-permute-done | bytes 393248 | tf_op jit(solution)/shard_map/ppermute | solution.py:37
  31.4 0.1 join.4
  31.5 0.1 collective-permute-start.11
  31.6 0.5 collective-permute-start.6
  32.1 3.2 %collective-permute-start.8 = (bf16[8,32,256]{2,1,0:T(8,128)(2,1)S(1)}, bf16[8,32,256]{2,1,0:T(8,128)(2,1)S(1)}, u32[]{:S(2)}, u32[]{:S(2)}) collective-permute-start(bf16[8,32,256]{2,1,0:T(8,128)(2,1)S(1)} %get-tuple-element.62), channel_id=1, source_target_pairs={{0,48},{8,56},{16,0},{24,8},{32,16},{40,24},{48,32},{56,40},{64,11... | collective-permute-start | bytes 393224 | tf_op jit(solution)/shard_map/ppermute | solution.py:37
  35.4 0.0 collective-permute-done.9.refs_2_
  35.4 3.3 %neighbor_mean.3 = (f32[25,32,256]{2,1,0:T(8,128)S(1)}, bf16[4,256,256]{2,1,0:T(8,128)(2,1)S(1)}) custom-call(s32[296]{0:T(512)S(1)} %pad_add_fusion.plan_ref, bf16[128,256,256]{2,1,0:T(8,128)(2,1)S(1)} %get-tuple-element.56.refs_0_.refs_3_, bf16[96,32,256]{2,1,0:T(8,128)(2,1)S(1)} %get-tuple-element.63.refs_1_, ...), custom_call_target="tpu_custom_call" | custom-call | tf_op jit(solution)/shard_map/neighbor_mean/pallas_call | solution.py:55
  38.7 0.0 collective-permute-done.6.one_ref
  38.7 0.1 collective-permute-done.7.two_ref
  38.9 0.1 collective-permute-start.10
  39.0 0.0 copy-start.1
  39.0 2.5 %neighbor_mean.4.refs_3_ = f32[25,32,256]{2,1,0:T(8,128)S(1)} custom-call(s32[296]{0:T(512)S(1)} %pad_add_fusion.plan_ref, bf16[128,256,256]{2,1,0:T(8,128)(2,1)S(1)} %get-tuple-element.56.refs_0_.refs_3_, bf16[72,32,256]{2,1,0:T(8,128)(2,1)S(1)} %get-tuple-element.64.refs_4_.refs_1_, ...), custom_call_target="tpu_custom_call", output_to_operand_aliasing={{}: (4, {})} | custom-call | tf_op jit(solution)/shard_map/neighbor_mean/pallas_call | solution.py:55
  41.6 1.4 %neighbor_mean.5 = (f32[25,32,256]{2,1,0:T(8,128)S(1)}, bf16[8,9,32,256]{3,2,1,0:T(8,128)(2,1)S(1)}) custom-call(s32[296]{0:T(512)S(1)} %pad_add_fusion.plan_ref, bf16[128,256,256]{2,1,0:T(8,128)(2,1)S(1)} %get-tuple-element.56.refs_0_.refs_3_, bf16[24,32,256]{2,1,0:T(8,128)(2,1)S(1)} %get-tuple-element.66.refs_1_, ...), custom_call_target="tpu_custom_call", output_to_operand_aliasing={{0}: (4, {})} | custom-call | tf_op jit(solution)/shard_map/neighbor_mean/pallas_call | solution.py:55
  43.0 26.0 %all_to_all.10 = bf16[8,288,256]{2,1,0:T(8,128)(2,1)S(1)} all-to-all(bf16[8,288,256]{2,1,0:T(8,128)(2,1)S(1)} %bitcast.28), channel_id=1, replica_groups=mesh['blk'=16,'col'=8] {'col'}, dimensions={0} | all-to-all | bytes 2359296 | tf_op jit(solution)/shard_map/all_to_all | solution.py:456
  69.0 2.0 %dense.1 = (bf16[8,11,32,256]{3,2,1,0:T(8,128)(2,1)S(1)}, bf16[128,256,256]{2,1,0:T(8,128)(2,1)S(1)}) custom-call(s32[296]{0:T(512)S(1)} %pad_add_fusion.plan_ref, bf16[8,9,32,256]{3,2,1,0:T(8,128)(2,1)S(1)} %bitcast.26, bf16[4,256,256]{2,1,0:T(8,128)(2,1)S(1)} %get-tuple-element.70.refs_1_, ...), custom_call_target="tpu_custom_call", output_to_operand_aliasing={{1}: (4, {})} | custom-call | tf_op jit(solution)/shard_map/dense/pallas_call | solution.py:55
  71.0 23.7 %all_to_all.11 = bf16[8,352,256]{2,1,0:T(8,128)(2,1)S(1)} all-to-all(bf16[8,352,256]{2,1,0:T(8,128)(2,1)S(1)} %bitcast.27), channel_id=1, replica_groups=mesh['blk'=16,'col'=8] {'col'}, dimensions={0} | all-to-all | bytes 2883584 | tf_op jit(solution)/shard_map/all_to_all | solution.py:456
  94.7 1.3 sums_far_swap.1
  96.0 0.1 collective-permute-start.12
  96.1 1.9 %sums_mid_swap.1 = (bf16[128,256,256]{2,1,0:T(8,128)(2,1)S(1)}, bf16[72,32,256]{2,1,0:T(8,128)(2,1)S(1)}) custom-call(s32[296]{0:T(512)S(1)} %pad_add_fusion.plan_ref, bf16[88,32,256]{2,1,0:T(8,128)(2,1)S(1)} %bitcast.19, bf16[128,256,256]{2,1,0:T(8,128)(2,1)S(1)} %get-tuple-element.73.refs_1_), custom_call_target="tpu_custom_call", output_to_operand_aliasing={{0}: (2, {})} | custom-call | tf_op jit(solution)/shard_map/sums_mid_swap/pallas_call | solution.py:55
  98.0 1.2 sums_far_own.1
  99.2 1.2 collective-permute-start.13
  100.4 3.5 %collective-permute-start.15 = (bf16[8,32,256]{2,1,0:T(8,128)(2,1)S(1)}, bf16[8,32,256]{2,1,0:T(8,128)(2,1)S(1)}, u32[]{:S(2)}, u32[]{:S(2)}) collective-permute-start(bf16[8,32,256]{2,1,0:T(8,128)(2,1)S(1)} %get-tuple-element.82), channel_id=1, source_target_pairs={{0,48},{8,56},{16,0},{24,8},{32,16},{40,24},{48,32},{56,40},{64,11... | collective-permute-start | bytes 393224 | tf_op jit(solution)/shard_map/ppermute | solution.py:37
  103.9 0.0 collective-permute-start.16
  103.9 2.5 %sums_near_swap.1 = (bf16[128,256,256]{2,1,0:T(8,128)(2,1)S(1)}, bf16[96,32,256]{2,1,0:T(8,128)(2,1)S(1)}) custom-call(s32[296]{0:T(512)S(1)} %pad_add_fusion.plan_ref, bf16[88,32,256]{2,1,0:T(8,128)(2,1)S(1)} %bitcast.21, bf16[128,256,256]{2,1,0:T(8,128)(2,1)S(1)} %get-tuple-element.78.refs_1_), custom_call_target="tpu_custom_call", output_to_operand_aliasing={{0}: (2, {})} | custom-call | tf_op jit(solution)/shard_map/sums_near_swap/pallas_call | solution.py:55
  106.4 0.2 collective-permute-done.15.refs_4_
  106.6 3.4 %collective-permute-done.16.refs_5_ = bf16[8,32,256]{2,1,0:T(8,128)(2,1)S(1)} collective-permute-done((bf16[8,32,256]{2,1,0:T(8,128)(2,1)S(1)}, bf16[8,32,256]{2,1,0:T(8,128)(2,1)S(1)}, u32[]{:S(2)}, u32[]{:S(2)}) %collective-permute-start.16) | collective-permute-done | bytes 131104 | tf_op jit(solution)/shard_map/ppermute | solution.py:37
  110.1 2.5 %sums_mid_own.1 = (bf16[128,256,256]{2,1,0:T(8,128)(2,1)S(1)}, bf16[24,32,256]{2,1,0:T(8,128)(2,1)S(1)}, bf16[26,32,256]{2,1,0:T(8,128)(2,1)S(1)}, bf16[26,32,25...) custom-call(s32[296]{0:T(512)S(1)} %pad_add_fusion.plan_ref, ...), custom_call_target="tpu_custom_call", output_to_operand_aliasing={{0}: (2, {}), {5}: (9, {})} | custom-call | tf_op jit(solution)/shard_map/sums_mid_own/pallas_call | solution.py:55
  112.6 0.1 collective-permute-start.17
  112.7 0.1 collective-permute-start.19
  112.7 2.0 %collective-permute-start.20 = (bf16[26,32,256]{2,1,0:T(8,128)(2,1)S(1)}, bf16[26,32,256]{2,1,0:T(8,128)(2,1)S(1)}, u32[]{:S(2)}, u32[]{:S(2)}) collective-permute-start(bf16[26,32,256]{2,1,0:T(8,128)(2,1)S(1)} %get-tuple-element.92), channel_id=1, source_target_pairs={{0,16},{8,24},{16,32},{24,40},{32,48},{40,56},{48,0},{56,8},{64,80... | collective-permute-start | bytes 1277960 | tf_op jit(solution)/shard_map/ppermute | solution.py:37
  114.8 1.3 collective-permute-done.17.refs_2_
  116.1 3.1 %sums_near_own.1 = (bf16[128,256,256]{2,1,0:T(8,128)(2,1)S(1)}, f32[24,32,256]{2,1,0:T(8,128)S(1)}, bf16[24,32,256]{2,1,0:T(8,128)(2,1)S(1)}, f32[24,32,256]{2,1,0:T(8,128)S(1)}, f32[24,32,256]{2,1,0:T(8,128)S(1)}) custom-call(s32[296]{0:T(512)S(1)} %pad_add_fusion.plan_ref, bf16[88,32,256]{2,1,0:T(8,128)(2,1)S(1)} %bitcast.23, ...), custom_call_target="tpu_custom_call", output_to_operand_aliasing={{0}: (2, {})} | custom-call | tf_op jit(solution)/shard_map/sums_near_own/pallas_call | solution.py:55
  119.2 6.4 %collective-permute-done.18.y_more_ref = bf16[24,32,256]{2,1,0:T(8,128)(2,1)S(1)} collective-permute-done((bf16[24,32,256]{2,1,0:T(8,128)(2,1)S(1)}, bf16[24,32,256]{2,1,0:T(8,128)(2,1)S(1)}, u32[]{:S(2)}, u32[]{:S(2)}) %collective-permute-start.18) | collective-permute-done | bytes 393248 | tf_op jit(solution)/shard_map/ppermute | solution.py:37
  125.7 0.4 collective-permute-done.20.z_two_ref.up_ref
  126.1 0.3 relay.1
  126.4 0.6 collective-permute-start.22
  127.0 0.0 collective-permute-start.23
  127.0 3.1 %collective-permute-start.21 = (bf16[24,32,256]{2,1,0:T(8,128)(2,1)S(1)}, bf16[24,32,256]{2,1,0:T(8,128)(2,1)S(1)}, u32[]{:S(2)}, u32[]{:S(2)}) collective-permute-start(bf16[24,32,256]{2,1,0:T(8,128)(2,1)S(1)} %get-tuple-element.95), channel_id=1, source_target_pairs={{0,48},{8,56},{16,0},{24,8},{32,16},{40,24},{48,32},{56,40},{64,11... | collective-permute-start | bytes 1179656 | tf_op jit(solution)/shard_map/ppermute | solution.py:37
  130.2 0.8 slice.4
  130.9 6.2 %collective-permute-done.23.over_ref = bf16[24,32,256]{2,1,0:T(8,128)(2,1)S(1)} collective-permute-done((bf16[24,32,256]{2,1,0:T(8,128)(2,1)S(1)}, bf16[24,32,256]{2,1,0:T(8,128)(2,1)S(1)}, u32[]{:S(2)}, u32[]{:S(2)}) %collective-permute-start.23) | collective-permute-done | bytes 393248 | tf_op jit(solution)/shard_map/ppermute | solution.py:37
  137.1 0.4 collective-permute-done.21.less_ref
  137.5 1.4 %collective-permute-done.22.more_ref = bf16[26,32,256]{2,1,0:T(8,128)(2,1)S(1)} collective-permute-done((bf16[26,32,256]{2,1,0:T(8,128)(2,1)S(1)}, bf16[26,32,256]{2,1,0:T(8,128)(2,1)S(1)}, u32[]{:S(2)}, u32[]{:S(2)}) %collective-permute-start.22) | collective-permute-done | bytes 426016 | tf_op jit(solution)/shard_map/ppermute | solution.py:37
  138.9 0.9 finish.1
  (22 shorter events, 0.1 us)
Async XLA Ops:
  0.6 15.1 %copy-start = (bf16[24,32,256]{2,1,0:T(8,128)(2,1)S(1)}, bf16[24,32,256]{2,1,0:T(8,128)(2,1)}, u32[]{:S(2)}) copy-start(bf16[24,32,256]{2,1,0:T(8,128)(2,1)} %refs_5_.1) | copy-start | bytes 1179652
  0.6 13.5 %collective-permute-start = (bf16[24,32,256]{2,1,0:T(8,128)(2,1)}, bf16[24,32,256]{2,1,0:T(8,128)(2,1)S(1)}, u32[]{:S(2)}, u32[]{:S(2)}) collective-permute-start(bf16[24,32,256]{2,1,0:T(8,128)(2,1)} %refs_5_.1), channel_id=1, source_target_pairs={{0,16},{8,24},{16,32},{24,40},{32,48},{40,56},{48,0},{56,8},{64,80... | collective-permute-start | bytes 1179656 | tf_op jit(solution)/shard_map/ppermute | solution.py:37
  2.7 11.4 %collective-permute-start.1 = (bf16[24,32,256]{2,1,0:T(8,128)(2,1)}, bf16[24,32,256]{2,1,0:T(8,128)(2,1)S(1)}, u32[]{:S(2)}, u32[]{:S(2)}) collective-permute-start(bf16[24,32,256]{2,1,0:T(8,128)(2,1)} %refs_5_.1), channel_id=1, source_target_pairs={{0,48},{8,56},{16,0},{24,8},{32,16},{40,24},{48,32},{56,40},{64,11... | collective-permute-start | bytes 1179656 | tf_op jit(solution)/shard_map/ppermute | solution.py:37
  4.9 10.8 %collective-permute-start.2 = (bf16[24,32,256]{2,1,0:T(8,128)(2,1)}, bf16[24,32,256]{2,1,0:T(8,128)(2,1)S(1)}, u32[]{:S(2)}, u32[]{:S(2)}) collective-permute-start(bf16[24,32,256]{2,1,0:T(8,128)(2,1)} %refs_5_.1), channel_id=1, source_target_pairs={{0,64},{8,72},{16,80},{24,88},{32,96},{40,104},{48,112},{56,120},{... | collective-permute-start | bytes 1179656 | tf_op jit(solution)/shard_map/ppermute | solution.py:37
  15.9 19.5 %collective-permute-start.9 = (bf16[96,32,256]{2,1,0:T(8,128)(2,1)S(1)}, bf16[96,32,256]{2,1,0:T(8,128)(2,1)S(1)}, u32[]{:S(2)}, u32[]{:S(2)}) collective-permute-start(bf16[96,32,256]{2,1,0:T(8,128)(2,1)S(1)} %get-tuple-element.63.refs_1_), channel_id=1, source_target_pairs={{0,8},{8,0},{16,24},{24,16},{32,40},{40,32},{48,56},{56,48},{64,72... | collective-permute-start | bytes 4718600 | tf_op jit(solution)/shard_map/ppermute | solution.py:37
  15.9 11.5 %collective-permute-start.3 = (bf16[24,32,256]{2,1,0:T(8,128)(2,1)S(1)}, bf16[24,32,256]{2,1,0:T(8,128)(2,1)S(1)}, u32[]{:S(2)}, u32[]{:S(2)}) collective-permute-start(bf16[24,32,256]{2,1,0:T(8,128)(2,1)S(1)} %get-tuple-element.57), channel_id=1, source_target_pairs={{0,64},{8,72},{16,80},{24,88},{32,96},{40,104},{48,112},{56,120},{... | collective-permute-start | bytes 1179656 | tf_op jit(solution)/shard_map/ppermute | solution.py:37
  17.6 11.2 %collective-permute-start.5 = (bf16[24,32,256]{2,1,0:T(8,128)(2,1)S(1)}, bf16[24,32,256]{2,1,0:T(8,128)(2,1)S(1)}, u32[]{:S(2)}, u32[]{:S(2)}) collective-permute-start(bf16[24,32,256]{2,1,0:T(8,128)(2,1)S(1)} %get-tuple-element.57), channel_id=1, source_target_pairs={{0,48},{8,56},{16,0},{24,8},{32,16},{40,24},{48,32},{56,40},{64,11... | collective-permute-start | bytes 1179656 | tf_op jit(solution)/shard_map/ppermute | solution.py:37
  19.3 12.1 %collective-permute-start.4 = (bf16[24,32,256]{2,1,0:T(8,128)(2,1)S(1)}, bf16[24,32,256]{2,1,0:T(8,128)(2,1)S(1)}, u32[]{:S(2)}, u32[]{:S(2)}) collective-permute-start(bf16[24,32,256]{2,1,0:T(8,128)(2,1)S(1)} %get-tuple-element.58), channel_id=1, source_target_pairs={{0,16},{8,24},{16,32},{24,40},{32,48},{40,56},{48,0},{56,8},{64,80... | collective-permute-start | bytes 1179656 | tf_op jit(solution)/shard_map/ppermute | solution.py:37
  19.6 15.7 %copy-start.2 = (bf16[256,256]{1,0:T(8,128)(2,1)S(1)}, bf16[256,256]{1,0:T(8,128)(2,1)}, u32[]{:S(2)}) copy-start(bf16[256,256]{1,0:T(8,128)(2,1)} %param.13) | copy-start | bytes 393220
  19.6 15.7 %copy-start.3 = (bf16[256,256]{1,0:T(8,128)(2,1)S(1)}, bf16[256,256]{1,0:T(8,128)(2,1)}, u32[]{:S(2)}) copy-start(bf16[256,256]{1,0:T(8,128)(2,1)} %param.12) | copy-start | bytes 393220
  31.5 7.5 %collective-permute-start.11 = (bf16[72,32,256]{2,1,0:T(8,128)(2,1)S(1)}, bf16[72,32,256]{2,1,0:T(8,128)(2,1)S(1)}, u32[]{:S(2)}, u32[]{:S(2)}) collective-permute-start(bf16[72,32,256]{2,1,0:T(8,128)(2,1)S(1)} %get-tuple-element.64.refs_4_.refs_1_), channel_id=1, source_target_pairs={{0,8},{8,0},{16,24},{24,16},{32,40},{40,32},{48,56},{56,48},{64,72... | collective-permute-start | bytes 3538952 | tf_op jit(solution)/shard_map/ppermute | solution.py:37
  31.6 7.1 %collective-permute-start.6 = (bf16[8,32,256]{2,1,0:T(8,128)(2,1)S(1)}, bf16[8,32,256]{2,1,0:T(8,128)(2,1)S(1)}, u32[]{:S(2)}, u32[]{:S(2)}) collective-permute-start(bf16[8,32,256]{2,1,0:T(8,128)(2,1)S(1)} %get-tuple-element.60), channel_id=1, source_target_pairs={{0,64},{8,72},{16,80},{24,88},{32,96},{40,104},{48,112},{56,120},{... | collective-permute-start | bytes 393224 | tf_op jit(solution)/shard_map/ppermute | solution.py:37
  32.1 6.8 %collective-permute-start.7 = (bf16[8,32,256]{2,1,0:T(8,128)(2,1)S(1)}, bf16[8,32,256]{2,1,0:T(8,128)(2,1)S(1)}, u32[]{:S(2)}, u32[]{:S(2)}) collective-permute-start(bf16[8,32,256]{2,1,0:T(8,128)(2,1)S(1)} %get-tuple-element.61), channel_id=1, source_target_pairs={{0,16},{8,24},{16,32},{24,40},{32,48},{40,56},{48,0},{56,8},{64,80... | collective-permute-start | bytes 393224 | tf_op jit(solution)/shard_map/ppermute | solution.py:37
  32.1 6.8 %collective-permute-start.8 = (bf16[8,32,256]{2,1,0:T(8,128)(2,1)S(1)}, bf16[8,32,256]{2,1,0:T(8,128)(2,1)S(1)}, u32[]{:S(2)}, u32[]{:S(2)}) collective-permute-start(bf16[8,32,256]{2,1,0:T(8,128)(2,1)S(1)} %get-tuple-element.62), channel_id=1, source_target_pairs={{0,48},{8,56},{16,0},{24,8},{32,16},{40,24},{48,32},{56,40},{64,11... | collective-permute-start | bytes 393224 | tf_op jit(solution)/shard_map/ppermute | solution.py:37
  38.9 2.7 %collective-permute-start.10 = (bf16[24,32,256]{2,1,0:T(8,128)(2,1)S(1)}, bf16[24,32,256]{2,1,0:T(8,128)(2,1)S(1)}, u32[]{:S(2)}, u32[]{:S(2)}) collective-permute-start(bf16[24,32,256]{2,1,0:T(8,128)(2,1)S(1)} %get-tuple-element.66.refs_1_), channel_id=1, source_target_pairs={{0,8},{8,0},{16,24},{24,16},{32,40},{40,32},{48,56},{56,48},{64,72... | collective-permute-start | bytes 1179656 | tf_op jit(solution)/shard_map/ppermute | solution.py:37
  39.0 2.6 %copy-start.1 = (bf16[24,32,256]{2,1,0:T(8,128)(2,1)S(1)}, bf16[24,32,256]{2,1,0:T(8,128)(2,1)}, u32[]{:S(2)}) copy-start(bf16[24,32,256]{2,1,0:T(8,128)(2,1)} %refs_6_.1) | copy-start | bytes 1179652
  96.0 2.0 %collective-permute-start.12 = (bf16[26,32,256]{2,1,0:T(8,128)(2,1)S(1)}, bf16[26,32,256]{2,1,0:T(8,128)(2,1)S(1)}, u32[]{:S(2)}, u32[]{:S(2)}) collective-permute-start(bf16[26,32,256]{2,1,0:T(8,128)(2,1)S(1)} %get-tuple-element.75), channel_id=1, source_target_pairs={{0,8},{8,0},{16,24},{24,16},{32,40},{40,32},{48,56},{56,48},{64,72... | collective-permute-start | bytes 1277960 | tf_op jit(solution)/shard_map/ppermute | solution.py:37
  99.2 10.9 %collective-permute-start.13 = (bf16[72,32,256]{2,1,0:T(8,128)(2,1)S(1)}, bf16[72,32,256]{2,1,0:T(8,128)(2,1)S(1)}, u32[]{:S(2)}, u32[]{:S(2)}) collective-permute-start(bf16[72,32,256]{2,1,0:T(8,128)(2,1)S(1)} %get-tuple-element.80), channel_id=1, source_target_pairs={{0,8},{8,0},{16,24},{24,16},{32,40},{40,32},{48,56},{56,48},{64,72... | collective-permute-start | bytes 3538952 | tf_op jit(solution)/shard_map/ppermute | solution.py:37
  100.4 9.7 %collective-permute-start.14 = (bf16[10,32,256]{2,1,0:T(8,128)(2,1)S(1)}, bf16[10,32,256]{2,1,0:T(8,128)(2,1)S(1)}, u32[]{:S(2)}, u32[]{:S(2)}) collective-permute-start(bf16[10,32,256]{2,1,0:T(8,128)(2,1)S(1)} %get-tuple-element.81), channel_id=1, source_target_pairs={{0,64},{8,72},{16,80},{24,88},{32,96},{40,104},{48,112},{56,120},{... | collective-permute-start | bytes 491528 | tf_op jit(solution)/shard_map/ppermute | solution.py:37
  100.4 6.2 %collective-permute-start.15 = (bf16[8,32,256]{2,1,0:T(8,128)(2,1)S(1)}, bf16[8,32,256]{2,1,0:T(8,128)(2,1)S(1)}, u32[]{:S(2)}, u32[]{:S(2)}) collective-permute-start(bf16[8,32,256]{2,1,0:T(8,128)(2,1)S(1)} %get-tuple-element.82), channel_id=1, source_target_pairs={{0,48},{8,56},{16,0},{24,8},{32,16},{40,24},{48,32},{56,40},{64,11... | collective-permute-start | bytes 393224 | tf_op jit(solution)/shard_map/ppermute | solution.py:37
  103.9 6.2 %collective-permute-start.16 = (bf16[8,32,256]{2,1,0:T(8,128)(2,1)S(1)}, bf16[8,32,256]{2,1,0:T(8,128)(2,1)S(1)}, u32[]{:S(2)}, u32[]{:S(2)}) collective-permute-start(bf16[8,32,256]{2,1,0:T(8,128)(2,1)S(1)} %get-tuple-element.83), channel_id=1, source_target_pairs={{0,16},{8,24},{16,32},{24,40},{32,48},{40,56},{48,0},{56,8},{64,80... | collective-permute-start | bytes 393224 | tf_op jit(solution)/shard_map/ppermute | solution.py:37
  112.6 3.5 %collective-permute-start.17 = (bf16[96,32,256]{2,1,0:T(8,128)(2,1)S(1)}, bf16[96,32,256]{2,1,0:T(8,128)(2,1)S(1)}, u32[]{:S(2)}, u32[]{:S(2)}) collective-permute-start(bf16[96,32,256]{2,1,0:T(8,128)(2,1)S(1)} %get-tuple-element.87), channel_id=1, source_target_pairs={{0,8},{8,0},{16,24},{24,16},{32,40},{40,32},{48,56},{56,48},{64,72... | collective-permute-start | bytes 4718600 | tf_op jit(solution)/shard_map/ppermute | solution.py:37
  112.7 13.0 %collective-permute-start.19 = (bf16[26,32,256]{2,1,0:T(8,128)(2,1)S(1)}, bf16[26,32,256]{2,1,0:T(8,128)(2,1)S(1)}, u32[]{:S(2)}, u32[]{:S(2)}) collective-permute-start(bf16[26,32,256]{2,1,0:T(8,128)(2,1)S(1)} %get-tuple-element.91), channel_id=1, source_target_pairs={{0,48},{8,56},{16,0},{24,8},{32,16},{40,24},{48,32},{56,40},{64,11... | collective-permute-start | bytes 1277960 | tf_op jit(solution)/shard_map/ppermute | solution.py:37
  112.7 13.3 %collective-permute-start.20 = (bf16[26,32,256]{2,1,0:T(8,128)(2,1)S(1)}, bf16[26,32,256]{2,1,0:T(8,128)(2,1)S(1)}, u32[]{:S(2)}, u32[]{:S(2)}) collective-permute-start(bf16[26,32,256]{2,1,0:T(8,128)(2,1)S(1)} %get-tuple-element.92), channel_id=1, source_target_pairs={{0,16},{8,24},{16,32},{24,40},{32,48},{40,56},{48,0},{56,8},{64,80... | collective-permute-start | bytes 1277960 | tf_op jit(solution)/shard_map/ppermute | solution.py:37
  114.8 10.9 %collective-permute-start.18 = (bf16[24,32,256]{2,1,0:T(8,128)(2,1)S(1)}, bf16[24,32,256]{2,1,0:T(8,128)(2,1)S(1)}, u32[]{:S(2)}, u32[]{:S(2)}) collective-permute-start(bf16[24,32,256]{2,1,0:T(8,128)(2,1)S(1)} %get-tuple-element.90), channel_id=1, source_target_pairs={{0,64},{8,72},{16,80},{24,88},{32,96},{40,104},{48,112},{56,120},{... | collective-permute-start | bytes 1179656 | tf_op jit(solution)/shard_map/ppermute | solution.py:37
  126.4 12.5 %collective-permute-start.22 = (bf16[26,32,256]{2,1,0:T(8,128)(2,1)S(1)}, bf16[26,32,256]{2,1,0:T(8,128)(2,1)S(1)}, u32[]{:S(2)}, u32[]{:S(2)}) collective-permute-start(bf16[26,32,256]{2,1,0:T(8,128)(2,1)S(1)} %get-tuple-element.96), channel_id=1, source_target_pairs={{0,16},{8,24},{16,32},{24,40},{32,48},{40,56},{48,0},{56,8},{64,80... | collective-permute-start | bytes 1277960 | tf_op jit(solution)/shard_map/ppermute | solution.py:37
  127.0 10.1 %collective-permute-start.23 = (bf16[24,32,256]{2,1,0:T(8,128)(2,1)S(1)}, bf16[24,32,256]{2,1,0:T(8,128)(2,1)S(1)}, u32[]{:S(2)}, u32[]{:S(2)}) collective-permute-start(bf16[24,32,256]{2,1,0:T(8,128)(2,1)S(1)} %get-tuple-element.97), channel_id=1, source_target_pairs={{0,64},{8,72},{16,80},{24,88},{32,96},{40,104},{48,112},{56,120},{... | collective-permute-start | bytes 1179656 | tf_op jit(solution)/shard_map/ppermute | solution.py:37
  127.0 10.5 %collective-permute-start.21 = (bf16[24,32,256]{2,1,0:T(8,128)(2,1)S(1)}, bf16[24,32,256]{2,1,0:T(8,128)(2,1)S(1)}, u32[]{:S(2)}, u32[]{:S(2)}) collective-permute-start(bf16[24,32,256]{2,1,0:T(8,128)(2,1)S(1)} %get-tuple-element.95), channel_id=1, source_target_pairs={{0,48},{8,56},{16,0},{24,8},{32,16},{40,24},{48,32},{56,40},{64,11... | collective-permute-start | bytes 1179656 | tf_op jit(solution)/shard_map/ppermute | solution.py:37

commit v4 on v3

--- a/solution.py
+++ b/solution.py
@@ -11,7 +11,7 @@
 UNROLL = 12
 HERE = 160
 ROWS = 168
-CUTS = (0, 4, 16)
+CUTS = (0, 11, 16)
 VMEM_BYTES = 14 * 1024 * 1024
 NT = (((1,), (1,)), ((), ()))
 WHOLE = pl.BlockSpec(memory_space=pltpu.VMEM)
@@ -69,9 +69,8 @@
     return jnp.where(lanes == ids, one, zero)
 
 
-def adjacency_kernel(first, last, fresh, final, plan_ref, ready, edge_ref, *refs):
-    if not fresh:
-        refs = refs[2:]
+def adjacency_kernel(first, last, fresh, final, idle, plan_ref, ready, edge_ref, *refs):
+    refs = refs[idle:] if fresh else refs[2 + idle :]
     adj_ref, deg_ref, refs = refs[0], refs[1], refs[2:]
     width = adj_ref.shape[1]
     edges = edge_ref.shape[1]
@@ -99,7 +98,7 @@
         inv_ref[...] = 1.0 / jnp.maximum(degree, 1.0)
 
 
-def adjacency(k, plan, edges, blocks, width, state=()):
+def adjacency(k, plan, edges, blocks, width, state=(), idle=()):
     slots, count = edges.shape
     fresh, final = k == 0, k == len(CUTS) - 2
     outs = [
@@ -109,54 +108,48 @@
     if final:
         outs.append(jax.ShapeDtypeStruct((blocks, 1, width), jnp.float32))
     return call(
-        functools.partial(adjacency_kernel, CUTS[k], CUTS[k + 1], fresh, final),
+        functools.partial(adjacency_kernel, CUTS[k], CUTS[k + 1], fresh, final, len(idle)),
         outs,
         (edges, *state),
         plan,
         aliases=None if fresh else {2: 0, 3: 1},
         name="adjacency",
-    )
-
-
-def near_kernel(own_ref, less_ref, more_ref, over_ref, kept_ref, deg_ref, near_ref, one_ref, two_ref):
-    rows = own_ref.shape[0]
-    for k, ref in enumerate((own_ref, less_ref, more_ref, over_ref)):
-        near_ref[k * rows : (k + 1) * rows] = ref[...]
-    one_ref[...] = more_ref[...]
-    two_ref[...] = over_ref[...]
-
-
-def join_near(pieces, deg):
-    rows, cols, width = pieces[0].shape
-    return call(
-        near_kernel,
-        [jax.ShapeDtypeStruct(deg.shape, deg.dtype)]
-        + [jax.ShapeDtypeStruct((n, cols, width), jnp.bfloat16) for n in (4 * rows, rows, rows)],
-        (*pieces, deg),
-        aliases={4: 0},
-        name="join",
-    )
-
-
-def mid_kernel(more_ref, less_ref, two_ref, kept_ref, sum_ref, mid_ref, *outs):
-    rows = more_ref.shape[0]
+        idle=idle,
+    )
+
+
+def copy_all(copies):
+    for copy in copies:
+        copy.start()
+    for copy in copies:
+        copy.wait()
+
+
+def join_kernel(kept_ref, *refs):
+    near, mid, (deg_ref, near_ref, mid_ref, *outs), sems = refs[:4], refs[4:7], refs[7:-1], refs[-1]
+    rows = mid[0].shape[0]
     third = rows // 3
-    for k, ref in enumerate((more_ref, less_ref, two_ref)):
-        mid_ref[k * rows : (k + 1) * rows] = ref[...]
-    outs[0][...] = two_ref[:third]
-    outs[1][...] = less_ref[third : 2 * third]
-    outs[2][...] = more_ref[2 * third :]
-
-
-def join_mid(pieces, kept):
-    rows, cols, width = pieces[0].shape
-    sizes = (3 * rows,) + (rows // 3,) * 3
-    return call(
-        mid_kernel,
+    copy_all([
+        pltpu.make_async_copy(ref, out.at[pl.ds(k * rows, rows)], sems.at[at + k])
+        for at, out, pieces in ((0, mid_ref, mid), (3, near_ref, near))
+        for k, ref in enumerate(pieces)
+    ])
+    outs[0][...] = mid_ref[2 * rows : 2 * rows + third]
+    outs[1][...] = mid_ref[rows + third : rows + 2 * third]
+    outs[2][...] = mid_ref[2 * third : rows]
+
+
+def join(near, mid, kept):
+    rows, cols, width = mid[0].shape
+    sizes = (4 * rows, 3 * rows) + (rows // 3,) * 3
+    return call(
+        join_kernel,
         [jax.ShapeDtypeStruct(kept.shape, kept.dtype)]
         + [jax.ShapeDtypeStruct((n, cols, width), jnp.bfloat16) for n in sizes],
-        (*pieces, kept),
-        aliases={3: 0},
+        (kept,),
+        scratch=[pltpu.SemaphoreType.DMA((7,))],
+        aliases={0: 0},
+        idle=(*near, *mid),
         name="join",
     )
 
@@ -195,13 +188,16 @@
     return item & 127, (item >> 7) & 31, (item >> 12) & 31, (item >> 17) & 15, item >> 21
 
 
-def mean_kernel(low, high, fresh, final, turns, idle, plan_ref, ready, adj_ref, here_ref, swap_ref, *refs):
+def mean_kernel(low, high, fresh, final, turns, idle, plan_ref, ready, adj_ref, *refs):
+    if fresh:
+        weight_ref, here_ref, swap_ref, refs = *refs[:3], refs[3 + idle :]
+    else:
+        here_ref, swap_ref, refs = *refs[:2], refs[2:]
     if not fresh:
         refs = refs[1:]
     if final:
-        inv_ref, x_ref, cot_ref, refs = *refs[:3], refs[3:]
+        inv_ref, refs = refs[0], refs[1:]
     if turns:
-        weight_ref, refs = refs[0], refs[1 + idle :]
         for k in range(2):
             refs[1][k] = weight_ref[k]
             refs[1][2 + k] = weight_ref[k].T
@@ -209,16 +205,23 @@
     blocks = sum_ref.shape[0] - 1
     slots = adj_ref.shape[0]
     if fresh:
+        copies = [
+            pltpu.make_async_copy(a, b, refs[-1].at[k])
+            for k, (a, b) in enumerate(zip((here_ref, swap_ref), refs[-3:-1]))
+        ]
+        for copy in copies:
+            copy.start()
+        here_ref, swap_ref = refs[-3:-1]
         sum_ref[...] = jnp.zeros_like(sum_ref)
     if final:
         out_ref = refs[1]
         parts, rows, cols, width = out_ref.shape
-        rows = rows // 3
-        out_ref[:, rows : 2 * rows] = x_ref[...].reshape(parts, rows, cols, width)
-        out_ref[:, 2 * rows :] = cot_ref[...].reshape(parts, rows, cols, width)
     ready()
 
     for core, feats_ref in enumerate((here_ref, swap_ref)):
+        if fresh:
+            copies[core].wait()
+
         def add(spot, valid):
             slot, row, col, key, _ = fields(plan_ref[spot])
             place = (key - low - 8 * core) * blocks + col
@@ -228,7 +231,7 @@
         ranged(plan_ref[slots + low + 8 * core], plan_ref[slots + high + 8 * core], add)
     if final:
         mean = (sum_ref[:blocks] * inv_ref[...]).astype(jnp.bfloat16)
-        out_ref[:, :rows] = mean.reshape(parts, rows, cols, width)
+        out_ref[...] = mean.reshape(parts, rows, cols, width)
 
 
 def mean_stage(plan, adj, low, high, pieces, before=None, last=(), parts=0, weights=None, idle=()):
@@ -237,31 +240,34 @@
     fresh, final = before is None, len(last) > 0
     outs = [jax.ShapeDtypeStruct((blocks + 1, cols, width), jnp.float32)]
     if final:
-        outs.append(jax.ShapeDtypeStruct((parts, 3 * blocks // parts, cols, width), jnp.bfloat16))
+        outs.append(jax.ShapeDtypeStruct((parts, blocks // parts, cols, width), jnp.bfloat16))
     turns = weights is not None
     if turns:
         outs.append(jax.ShapeDtypeStruct((4,) + weights.shape[1:], jnp.bfloat16))
+    scratch = []
+    if fresh:
+        scratch = [pltpu.VMEM(pieces[0].shape, jnp.bfloat16)] * 2 + [pltpu.SemaphoreType.DMA((2,))]
     return call(
         functools.partial(mean_kernel, low, high, fresh, final, turns, len(idle)),
         outs,
-        [adj, *pieces] + ([] if fresh else [before]) + list(last) + ([weights] if turns else []),
+        [adj, weights] if fresh else [adj, *pieces, before, *last],
         plan,
+        scratch,
         aliases=None if fresh else {4: 0},
-        idle=idle,
+        idle=(*pieces, *idle) if fresh else (),
         name="neighbor_mean",
     )
 
 
-def dense_kernel(plan_ref, ready, in_ref, turn_ref, inv_ref, adj_ref, out_ref, kept_ref, gs_ref, gn_ref):
+def dense_kernel(plan_ref, ready, in_ref, xc_ref, turn_ref, inv_ref, adj_ref, out_ref, kept_ref, gs_ref, gn_ref):
     parts, rows, cols, width = in_ref.shape
-    rows = rows // 3
     feats = parts * cols
     ready()
     here = plan_ref[HERE]
     for i in range(rows):
         mean = in_ref[:, i].reshape(feats, width)
-        x = in_ref[:, rows + i].reshape(feats, width)
-        cot = in_ref[:, 2 * rows + i].reshape(feats, width).astype(jnp.float32)
+        x = xc_ref[:, i].reshape(feats, width)
+        cot = xc_ref[:, rows + i].reshape(feats, width).astype(jnp.float32)
         preact = jnp.dot(turn_ref[2], x, preferred_element_type=jnp.float32)
         preact = preact + jnp.dot(turn_ref[3], mean, preferred_element_type=jnp.float32)
         gate = jax.nn.sigmoid(preact)
@@ -280,20 +286,20 @@
         out_ref[:, 3 * rows + k] = ref[...].astype(jnp.bfloat16).reshape(parts, cols, width)
 
 
-def dense(plan, packed, turn, inverse, adj):
+def dense(plan, packed, x_cot, turn, inverse, adj):
     parts, rows, cols, width = packed.shape
     feats = parts * cols
     grad = pltpu.VMEM((feats, feats), jnp.float32)
     return call(
         dense_kernel,
         [
-            jax.ShapeDtypeStruct((parts, rows + 2, cols, width), jnp.bfloat16),
+            jax.ShapeDtypeStruct((parts, 3 * rows + 2, cols, width), jnp.bfloat16),
             jax.ShapeDtypeStruct(adj.shape, adj.dtype),
         ],
-        (packed, turn, inverse, adj),
+        (packed, x_cot, turn, inverse, adj),
         plan,
         [grad, grad],
-        aliases={4: 1},
+        aliases={5: 1},
         name="dense",
     )
 
@@ -462,14 +468,17 @@
     build = functools.partial(
         adjacency, plan=plan, edges=edge_src + (edge_dst << 8), blocks=blocks, width=width
     )
-    adj, deg = build(0)
-    deg, near, z_more, y_own = join_near((own, z_less, z_more, y_own), deg)
+    x_cot = over_col(
+        jnp.concatenate([a.reshape(n_col, per, cols, width) for a in (features, cotangent)], axis=1),
+        2 * per,
+    )
     y_more, y_less, z_two = send(z_more, "over"), send(y_own, "up"), send(z_more, "down")
+    adj, deg = build(0, idle=(x_cot,))
+    deg, near, mid, *cut = join((own, z_less, z_more, y_own), (y_more, y_less, z_two), deg)
     near_swap = send(near, "core")
-    adj, deg, inverse = build(1, state=(adj, deg))
-    inverse, mid, *cut = join_mid((y_more, y_less, z_two), inverse)
     cut = [send(cut[0], "over"), send(cut[1], "up"), send(cut[2], "down")]
     mid_swap = send(mid, "core")
+    adj, deg, inverse = build(1, state=(adj, deg))
     sums, turn = mean_stage(
         plan, adj, 0, 4, [near, near_swap], weights=jnp.stack([w_self, w_neigh]), idle=(mid,)
     )
@@ -477,10 +486,10 @@
     y_swap = send(y_two, "core")
     (sums,) = mean_stage(plan, adj, 4, 7, [mid, mid_swap], sums)
     _, packed = mean_stage(
-        plan, adj, 7, 8, [y_two, y_swap], sums, (inverse, own, cotangent), n_col
-    )
-
-    out, adj = dense(plan, over_col(packed, 3 * per), turn, inverse, adj)
+        plan, adj, 7, 8, [y_two, y_swap], sums, (inverse,), n_col
+    )
+
+    out, adj = dense(plan, over_col(packed, per), x_cot, turn, inverse, adj)
     moved = over_col(out, 3 * per + 2)
     hidden = moved[:, per : 2 * per].reshape(blocks, cols, width)
     grads = moved.reshape(n_col * (3 * per + 2), cols, width)

time: 140 us -> 137 us (0.979)
  blocking collectives: 49.7 us -> 39.1 us
  starting transfers between devices: 24.3 us -> 31.2 us
  Pallas kernels: 33.8 us -> 31.9 us
    all_to_all x2, blocking collectives: 49.7 us -> 39.1 us  [over_col(): moved = lax.all_to_all(a.reshape(n_col, rows * cols, width), 'col', 0, 0)]
    all_to_all x0 -> x1, waiting for transfers between devices: none -> 8.09 us  [over_col(): moved = lax.all_to_all(a.reshape(n_col, rows * cols, width), 'col', 0, 0)]
    ppermute x24, waiting for transfers between devices: 26.8 us -> 19.7 us  [send(): return lax.ppermute(value, 'blk', ROUTES[route])]
    all_to_all x0 -> x1, starting transfers between devices: none -> 6.77 us  [over_col(): moved = lax.all_to_all(a.reshape(n_col, rows * cols, width), 'col', 0, 0)]
    concatenate x0 -> x1, other arithmetic: none -> 2.11 us  [local(): jnp.concatenate([a.reshape(n_col, per, cols, width) for a in (features, c...]
    pallas_call x17 -> x16, Pallas kernels: 33.8 us -> 31.9 us  [call(): pl.pallas_call(kernel, in_specs=[IDLE] * len(lead) + [WHOLE] * len(operan...]
  transfers between devices with their start and end apart: 24 -> 25, of which waited for: 14 -> 8; matrix products, arithmetic and copies ran while one was open for 3% -> 3% of each run, Pallas kernels for 17% -> 16%
where the time goes in v4:
time: 137 us; the launch traced here: 136 us
  blocking collectives  39.1 us (29%)
  Pallas kernels  31.9 us (23%)
  starting transfers between devices  31.2 us (23%)
  waiting for transfers between devices  27.8 us (20%)
  other arithmetic  3.76 us (3%)
  between operations  1.65 us (1%)
    all_to_all x2, blocking collectives, over_col(): moved = lax.all_to_all(a.reshape(n_col, rows * cols, width), 'col', 0, 0)  39.1 us
    pallas_call x16, Pallas kernels, call(): pl.pallas_call(kernel, in_specs=[IDLE] * len(lead) + [WHOLE] * len(operan...  31.9 us
    ppermute x24, starting transfers between devices, send(): return lax.ppermute(value, 'blk', ROUTES[route])  24.4 us
    ppermute x24, waiting for transfers between devices, send(): return lax.ppermute(value, 'blk', ROUTES[route])  19.7 us
    all_to_all x1, waiting for transfers between devices, over_col(): moved = lax.all_to_all(a.reshape(n_col, rows * cols, width), 'col', 0, 0)  8.09 us
    all_to_all x1, starting transfers between devices, over_col(): moved = lax.all_to_all(a.reshape(n_col, rows * cols, width), 'col', 0, 0)  6.77 us
  transfers between devices with their start and end apart: 25, of which 8 were waited for; matrix products, arithmetic and copies ran while one was open for 3% of the time, Pallas kernels for 16%

profile of v4, /device:TPU:0, one launch (start us, length us, event | category | flops | bytes accessed | tf_op | source)
XLA Modules:
  0.0 136.2 jit_solution(6040218354777895942)
XLA Ops:
  0.6 4.2 %collective-permute-start.1 = (bf16[24,32,256]{2,1,0:T(8,128)(2,1)}, bf16[24,32,256]{2,1,0:T(8,128)(2,1)S(1)}, u32[]{:S(2)}, u32[]{:S(2)}) collective-permute-start(bf16[24,32,256]{2,1,0:T(8,128)(2,1)} %refs_0_.1), channel_id=1, source_target_pairs={{0,48},{8,56},{16,0},{24,8},{32,16},{40,24},{48,32},{56,40},{64,11... | collective-permute-start | bytes 1179656 | tf_op jit(solution)/shard_map/ppermute | solution.py:37
  4.8 1.6 %collective-permute-start.2 = (bf16[24,32,256]{2,1,0:T(8,128)(2,1)}, bf16[24,32,256]{2,1,0:T(8,128)(2,1)S(1)}, u32[]{:S(2)}, u32[]{:S(2)}) collective-permute-start(bf16[24,32,256]{2,1,0:T(8,128)(2,1)} %refs_0_.1), channel_id=1, source_target_pairs={{0,64},{8,72},{16,80},{24,88},{32,96},{40,104},{48,112},{56,120},{... | collective-permute-start | bytes 1179656 | tf_op jit(solution)/shard_map/ppermute | solution.py:37
  6.4 2.1 %pad_maximum_fusion = bf16[8,6,32,256]{3,2,1,0:T(8,128)(2,1)} fusion(bf16[8,3,32,256]{3,2,1,0:T(8,128)(2,1)} %bitcast.37, bf16[8,3,32,256]{3,2,1,0:T(8,128)(2,1)} %bitcast.32), kind=kLoop, calls=%fused_computation | loop fusion | flops 393216 | bytes 1572864 | tf_op jit(solution)/shard_map/concatenate | solution.py:472
  8.5 6.8 %all-to-all-start = ((bf16[8,192,256]{2,1,0:T(8,128)(2,1)}), bf16[8,192,256]{2,1,0:T(8,128)(2,1)S(1)}, u32[]{:S(2)}, u32[]{:S(2)}) async-start(bf16[8,192,256]{2,1,0:T(8,128)(2,1)} %bitcast.5), calls=%async_computation | async-start | bytes 1572864 | tf_op jit(solution)/shard_map/all_to_all | solution.py:462
  16.0 0.2 convert_reduce_fusion
  16.2 0.1 select_reduce_fusion
  16.3 0.0 collective-permute-done.1.refs_2_
  16.3 0.2 collective-permute-start.3
  16.6 3.2 %collective-permute-start.5 = (bf16[24,32,256]{2,1,0:T(8,128)(2,1)S(1)}, bf16[24,32,256]{2,1,0:T(8,128)(2,1)S(1)}, u32[]{:S(2)}, u32[]{:S(2)}) collective-permute-start(bf16[24,32,256]{2,1,0:T(8,128)(2,1)S(1)} %collective-permute-done.1.refs_2_), channel_id=1, source_target_pairs={{0,48},{8,56},{16,0},{24,8},{32,16},{40,24},{48,32},{56,40},{64,11... | collective-permute-start | bytes 1179656 | tf_op jit(solution)/shard_map/ppermute | solution.py:37
  19.8 0.0 collective-permute-done.2.refs_3_
  19.8 0.0 collective-permute-start.4
  19.8 0.1 convert_reduce_fusion.1
  19.9 0.1 pad_add_fusion.plan_ref
  20.0 1.1 shift-left_add_fusion.refs_0_
  21.1 8.1 %all-to-all-done = bf16[8,192,256]{2,1,0:T(8,128)(2,1)S(1)} async-done(((bf16[8,192,256]{2,1,0:T(8,128)(2,1)}), bf16[8,192,256]{2,1,0:T(8,128)(2,1)S(1)}, u32[]{:S(2)}, u32[]{:S(2)}) %all-to-all-start) | async-done | bytes 786464 | tf_op jit(solution)/shard_map/all_to_all | solution.py:462
  29.2 7.0 %adjacency.2 = (bf16[128,256,256]{2,1,0:T(8,128)(2,1)S(1)}, f32[25,8,256]{2,1,0:T(8,128)S(1)}) custom-call(s32[296]{0:T(512)S(1)} %pad_add_fusion.plan_ref, s32[128,640]{1,0:T(8,128)S(1)} %shift-left_add_fusion.refs_0_, bf16[8,6,32,256]{3,2,1,0:T(8,128)(2,1)S(1)} %bitcast.30), custom_call_target="tpu_custom_call" | custom-call | tf_op jit(solution)/shard_map/adjacency/pallas_call | solution.py:55
  36.2 0.0 copy-start.1
  36.2 0.0 copy-start.2
  36.2 0.0 collective-permute-done.refs_1_
  36.2 0.0 collective-permute-done.3.refs_4_
  36.2 1.3 join.2
  37.5 0.1 collective-permute-start.9
  37.6 0.5 collective-permute-start.11
  38.1 0.1 collective-permute-start.6
  38.2 0.0 collective-permute-start.7
  38.2 3.2 %collective-permute-start.8 = (bf16[8,32,256]{2,1,0:T(8,128)(2,1)S(1)}, bf16[8,32,256]{2,1,0:T(8,128)(2,1)S(1)}, u32[]{:S(2)}, u32[]{:S(2)}) collective-permute-start(bf16[8,32,256]{2,1,0:T(8,128)(2,1)S(1)} %get-tuple-element.56), channel_id=1, source_target_pairs={{0,48},{8,56},{16,0},{24,8},{32,16},{40,24},{48,32},{56,40},{64,11... | collective-permute-start | bytes 393224 | tf_op jit(solution)/shard_map/ppermute | solution.py:37
  41.5 3.6 %adjacency.3 = (bf16[128,256,256]{2,1,0:T(8,128)(2,1)S(1)}, f32[25,8,256]{2,1,0:T(8,128)S(1)}, f32[24,1,256]{2,1,0:T(1,128)S(1)}) custom-call(s32[296]{0:T(512)S(1)} %pad_add_fusion.plan_ref, s32[128,640]{1,0:T(8,128)S(1)} %shift-left_add_fusion.refs_0_, ...), custom_call_target="tpu_custom_call", output_to_operand_aliasing={{0}: (2, {}), {1}: (3, {})} | custom-call | tf_op jit(solution)/shard_map/adjacency/pallas_call | solution.py:55
  45.1 0.0 collective-permute-done.9.refs_3_
  45.1 2.6 %neighbor_mean.3 = (f32[25,32,256]{2,1,0:T(8,128)S(1)}, bf16[4,256,256]{2,1,0:T(8,128)(2,1)S(1)}) custom-call(s32[296]{0:T(512)S(1)} %pad_add_fusion.plan_ref, bf16[128,256,256]{2,1,0:T(8,128)(2,1)S(1)} %get-tuple-element.53.refs_0_.refs_4_, bf16[2,256,256]{2,1,0:T(8,128)(2,1)S(1)} %pad_maximum_fusion.1.refs_1_, ...), custom_call_target="tpu_custom_call" | custom-call | tf_op jit(solution)/shard_map/neighbor_mean/pallas_call | solution.py:55
  47.7 0.0 collective-permute-done.6.one_ref
  47.8 0.1 collective-permute-start.10
  47.9 2.2 %neighbor_mean.4.refs_3_ = f32[25,32,256]{2,1,0:T(8,128)S(1)} custom-call(s32[296]{0:T(512)S(1)} %pad_add_fusion.plan_ref, bf16[128,256,256]{2,1,0:T(8,128)(2,1)S(1)} %get-tuple-element.53.refs_0_.refs_4_, bf16[72,32,256]{2,1,0:T(8,128)(2,1)S(1)} %get-tuple-element.58.refs_4_.refs_1_, ...), custom_call_target="tpu_custom_call", output_to_operand_aliasing={{}: (4, {})} | custom-call | tf_op jit(solution)/shard_map/neighbor_mean/pallas_call | solution.py:55
  50.0 1.4 %neighbor_mean.5 = (f32[25,32,256]{2,1,0:T(8,128)S(1)}, bf16[8,3,32,256]{3,2,1,0:T(8,128)(2,1)S(1)}) custom-call(s32[296]{0:T(512)S(1)} %pad_add_fusion.plan_ref, bf16[128,256,256]{2,1,0:T(8,128)(2,1)S(1)} %get-tuple-element.53.refs_0_.refs_4_, bf16[24,32,256]{2,1,0:T(8,128)(2,1)S(1)} %get-tuple-element.60.refs_1_, ...), custom_call_target="tpu_custom_call", output_to_operand_aliasing={{0}: (4, {})} | custom-call | tf_op jit(solution)/shard_map/neighbor_mean/pallas_call | solution.py:55
  51.5 15.4 %all_to_all.15 = bf16[8,96,256]{2,1,0:T(8,128)(2,1)S(1)} all-to-all(bf16[8,96,256]{2,1,0:T(8,128)(2,1)S(1)} %bitcast.35), channel_id=1, replica_groups=mesh['blk'=16,'col'=8] {'col'}, dimensions={0} | all-to-all | bytes 786432 | tf_op jit(solution)/shard_map/all_to_all | solution.py:462
  66.9 2.0 %dense.1 = (bf16[8,11,32,256]{3,2,1,0:T(8,128)(2,1)S(1)}, bf16[128,256,256]{2,1,0:T(8,128)(2,1)S(1)}) custom-call(s32[296]{0:T(512)S(1)} %pad_add_fusion.plan_ref, bf16[8,3,32,256]{3,2,1,0:T(8,128)(2,1)S(1)} %bitcast.33, bf16[8,6,32,256]{3,2,1,0:T(8,128)(2,1)S(1)} %bitcast.31, ...), custom_call_target="tpu_custom_call", output_to_operand_aliasing={{1}: (5, {})} | custom-call | tf_op jit(solution)/shard_map/dense/pallas_call | solution.py:55
  68.9 23.7 %all_to_all.16 = bf16[8,352,256]{2,1,0:T(8,128)(2,1)S(1)} all-to-all(bf16[8,352,256]{2,1,0:T(8,128)(2,1)S(1)} %bitcast.34), channel_id=1, replica_groups=mesh['blk'=16,'col'=8] {'col'}, dimensions={0} | all-to-all | bytes 2883584 | tf_op jit(solution)/shard_map/all_to_all | solution.py:462
  92.6 1.3 sums_far_swap.1
  93.9 0.1 collective-permute-start.12
  94.0 1.9 %sums_mid_swap.1 = (bf16[128,256,256]{2,1,0:T(8,128)(2,1)S(1)}, bf16[72,32,256]{2,1,0:T(8,128)(2,1)S(1)}) custom-call(s32[296]{0:T(512)S(1)} %pad_add_fusion.plan_ref, bf16[88,32,256]{2,1,0:T(8,128)(2,1)S(1)} %bitcast.23, bf16[128,256,256]{2,1,0:T(8,128)(2,1)S(1)} %get-tuple-element.67.refs_1_), custom_call_target="tpu_custom_call", output_to_operand_aliasing={{0}: (2, {})} | custom-call | tf_op jit(solution)/shard_map/sums_mid_swap/pallas_call | solution.py:55
  95.9 1.2 sums_far_own.1
  97.1 0.6 collective-permute-start.13
  97.7 0.6 collective-permute-start.14
  98.2 1.4 %collective-permute-start.15 = (bf16[8,32,256]{2,1,0:T(8,128)(2,1)S(1)}, bf16[8,32,256]{2,1,0:T(8,128)(2,1)S(1)}, u32[]{:S(2)}, u32[]{:S(2)}) collective-permute-start(bf16[8,32,256]{2,1,0:T(8,128)(2,1)S(1)} %get-tuple-element.76), channel_id=1, source_target_pairs={{0,48},{8,56},{16,0},{24,8},{32,16},{40,24},{48,32},{56,40},{64,11... | collective-permute-start | bytes 393224 | tf_op jit(solution)/shard_map/ppermute | solution.py:37
  99.7 0.6 collective-permute-start.16
  100.3 2.5 %sums_near_swap.1 = (bf16[128,256,256]{2,1,0:T(8,128)(2,1)S(1)}, bf16[96,32,256]{2,1,0:T(8,128)(2,1)S(1)}) custom-call(s32[296]{0:T(512)S(1)} %pad_add_fusion.plan_ref, bf16[88,32,256]{2,1,0:T(8,128)(2,1)S(1)} %bitcast.25, bf16[128,256,256]{2,1,0:T(8,128)(2,1)S(1)} %get-tuple-element.72.refs_1_), custom_call_target="tpu_custom_call", output_to_operand_aliasing={{0}: (2, {})} | custom-call | tf_op jit(solution)/shard_map/sums_near_swap/pallas_call | solution.py:55
  102.8 1.0 collective-permute-done.15.refs_4_
  103.8 2.6 %collective-permute-done.16.refs_5_ = bf16[8,32,256]{2,1,0:T(8,128)(2,1)S(1)} collective-permute-done((bf16[8,32,256]{2,1,0:T(8,128)(2,1)S(1)}, bf16[8,32,256]{2,1,0:T(8,128)(2,1)S(1)}, u32[]{:S(2)}, u32[]{:S(2)}) %collective-permute-start.16) | collective-permute-done | bytes 131104 | tf_op jit(solution)/shard_map/ppermute | solution.py:37
  106.4 1.9 %sums_mid_own.1 = (bf16[128,256,256]{2,1,0:T(8,128)(2,1)S(1)}, bf16[24,32,256]{2,1,0:T(8,128)(2,1)S(1)}, bf16[26,32,256]{2,1,0:T(8,128)(2,1)S(1)}, bf16[26,32,25...) custom-call(s32[296]{0:T(512)S(1)} %pad_add_fusion.plan_ref, ...), custom_call_target="tpu_custom_call", output_to_operand_aliasing={{0}: (2, {}), {5}: (9, {})} | custom-call | tf_op jit(solution)/shard_map/sums_mid_own/pallas_call | solution.py:55
  108.3 0.1 collective-permute-start.17
  108.3 1.3 collective-permute-start.19
  109.6 0.8 collective-permute-start.20
  110.4 1.5 %collective-permute-start.18 = (bf16[24,32,256]{2,1,0:T(8,128)(2,1)S(1)}, bf16[24,32,256]{2,1,0:T(8,128)(2,1)S(1)}, u32[]{:S(2)}, u32[]{:S(2)}) collective-permute-start(bf16[24,32,256]{2,1,0:T(8,128)(2,1)S(1)} %get-tuple-element.84), channel_id=1, source_target_pairs={{0,64},{8,72},{16,80},{24,88},{32,96},{40,104},{48,112},{56,120},{... | collective-permute-start | bytes 1179656 | tf_op jit(solution)/shard_map/ppermute | solution.py:37
  112.0 2.0 %sums_near_own.1 = (bf16[128,256,256]{2,1,0:T(8,128)(2,1)S(1)}, f32[24,32,256]{2,1,0:T(8,128)S(1)}, bf16[24,32,256]{2,1,0:T(8,128)(2,1)S(1)}, f32[24,32,256]{2,1,0:T(8,128)S(1)}, f32[24,32,256]{2,1,0:T(8,128)S(1)}) custom-call(s32[296]{0:T(512)S(1)} %pad_add_fusion.plan_ref, bf16[88,32,256]{2,1,0:T(8,128)(2,1)S(1)} %bitcast.27, ...), custom_call_target="tpu_custom_call", output_to_operand_aliasing={{0}: (2, {})} | custom-call | tf_op jit(solution)/shard_map/sums_near_own/pallas_call | solution.py:55
  113.9 7.4 %collective-permute-done.18.y_more_ref = bf16[24,32,256]{2,1,0:T(8,128)(2,1)S(1)} collective-permute-done((bf16[24,32,256]{2,1,0:T(8,128)(2,1)S(1)}, bf16[24,32,256]{2,1,0:T(8,128)(2,1)S(1)}, u32[]{:S(2)}, u32[]{:S(2)}) %collective-permute-start.18) | collective-permute-done | bytes 393248 | tf_op jit(solution)/shard_map/ppermute | solution.py:37
  121.3 1.3 collective-permute-done.20.z_two_ref.up_ref
  122.7 0.2 relay.1
  122.9 0.1 collective-permute-start.22
  123.0 1.1 collective-permute-start.23
  124.2 3.0 %collective-permute-start.21 = (bf16[24,32,256]{2,1,0:T(8,128)(2,1)S(1)}, bf16[24,32,256]{2,1,0:T(8,128)(2,1)S(1)}, u32[]{:S(2)}, u32[]{:S(2)}) collective-permute-start(bf16[24,32,256]{2,1,0:T(8,128)(2,1)S(1)} %get-tuple-element.89), channel_id=1, source_target_pairs={{0,48},{8,56},{16,0},{24,8},{32,16},{40,24},{48,32},{56,40},{64,11... | collective-permute-start | bytes 1179656 | tf_op jit(solution)/shard_map/ppermute | solution.py:37
  127.2 0.8 slice.4
  127.9 5.5 %collective-permute-done.23.over_ref = bf16[24,32,256]{2,1,0:T(8,128)(2,1)S(1)} collective-permute-done((bf16[24,32,256]{2,1,0:T(8,128)(2,1)S(1)}, bf16[24,32,256]{2,1,0:T(8,128)(2,1)S(1)}, u32[]{:S(2)}, u32[]{:S(2)}) %collective-permute-start.23) | collective-permute-done | bytes 393248 | tf_op jit(solution)/shard_map/ppermute | solution.py:37
  133.5 1.0 collective-permute-done.21.less_ref
  134.5 0.8 collective-permute-done.22.more_ref
  135.3 0.9 finish.1
  (28 shorter events, 0.1 us)
Async XLA Ops:
  0.6 15.7 %collective-permute-start.1 = (bf16[24,32,256]{2,1,0:T(8,128)(2,1)}, bf16[24,32,256]{2,1,0:T(8,128)(2,1)S(1)}, u32[]{:S(2)}, u32[]{:S(2)}) collective-permute-start(bf16[24,32,256]{2,1,0:T(8,128)(2,1)} %refs_0_.1), channel_id=1, source_target_pairs={{0,48},{8,56},{16,0},{24,8},{32,16},{40,24},{48,32},{56,40},{64,11... | collective-permute-start | bytes 1179656 | tf_op jit(solution)/shard_map/ppermute | solution.py:37
  4.8 15.0 %collective-permute-start.2 = (bf16[24,32,256]{2,1,0:T(8,128)(2,1)}, bf16[24,32,256]{2,1,0:T(8,128)(2,1)S(1)}, u32[]{:S(2)}, u32[]{:S(2)}) collective-permute-start(bf16[24,32,256]{2,1,0:T(8,128)(2,1)} %refs_0_.1), channel_id=1, source_target_pairs={{0,64},{8,72},{16,80},{24,88},{32,96},{40,104},{48,112},{56,120},{... | collective-permute-start | bytes 1179656 | tf_op jit(solution)/shard_map/ppermute | solution.py:37
  6.4 29.8 %collective-permute-start = (bf16[24,32,256]{2,1,0:T(8,128)(2,1)}, bf16[24,32,256]{2,1,0:T(8,128)(2,1)S(1)}, u32[]{:S(2)}, u32[]{:S(2)}) collective-permute-start(bf16[24,32,256]{2,1,0:T(8,128)(2,1)} %refs_0_.1), channel_id=1, source_target_pairs={{0,16},{8,24},{16,32},{24,40},{32,48},{40,56},{48,0},{56,8},{64,80... | collective-permute-start | bytes 1179656 | tf_op jit(solution)/shard_map/ppermute | solution.py:37
  6.4 9.5 %copy-start.3 = (s32[128,1]{0,1:T(1,128)S(1)}, s32[128,1]{0,1:T(1,128)}, u32[]{:S(2)}) copy-start(s32[128,1]{0,1:T(1,128)} %param.15) | copy-start | bytes 1540
  6.4 9.6 %copy-start.4 = (s32[128]{0:T(128)S(1)}, s32[128]{0:T(128)}, u32[]{:S(2)}) copy-start(s32[128]{0:T(128)} %param.14) | copy-start | bytes 1540
  6.4 9.6 %copy-start.5 = (s32[128]{0:T(128)S(1)}, s32[128]{0:T(128)}, u32[]{:S(2)}) copy-start(s32[128]{0:T(128)} %param.16) | copy-start | bytes 1540
  8.5 27.7 %copy-start = (bf16[24,32,256]{2,1,0:T(8,128)(2,1)S(1)}, bf16[24,32,256]{2,1,0:T(8,128)(2,1)}, u32[]{:S(2)}) copy-start(bf16[24,32,256]{2,1,0:T(8,128)(2,1)} %refs_0_.1) | copy-start | bytes 1179652
  8.5 20.7 %all-to-all-start = ((bf16[8,192,256]{2,1,0:T(8,128)(2,1)}), bf16[8,192,256]{2,1,0:T(8,128)(2,1)S(1)}, u32[]{:S(2)}, u32[]{:S(2)}) async-start(bf16[8,192,256]{2,1,0:T(8,128)(2,1)} %bitcast.5), calls=%async_computation | async-start | bytes 1572864 | tf_op jit(solution)/shard_map/all_to_all | solution.py:462
  16.3 19.9 %collective-permute-start.3 = (bf16[24,32,256]{2,1,0:T(8,128)(2,1)S(1)}, bf16[24,32,256]{2,1,0:T(8,128)(2,1)S(1)}, u32[]{:S(2)}, u32[]{:S(2)}) collective-permute-start(bf16[24,32,256]{2,1,0:T(8,128)(2,1)S(1)} %collective-permute-done.1.refs_2_), channel_id=1, source_target_pairs={{0,64},{8,72},{16,80},{24,88},{32,96},{40,104},{48,112},{56,120},{... | collective-permute-start | bytes 1179656 | tf_op jit(solution)/shard_map/ppermute | solution.py:37
  16.6 19.6 %collective-permute-start.5 = (bf16[24,32,256]{2,1,0:T(8,128)(2,1)S(1)}, bf16[24,32,256]{2,1,0:T(8,128)(2,1)S(1)}, u32[]{:S(2)}, u32[]{:S(2)}) collective-permute-start(bf16[24,32,256]{2,1,0:T(8,128)(2,1)S(1)} %collective-permute-done.1.refs_2_), channel_id=1, source_target_pairs={{0,48},{8,56},{16,0},{24,8},{32,16},{40,24},{48,32},{56,40},{64,11... | collective-permute-start | bytes 1179656 | tf_op jit(solution)/shard_map/ppermute | solution.py:37
  19.8 16.4 %collective-permute-start.4 = (bf16[24,32,256]{2,1,0:T(8,128)(2,1)S(1)}, bf16[24,32,256]{2,1,0:T(8,128)(2,1)}, u32[]{:S(2)}, u32[]{:S(2)}) collective-permute-start(bf16[24,32,256]{2,1,0:T(8,128)(2,1)S(1)} %collective-permute-done.2.refs_3_), channel_id=1, source_target_pairs={{0,16},{8,24},{16,32},{24,40},{32,48},{40,56},{48,0},{56,8},{64,80... | collective-permute-start | bytes 1179656 | tf_op jit(solution)/shard_map/ppermute | solution.py:37
  36.2 5.3 %copy-start.1 = (bf16[256,256]{1,0:T(8,128)(2,1)S(1)}, bf16[256,256]{1,0:T(8,128)(2,1)}, u32[]{:S(2)}) copy-start(bf16[256,256]{1,0:T(8,128)(2,1)} %param.13) | copy-start | bytes 393220
  36.2 5.3 %copy-start.2 = (bf16[256,256]{1,0:T(8,128)(2,1)S(1)}, bf16[256,256]{1,0:T(8,128)(2,1)}, u32[]{:S(2)}) copy-start(bf16[256,256]{1,0:T(8,128)(2,1)} %param.12) | copy-start | bytes 393220
  37.5 7.6 %collective-permute-start.9 = (bf16[96,32,256]{2,1,0:T(8,128)(2,1)S(1)}, bf16[96,32,256]{2,1,0:T(8,128)(2,1)S(1)}, u32[]{:S(2)}, u32[]{:S(2)}) collective-permute-start(bf16[96,32,256]{2,1,0:T(8,128)(2,1)S(1)} %get-tuple-element.57.refs_2_), channel_id=1, source_target_pairs={{0,8},{8,0},{16,24},{24,16},{32,40},{40,32},{48,56},{56,48},{64,72... | collective-permute-start | bytes 4718600 | tf_op jit(solution)/shard_map/ppermute | solution.py:37
  37.6 10.2 %collective-permute-start.11 = (bf16[72,32,256]{2,1,0:T(8,128)(2,1)S(1)}, bf16[72,32,256]{2,1,0:T(8,128)(2,1)S(1)}, u32[]{:S(2)}, u32[]{:S(2)}) collective-permute-start(bf16[72,32,256]{2,1,0:T(8,128)(2,1)S(1)} %get-tuple-element.58.refs_4_.refs_1_), channel_id=1, source_target_pairs={{0,8},{8,0},{16,24},{24,16},{32,40},{40,32},{48,56},{56,48},{64,72... | collective-permute-start | bytes 3538952 | tf_op jit(solution)/shard_map/ppermute | solution.py:37
  38.1 9.6 %collective-permute-start.6 = (bf16[8,32,256]{2,1,0:T(8,128)(2,1)S(1)}, bf16[8,32,256]{2,1,0:T(8,128)(2,1)S(1)}, u32[]{:S(2)}, u32[]{:S(2)}) collective-permute-start(bf16[8,32,256]{2,1,0:T(8,128)(2,1)S(1)} %get-tuple-element.54), channel_id=1, source_target_pairs={{0,64},{8,72},{16,80},{24,88},{32,96},{40,104},{48,112},{56,120},{... | collective-permute-start | bytes 393224 | tf_op jit(solution)/shard_map/ppermute | solution.py:37
  38.2 9.5 %collective-permute-start.7 = (bf16[8,32,256]{2,1,0:T(8,128)(2,1)S(1)}, bf16[8,32,256]{2,1,0:T(8,128)(2,1)S(1)}, u32[]{:S(2)}, u32[]{:S(2)}) collective-permute-start(bf16[8,32,256]{2,1,0:T(8,128)(2,1)S(1)} %get-tuple-element.55), channel_id=1, source_target_pairs={{0,16},{8,24},{16,32},{24,40},{32,48},{40,56},{48,0},{56,8},{64,80... | collective-permute-start | bytes 393224 | tf_op jit(solution)/shard_map/ppermute | solution.py:37
  38.2 9.5 %collective-permute-start.8 = (bf16[8,32,256]{2,1,0:T(8,128)(2,1)S(1)}, bf16[8,32,256]{2,1,0:T(8,128)(2,1)S(1)}, u32[]{:S(2)}, u32[]{:S(2)}) collective-permute-start(bf16[8,32,256]{2,1,0:T(8,128)(2,1)S(1)} %get-tuple-element.56), channel_id=1, source_target_pairs={{0,48},{8,56},{16,0},{24,8},{32,16},{40,24},{48,32},{56,40},{64,11... | collective-permute-start | bytes 393224 | tf_op jit(solution)/shard_map/ppermute | solution.py:37
  47.8 2.3 %collective-permute-start.10 = (bf16[24,32,256]{2,1,0:T(8,128)(2,1)S(1)}, bf16[24,32,256]{2,1,0:T(8,128)(2,1)S(1)}, u32[]{:S(2)}, u32[]{:S(2)}) collective-permute-start(bf16[24,32,256]{2,1,0:T(8,128)(2,1)S(1)} %get-tuple-element.60.refs_1_), channel_id=1, source_target_pairs={{0,8},{8,0},{16,24},{24,16},{32,40},{40,32},{48,56},{56,48},{64,72... | collective-permute-start | bytes 1179656 | tf_op jit(solution)/shard_map/ppermute | solution.py:37
  93.9 2.0 %collective-permute-start.12 = (bf16[26,32,256]{2,1,0:T(8,128)(2,1)S(1)}, bf16[26,32,256]{2,1,0:T(8,128)(2,1)S(1)}, u32[]{:S(2)}, u32[]{:S(2)}) collective-permute-start(bf16[26,32,256]{2,1,0:T(8,128)(2,1)S(1)} %get-tuple-element.69), channel_id=1, source_target_pairs={{0,8},{8,0},{16,24},{24,16},{32,40},{40,32},{48,56},{56,48},{64,72... | collective-permute-start | bytes 1277960 | tf_op jit(solution)/shard_map/ppermute | solution.py:37
  97.1 9.3 %collective-permute-start.13 = (bf16[72,32,256]{2,1,0:T(8,128)(2,1)S(1)}, bf16[72,32,256]{2,1,0:T(8,128)(2,1)S(1)}, u32[]{:S(2)}, u32[]{:S(2)}) collective-permute-start(bf16[72,32,256]{2,1,0:T(8,128)(2,1)S(1)} %get-tuple-element.74), channel_id=1, source_target_pairs={{0,8},{8,0},{16,24},{24,16},{32,40},{40,32},{48,56},{56,48},{64,72... | collective-permute-start | bytes 3538952 | tf_op jit(solution)/shard_map/ppermute | solution.py:37
  97.7 8.7 %collective-permute-start.14 = (bf16[10,32,256]{2,1,0:T(8,128)(2,1)S(1)}, bf16[10,32,256]{2,1,0:T(8,128)(2,1)S(1)}, u32[]{:S(2)}, u32[]{:S(2)}) collective-permute-start(bf16[10,32,256]{2,1,0:T(8,128)(2,1)S(1)} %get-tuple-element.75), channel_id=1, source_target_pairs={{0,64},{8,72},{16,80},{24,88},{32,96},{40,104},{48,112},{56,120},{... | collective-permute-start | bytes 491528 | tf_op jit(solution)/shard_map/ppermute | solution.py:37
  98.2 5.6 %collective-permute-start.15 = (bf16[8,32,256]{2,1,0:T(8,128)(2,1)S(1)}, bf16[8,32,256]{2,1,0:T(8,128)(2,1)S(1)}, u32[]{:S(2)}, u32[]{:S(2)}) collective-permute-start(bf16[8,32,256]{2,1,0:T(8,128)(2,1)S(1)} %get-tuple-element.76), channel_id=1, source_target_pairs={{0,48},{8,56},{16,0},{24,8},{32,16},{40,24},{48,32},{56,40},{64,11... | collective-permute-start | bytes 393224 | tf_op jit(solution)/shard_map/ppermute | solution.py:37
  99.7 6.7 %collective-permute-start.16 = (bf16[8,32,256]{2,1,0:T(8,128)(2,1)S(1)}, bf16[8,32,256]{2,1,0:T(8,128)(2,1)S(1)}, u32[]{:S(2)}, u32[]{:S(2)}) collective-permute-start(bf16[8,32,256]{2,1,0:T(8,128)(2,1)S(1)} %get-tuple-element.77), channel_id=1, source_target_pairs={{0,16},{8,24},{16,32},{24,40},{32,48},{40,56},{48,0},{56,8},{64,80... | collective-permute-start | bytes 393224 | tf_op jit(solution)/shard_map/ppermute | solution.py:37
  108.3 3.7 %collective-permute-start.17 = (bf16[96,32,256]{2,1,0:T(8,128)(2,1)S(1)}, bf16[96,32,256]{2,1,0:T(8,128)(2,1)S(1)}, u32[]{:S(2)}, u32[]{:S(2)}) collective-permute-start(bf16[96,32,256]{2,1,0:T(8,128)(2,1)S(1)} %get-tuple-element.81), channel_id=1, source_target_pairs={{0,8},{8,0},{16,24},{24,16},{32,40},{40,32},{48,56},{56,48},{64,72... | collective-permute-start | bytes 4718600 | tf_op jit(solution)/shard_map/ppermute | solution.py:37
  108.3 13.0 %collective-permute-start.19 = (bf16[26,32,256]{2,1,0:T(8,128)(2,1)S(1)}, bf16[26,32,256]{2,1,0:T(8,128)(2,1)S(1)}, u32[]{:S(2)}, u32[]{:S(2)}) collective-permute-start(bf16[26,32,256]{2,1,0:T(8,128)(2,1)S(1)} %get-tuple-element.85), channel_id=1, source_target_pairs={{0,48},{8,56},{16,0},{24,8},{32,16},{40,24},{48,32},{56,40},{64,11... | collective-permute-start | bytes 1277960 | tf_op jit(solution)/shard_map/ppermute | solution.py:37
  109.6 13.1 %collective-permute-start.20 = (bf16[26,32,256]{2,1,0:T(8,128)(2,1)S(1)}, bf16[26,32,256]{2,1,0:T(8,128)(2,1)S(1)}, u32[]{:S(2)}, u32[]{:S(2)}) collective-permute-start(bf16[26,32,256]{2,1,0:T(8,128)(2,1)S(1)} %get-tuple-element.86), channel_id=1, source_target_pairs={{0,16},{8,24},{16,32},{24,40},{32,48},{40,56},{48,0},{56,8},{64,80... | collective-permute-start | bytes 1277960 | tf_op jit(solution)/shard_map/ppermute | solution.py:37
  110.4 10.9 %collective-permute-start.18 = (bf16[24,32,256]{2,1,0:T(8,128)(2,1)S(1)}, bf16[24,32,256]{2,1,0:T(8,128)(2,1)S(1)}, u32[]{:S(2)}, u32[]{:S(2)}) collective-permute-start(bf16[24,32,256]{2,1,0:T(8,128)(2,1)S(1)} %get-tuple-element.84), channel_id=1, source_target_pairs={{0,64},{8,72},{16,80},{24,88},{32,96},{40,104},{48,112},{56,120},{... | collective-permute-start | bytes 1179656 | tf_op jit(solution)/shard_map/ppermute | solution.py:37
  122.9 12.3 %collective-permute-start.22 = (bf16[26,32,256]{2,1,0:T(8,128)(2,1)S(1)}, bf16[26,32,256]{2,1,0:T(8,128)(2,1)S(1)}, u32[]{:S(2)}, u32[]{:S(2)}) collective-permute-start(bf16[26,32,256]{2,1,0:T(8,128)(2,1)S(1)} %get-tuple-element.90), channel_id=1, source_target_pairs={{0,16},{8,24},{16,32},{24,40},{32,48},{40,56},{48,0},{56,8},{64,80... | collective-permute-start | bytes 1277960 | tf_op jit(solution)/shard_map/ppermute | solution.py:37
  123.0 10.4 %collective-permute-start.23 = (bf16[24,32,256]{2,1,0:T(8,128)(2,1)S(1)}, bf16[24,32,256]{2,1,0:T(8,128)(2,1)S(1)}, u32[]{:S(2)}, u32[]{:S(2)}) collective-permute-start(bf16[24,32,256]{2,1,0:T(8,128)(2,1)S(1)} %get-tuple-element.91), channel_id=1, source_target_pairs={{0,64},{8,72},{16,80},{24,88},{32,96},{40,104},{48,112},{56,120},{... | collective-permute-start | bytes 1179656 | tf_op jit(solution)/shard_map/ppermute | solution.py:37
  124.2 10.3 %collective-permute-start.21 = (bf16[24,32,256]{2,1,0:T(8,128)(2,1)S(1)}, bf16[24,32,256]{2,1,0:T(8,128)(2,1)S(1)}, u32[]{:S(2)}, u32[]{:S(2)}) collective-permute-start(bf16[24,32,256]{2,1,0:T(8,128)(2,1)S(1)} %get-tuple-element.89), channel_id=1, source_target_pairs={{0,48},{8,56},{16,0},{24,8},{32,16},{40,24},{48,32},{56,40},{64,11... | collective-permute-start | bytes 1179656 | tf_op jit(solution)/shard_map/ppermute | solution.py:37

commit v5 on v4

--- a/solution.py
+++ b/solution.py
@@ -128,20 +128,19 @@
 def join_kernel(kept_ref, *refs):
     near, mid, (deg_ref, near_ref, mid_ref, *outs), sems = refs[:4], refs[4:7], refs[7:-1], refs[-1]
     rows = mid[0].shape[0]
-    third = rows // 3
+    half = rows // 2
     copy_all([
         pltpu.make_async_copy(ref, out.at[pl.ds(k * rows, rows)], sems.at[at + k])
         for at, out, pieces in ((0, mid_ref, mid), (3, near_ref, near))
         for k, ref in enumerate(pieces)
     ])
-    outs[0][...] = mid_ref[2 * rows : 2 * rows + third]
-    outs[1][...] = mid_ref[rows + third : rows + 2 * third]
-    outs[2][...] = mid_ref[2 * third : rows]
+    outs[0][...] = mid_ref[rows : rows + half]
+    outs[1][...] = mid_ref[half:rows]
 
 
 def join(near, mid, kept):
     rows, cols, width = mid[0].shape
-    sizes = (4 * rows, 3 * rows) + (rows // 3,) * 3
+    sizes = (4 * rows, 3 * rows) + (rows // 2,) * 2
     return call(
         join_kernel,
         [jax.ShapeDtypeStruct(kept.shape, kept.dtype)]
@@ -154,10 +153,10 @@
     )
 
 
-def far_kernel(one_ref, two_ref, three_ref, kept_ref, sum_ref, far_ref):
+def far_kernel(one_ref, two_ref, kept_ref, sum_ref, far_ref):
     rows = one_ref.shape[0]
-    for k, ref in enumerate((one_ref, two_ref, three_ref)):
-        far_ref[k * rows : (k + 1) * rows] = ref[...]
+    far_ref[:rows] = one_ref[...]
+    far_ref[rows:] = two_ref[...]
 
 
 def join_far(pieces, sums):
@@ -166,22 +165,22 @@
         far_kernel,
         [
             jax.ShapeDtypeStruct(sums.shape, sums.dtype),
-            jax.ShapeDtypeStruct((3 * rows, cols, width), jnp.bfloat16),
+            jax.ShapeDtypeStruct((2 * rows, cols, width), jnp.bfloat16),
         ],
         (*pieces, sums),
-        aliases={3: 0},
+        aliases={2: 0},
         name="join",
     )
 
 
-def ranged(start, stop, body):
+def ranged(start, stop, body, unroll=UNROLL):
     def step(i, carry):
-        for j in range(UNROLL):
-            spot = start + i * UNROLL + j
+        for j in range(unroll):
+            spot = start + i * unroll + j
             body(jnp.minimum(spot, stop - 1), spot < stop)
         return carry
 
-    lax.fori_loop(0, (stop - start + UNROLL - 1) // UNROLL, step, 0)
+    lax.fori_loop(0, (stop - start + unroll - 1) // unroll, step, 0)
 
 
 def fields(item):
@@ -228,7 +227,10 @@
             flow = jnp.dot(feats_ref[place], adj_ref[slot], preferred_element_type=jnp.float32)
             sum_ref[jnp.where(valid, row, blocks)] += flow
 
-        ranged(plan_ref[slots + low + 8 * core], plan_ref[slots + high + 8 * core], add)
+        ranged(
+            plan_ref[slots + low + 8 * core], plan_ref[slots + high + 8 * core], add,
+            16 if high - low == 4 else UNROLL,
+        )
     if final:
         mean = (sum_ref[:blocks] * inv_ref[...]).astype(jnp.bfloat16)
         out_ref[...] = mean.reshape(parts, rows, cols, width)
@@ -476,7 +478,7 @@
     adj, deg = build(0, idle=(x_cot,))
     deg, near, mid, *cut = join((own, z_less, z_more, y_own), (y_more, y_less, z_two), deg)
     near_swap = send(near, "core")
-    cut = [send(cut[0], "over"), send(cut[1], "up"), send(cut[2], "down")]
+    cut = [send(cut[0], "up"), send(cut[1], "down")]
     mid_swap = send(mid, "core")
     adj, deg, inverse = build(1, state=(adj, deg))
     sums, turn = mean_stage(

time: 137 us -> 135 us (0.985)
  waiting for transfers between devices: 27.8 us -> 24.9 us
  starting transfers between devices: 31.2 us -> 33.6 us
    ppermute x24 -> x23, waiting for transfers between devices: 19.7 us -> 16.9 us  [send(): return lax.ppermute(value, 'blk', ROUTES[route])]
    ppermute x24 -> x23, starting transfers between devices: 24.4 us -> 26.8 us  [send(): return lax.ppermute(value, 'blk', ROUTES[route])]
  transfers between devices with their start and end apart: 25 -> 24, of which waited for: 8 -> 8; matrix products, arithmetic and copies ran while one was open for 3% -> 3% of each run, Pallas kernels for 16% -> 16%
where the time goes in v5:
time: 135 us
  blocking collectives  38.7 us (29%)
  starting transfers between devices  33.6 us (25%)
  Pallas kernels  31.5 us (23%)
  waiting for transfers between devices  24.9 us (18%)
  other arithmetic  3.76 us (3%)
  between operations  1.62 us (1%)
    all_to_all x2, blocking collectives, over_col(): moved = lax.all_to_all(a.reshape(n_col, rows * cols, width), 'col', 0, 0)  38.7 us
    pallas_call x16, Pallas kernels, call(): pl.pallas_call(kernel, in_specs=[IDLE] * len(lead) + [WHOLE] * len(operan...  31.5 us
    ppermute x23, starting transfers between devices, send(): return lax.ppermute(value, 'blk', ROUTES[route])  26.8 us
    ppermute x23, waiting for transfers between devices, send(): return lax.ppermute(value, 'blk', ROUTES[route])  16.9 us
    all_to_all x1, waiting for transfers between devices, over_col(): moved = lax.all_to_all(a.reshape(n_col, rows * cols, width), 'col', 0, 0)  8.09 us
    all_to_all x1, starting transfers between devices, over_col(): moved = lax.all_to_all(a.reshape(n_col, rows * cols, width), 'col', 0, 0)  6.77 us
  transfers between devices with their start and end apart: 24, of which 8 were waited for; matrix products, arithmetic and copies ran while one was open for 3% of the time, Pallas kernels for 16%

profile of v5, /device:TPU:0, one launch (start us, length us, event | category | flops | bytes accessed | tf_op | source)
XLA Modules:
  0.0 134.9 jit_solution(5311679069449956708)
XLA Ops:
  0.6 4.2 %collective-permute-start.1 = (bf16[24,32,256]{2,1,0:T(8,128)(2,1)}, bf16[24,32,256]{2,1,0:T(8,128)(2,1)S(1)}, u32[]{:S(2)}, u32[]{:S(2)}) collective-permute-start(bf16[24,32,256]{2,1,0:T(8,128)(2,1)} %refs_0_.1), channel_id=1, source_target_pairs={{0,48},{8,56},{16,0},{24,8},{32,16},{40,24},{48,32},{56,40},{64,11... | collective-permute-start | bytes 1179656 | tf_op jit(solution)/shard_map/ppermute | solution.py:37
  4.8 1.6 %collective-permute-start.2 = (bf16[24,32,256]{2,1,0:T(8,128)(2,1)}, bf16[24,32,256]{2,1,0:T(8,128)(2,1)S(1)}, u32[]{:S(2)}, u32[]{:S(2)}) collective-permute-start(bf16[24,32,256]{2,1,0:T(8,128)(2,1)} %refs_0_.1), channel_id=1, source_target_pairs={{0,64},{8,72},{16,80},{24,88},{32,96},{40,104},{48,112},{56,120},{... | collective-permute-start | bytes 1179656 | tf_op jit(solution)/shard_map/ppermute | solution.py:37
  6.4 0.0 collective-permute-start
  6.4 2.1 %pad_maximum_fusion = bf16[8,6,32,256]{3,2,1,0:T(8,128)(2,1)} fusion(bf16[8,3,32,256]{3,2,1,0:T(8,128)(2,1)} %bitcast.37, bf16[8,3,32,256]{3,2,1,0:T(8,128)(2,1)} %bitcast.32), kind=kLoop, calls=%fused_computation | loop fusion | flops 393216 | bytes 1572864 | tf_op jit(solution)/shard_map/concatenate | solution.py:474
  8.5 6.8 %all-to-all-start = ((bf16[8,192,256]{2,1,0:T(8,128)(2,1)}), bf16[8,192,256]{2,1,0:T(8,128)(2,1)S(1)}, u32[]{:S(2)}, u32[]{:S(2)}) async-start(bf16[8,192,256]{2,1,0:T(8,128)(2,1)} %bitcast.5), calls=%async_computation | async-start | bytes 1572864 | tf_op jit(solution)/shard_map/all_to_all | solution.py:464
  16.0 0.2 convert_reduce_fusion
  16.2 0.1 select_reduce_fusion
  16.3 0.2 collective-permute-start.3
  16.6 3.2 %collective-permute-start.5 = (bf16[24,32,256]{2,1,0:T(8,128)(2,1)S(1)}, bf16[24,32,256]{2,1,0:T(8,128)(2,1)S(1)}, u32[]{:S(2)}, u32[]{:S(2)}) collective-permute-start(bf16[24,32,256]{2,1,0:T(8,128)(2,1)S(1)} %collective-permute-done.1.refs_2_), channel_id=1, source_target_pairs={{0,48},{8,56},{16,0},{24,8},{32,16},{40,24},{48,32},{56,40},{64,11... | collective-permute-start | bytes 1179656 | tf_op jit(solution)/shard_map/ppermute | solution.py:37
  19.8 0.0 collective-permute-done.2.refs_3_
  19.8 0.0 collective-permute-start.4
  19.8 0.1 convert_reduce_fusion.1
  19.9 0.1 pad_add_fusion.plan_ref
  20.0 1.1 shift-left_add_fusion.refs_0_
  21.1 8.1 %all-to-all-done = bf16[8,192,256]{2,1,0:T(8,128)(2,1)S(1)} async-done(((bf16[8,192,256]{2,1,0:T(8,128)(2,1)}), bf16[8,192,256]{2,1,0:T(8,128)(2,1)S(1)}, u32[]{:S(2)}, u32[]{:S(2)}) %all-to-all-start) | async-done | bytes 786464 | tf_op jit(solution)/shard_map/all_to_all | solution.py:464
  29.2 6.9 %adjacency.2 = (bf16[128,256,256]{2,1,0:T(8,128)(2,1)S(1)}, f32[25,8,256]{2,1,0:T(8,128)S(1)}) custom-call(s32[296]{0:T(512)S(1)} %pad_add_fusion.plan_ref, s32[128,640]{1,0:T(8,128)S(1)} %shift-left_add_fusion.refs_0_, bf16[8,6,32,256]{3,2,1,0:T(8,128)(2,1)S(1)} %bitcast.30), custom_call_target="tpu_custom_call" | custom-call | tf_op jit(solution)/shard_map/adjacency/pallas_call | solution.py:55
  36.1 0.0 copy-start.1
  36.2 0.0 copy-start.2
  36.2 0.0 collective-permute-done.refs_1_
  36.2 0.0 collective-permute-done.3.refs_4_
  36.2 0.0 collective-permute-done.4.refs_5_
  36.2 1.3 join.2
  37.5 0.1 collective-permute-start.8
  37.6 0.5 collective-permute-start.10
  38.1 0.0 collective-permute-start.6
  38.1 3.2 %collective-permute-start.7 = (bf16[12,32,256]{2,1,0:T(8,128)(2,1)S(1)}, bf16[12,32,256]{2,1,0:T(8,128)(2,1)S(1)}, u32[]{:S(2)}, u32[]{:S(2)}) collective-permute-start(bf16[12,32,256]{2,1,0:T(8,128)(2,1)S(1)} %get-tuple-element.54), channel_id=1, source_target_pairs={{0,48},{8,56},{16,0},{24,8},{32,16},{40,24},{48,32},{56,40},{64,11... | collective-permute-start | bytes 589832 | tf_op jit(solution)/shard_map/ppermute | solution.py:37
  41.4 3.6 %adjacency.3 = (bf16[128,256,256]{2,1,0:T(8,128)(2,1)S(1)}, f32[25,8,256]{2,1,0:T(8,128)S(1)}, f32[24,1,256]{2,1,0:T(1,128)S(1)}) custom-call(s32[296]{0:T(512)S(1)} %pad_add_fusion.plan_ref, s32[128,640]{1,0:T(8,128)S(1)} %shift-left_add_fusion.refs_0_, ...), custom_call_target="tpu_custom_call", output_to_operand_aliasing={{0}: (2, {}), {1}: (3, {})} | custom-call | tf_op jit(solution)/shard_map/adjacency/pallas_call | solution.py:55
  45.0 0.0 collective-permute-done.8.refs_3_
  45.0 2.5 %neighbor_mean.3 = (f32[25,32,256]{2,1,0:T(8,128)S(1)}, bf16[4,256,256]{2,1,0:T(8,128)(2,1)S(1)}) custom-call(s32[296]{0:T(512)S(1)} %pad_add_fusion.plan_ref, bf16[128,256,256]{2,1,0:T(8,128)(2,1)S(1)} %get-tuple-element.52.refs_0_.refs_4_, bf16[2,256,256]{2,1,0:T(8,128)(2,1)S(1)} %pad_maximum_fusion.1.refs_1_, ...), custom_call_target="tpu_custom_call" | custom-call | tf_op jit(solution)/shard_map/neighbor_mean/pallas_call | solution.py:55
  47.6 0.1 collective-permute-start.9
  47.7 1.8 %neighbor_mean.4.refs_3_ = f32[25,32,256]{2,1,0:T(8,128)S(1)} custom-call(s32[296]{0:T(512)S(1)} %pad_add_fusion.plan_ref, bf16[128,256,256]{2,1,0:T(8,128)(2,1)S(1)} %get-tuple-element.52.refs_0_.refs_4_, bf16[72,32,256]{2,1,0:T(8,128)(2,1)S(1)} %get-tuple-element.56.refs_4_.refs_1_, ...), custom_call_target="tpu_custom_call", output_to_operand_aliasing={{}: (4, {})} | custom-call | tf_op jit(solution)/shard_map/neighbor_mean/pallas_call | solution.py:55
  49.5 1.4 %neighbor_mean.5 = (f32[25,32,256]{2,1,0:T(8,128)S(1)}, bf16[8,3,32,256]{3,2,1,0:T(8,128)(2,1)S(1)}) custom-call(s32[296]{0:T(512)S(1)} %pad_add_fusion.plan_ref, bf16[128,256,256]{2,1,0:T(8,128)(2,1)S(1)} %get-tuple-element.52.refs_0_.refs_4_, bf16[24,32,256]{2,1,0:T(8,128)(2,1)S(1)} %get-tuple-element.58.refs_1_, ...), custom_call_target="tpu_custom_call", output_to_operand_aliasing={{0}: (4, {})} | custom-call | tf_op jit(solution)/shard_map/neighbor_mean/pallas_call | solution.py:55
  50.9 14.7 %all_to_all.15 = bf16[8,96,256]{2,1,0:T(8,128)(2,1)S(1)} all-to-all(bf16[8,96,256]{2,1,0:T(8,128)(2,1)S(1)} %bitcast.35), channel_id=1, replica_groups=mesh['blk'=16,'col'=8] {'col'}, dimensions={0} | all-to-all | bytes 786432 | tf_op jit(solution)/shard_map/all_to_all | solution.py:464
  65.6 2.0 %dense.1 = (bf16[8,11,32,256]{3,2,1,0:T(8,128)(2,1)S(1)}, bf16[128,256,256]{2,1,0:T(8,128)(2,1)S(1)}) custom-call(s32[296]{0:T(512)S(1)} %pad_add_fusion.plan_ref, bf16[8,3,32,256]{3,2,1,0:T(8,128)(2,1)S(1)} %bitcast.33, bf16[8,6,32,256]{3,2,1,0:T(8,128)(2,1)S(1)} %bitcast.31, ...), custom_call_target="tpu_custom_call", output_to_operand_aliasing={{1}: (5, {})} | custom-call | tf_op jit(solution)/shard_map/dense/pallas_call | solution.py:55
  67.6 24.0 %all_to_all.16 = bf16[8,352,256]{2,1,0:T(8,128)(2,1)S(1)} all-to-all(bf16[8,352,256]{2,1,0:T(8,128)(2,1)S(1)} %bitcast.34), channel_id=1, replica_groups=mesh['blk'=16,'col'=8] {'col'}, dimensions={0} | all-to-all | bytes 2883584 | tf_op jit(solution)/shard_map/all_to_all | solution.py:464
  91.6 1.3 sums_far_swap.1
  92.9 0.1 collective-permute-start.11
  93.0 1.3 sums_mid_swap.1
  94.3 0.5 collective-permute-done.11.refs_2_.refs_4_
  94.7 1.2 sums_far_own.1
  96.0 0.7 collective-permute-start.12
  96.7 2.0 %collective-permute-start.13 = (bf16[10,32,256]{2,1,0:T(8,128)(2,1)S(1)}, bf16[10,32,256]{2,1,0:T(8,128)(2,1)S(1)}, u32[]{:S(2)}, u32[]{:S(2)}) collective-permute-start(bf16[10,32,256]{2,1,0:T(8,128)(2,1)S(1)} %get-tuple-element.73), channel_id=1, source_target_pairs={{0,64},{8,72},{16,80},{24,88},{32,96},{40,104},{48,112},{56,120},{... | collective-permute-start | bytes 491528 | tf_op jit(solution)/shard_map/ppermute | solution.py:37
  98.7 0.9 collective-permute-start.14
  99.6 1.1 collective-permute-start.15
  100.7 2.5 %sums_near_swap.1 = (bf16[128,256,256]{2,1,0:T(8,128)(2,1)S(1)}, bf16[96,32,256]{2,1,0:T(8,128)(2,1)S(1)}) custom-call(s32[296]{0:T(512)S(1)} %pad_add_fusion.plan_ref, bf16[88,32,256]{2,1,0:T(8,128)(2,1)S(1)} %bitcast.25, bf16[128,256,256]{2,1,0:T(8,128)(2,1)S(1)} %get-tuple-element.70.refs_1_), custom_call_target="tpu_custom_call", output_to_operand_aliasing={{0}: (2, {})} | custom-call | tf_op jit(solution)/shard_map/sums_near_swap/pallas_call | solution.py:55
  103.3 0.7 collective-permute-done.14.refs_4_
  103.9 2.0 %collective-permute-done.15.refs_5_ = bf16[8,32,256]{2,1,0:T(8,128)(2,1)S(1)} collective-permute-done((bf16[8,32,256]{2,1,0:T(8,128)(2,1)S(1)}, bf16[8,32,256]{2,1,0:T(8,128)(2,1)S(1)}, u32[]{:S(2)}, u32[]{:S(2)}) %collective-permute-start.15) | collective-permute-done | bytes 131104 | tf_op jit(solution)/shard_map/ppermute | solution.py:37
  105.9 1.9 %sums_mid_own.1 = (bf16[128,256,256]{2,1,0:T(8,128)(2,1)S(1)}, bf16[24,32,256]{2,1,0:T(8,128)(2,1)S(1)}, bf16[26,32,256]{2,1,0:T(8,128)(2,1)S(1)}, bf16[26,32,25...) custom-call(s32[296]{0:T(512)S(1)} %pad_add_fusion.plan_ref, ...), custom_call_target="tpu_custom_call", output_to_operand_aliasing={{0}: (2, {}), {5}: (9, {})} | custom-call | tf_op jit(solution)/shard_map/sums_mid_own/pallas_call | solution.py:55
  107.8 0.1 collective-permute-start.16
  107.9 0.4 collective-permute-start.18
  108.3 1.7 %collective-permute-start.19 = (bf16[26,32,256]{2,1,0:T(8,128)(2,1)S(1)}, bf16[26,32,256]{2,1,0:T(8,128)(2,1)S(1)}, u32[]{:S(2)}, u32[]{:S(2)}) collective-permute-start(bf16[26,32,256]{2,1,0:T(8,128)(2,1)S(1)} %get-tuple-element.84), channel_id=1, source_target_pairs={{0,16},{8,24},{16,32},{24,40},{32,48},{40,56},{48,0},{56,8},{64,80... | collective-permute-start | bytes 1277960 | tf_op jit(solution)/shard_map/ppermute | solution.py:37
  110.0 1.7 %collective-permute-start.17 = (bf16[24,32,256]{2,1,0:T(8,128)(2,1)S(1)}, bf16[24,32,256]{2,1,0:T(8,128)(2,1)S(1)}, u32[]{:S(2)}, u32[]{:S(2)}) collective-permute-start(bf16[24,32,256]{2,1,0:T(8,128)(2,1)S(1)} %get-tuple-element.82), channel_id=1, source_target_pairs={{0,64},{8,72},{16,80},{24,88},{32,96},{40,104},{48,112},{56,120},{... | collective-permute-start | bytes 1179656 | tf_op jit(solution)/shard_map/ppermute | solution.py:37
  111.7 2.6 %sums_near_own.1 = (bf16[128,256,256]{2,1,0:T(8,128)(2,1)S(1)}, f32[24,32,256]{2,1,0:T(8,128)S(1)}, bf16[24,32,256]{2,1,0:T(8,128)(2,1)S(1)}, f32[24,32,256]{2,1,0:T(8,128)S(1)}, f32[24,32,256]{2,1,0:T(8,128)S(1)}) custom-call(s32[296]{0:T(512)S(1)} %pad_add_fusion.plan_ref, bf16[88,32,256]{2,1,0:T(8,128)(2,1)S(1)} %bitcast.27, ...), custom_call_target="tpu_custom_call", output_to_operand_aliasing={{0}: (2, {})} | custom-call | tf_op jit(solution)/shard_map/sums_near_own/pallas_call | solution.py:55
  114.3 6.6 %collective-permute-done.17.y_more_ref = bf16[24,32,256]{2,1,0:T(8,128)(2,1)S(1)} collective-permute-done((bf16[24,32,256]{2,1,0:T(8,128)(2,1)S(1)}, bf16[24,32,256]{2,1,0:T(8,128)(2,1)S(1)}, u32[]{:S(2)}, u32[]{:S(2)}) %collective-permute-start.17) | collective-permute-done | bytes 393248 | tf_op jit(solution)/shard_map/ppermute | solution.py:37
  120.9 0.5 collective-permute-done.19.z_two_ref.up_ref
  121.4 0.3 relay.1
  121.7 0.6 collective-permute-start.21
  122.3 1.7 %collective-permute-start.22 = (bf16[24,32,256]{2,1,0:T(8,128)(2,1)S(1)}, bf16[24,32,256]{2,1,0:T(8,128)(2,1)S(1)}, u32[]{:S(2)}, u32[]{:S(2)}) collective-permute-start(bf16[24,32,256]{2,1,0:T(8,128)(2,1)S(1)} %get-tuple-element.89), channel_id=1, source_target_pairs={{0,64},{8,72},{16,80},{24,88},{32,96},{40,104},{48,112},{56,120},{... | collective-permute-start | bytes 1179656 | tf_op jit(solution)/shard_map/ppermute | solution.py:37
  124.0 2.7 %collective-permute-start.20 = (bf16[24,32,256]{2,1,0:T(8,128)(2,1)S(1)}, bf16[24,32,256]{2,1,0:T(8,128)(2,1)S(1)}, u32[]{:S(2)}, u32[]{:S(2)}) collective-permute-start(bf16[24,32,256]{2,1,0:T(8,128)(2,1)S(1)} %get-tuple-element.87), channel_id=1, source_target_pairs={{0,48},{8,56},{16,0},{24,8},{32,16},{40,24},{48,32},{56,40},{64,11... | collective-permute-start | bytes 1179656 | tf_op jit(solution)/shard_map/ppermute | solution.py:37
  126.7 0.8 slice.4
  127.4 4.9 %collective-permute-done.22.over_ref = bf16[24,32,256]{2,1,0:T(8,128)(2,1)S(1)} collective-permute-done((bf16[24,32,256]{2,1,0:T(8,128)(2,1)S(1)}, bf16[24,32,256]{2,1,0:T(8,128)(2,1)S(1)}, u32[]{:S(2)}, u32[]{:S(2)}) %collective-permute-start.22) | collective-permute-done | bytes 393248 | tf_op jit(solution)/shard_map/ppermute | solution.py:37
  132.3 1.6 %collective-permute-done.20.less_ref = bf16[24,32,256]{2,1,0:T(8,128)(2,1)S(1)} collective-permute-done((bf16[24,32,256]{2,1,0:T(8,128)(2,1)S(1)}, bf16[24,32,256]{2,1,0:T(8,128)(2,1)S(1)}, u32[]{:S(2)}, u32[]{:S(2)}) %collective-permute-start.20) | collective-permute-done | bytes 393248 | tf_op jit(solution)/shard_map/ppermute | solution.py:37
  134.0 0.0 collective-permute-done.21.more_ref
  134.0 0.9 finish.1
  (26 shorter events, 0.1 us)
Async XLA Ops:
  0.6 15.7 %collective-permute-start.1 = (bf16[24,32,256]{2,1,0:T(8,128)(2,1)}, bf16[24,32,256]{2,1,0:T(8,128)(2,1)S(1)}, u32[]{:S(2)}, u32[]{:S(2)}) collective-permute-start(bf16[24,32,256]{2,1,0:T(8,128)(2,1)} %refs_0_.1), channel_id=1, source_target_pairs={{0,48},{8,56},{16,0},{24,8},{32,16},{40,24},{48,32},{56,40},{64,11... | collective-permute-start | bytes 1179656 | tf_op jit(solution)/shard_map/ppermute | solution.py:37
  4.8 15.0 %collective-permute-start.2 = (bf16[24,32,256]{2,1,0:T(8,128)(2,1)}, bf16[24,32,256]{2,1,0:T(8,128)(2,1)S(1)}, u32[]{:S(2)}, u32[]{:S(2)}) collective-permute-start(bf16[24,32,256]{2,1,0:T(8,128)(2,1)} %refs_0_.1), channel_id=1, source_target_pairs={{0,64},{8,72},{16,80},{24,88},{32,96},{40,104},{48,112},{56,120},{... | collective-permute-start | bytes 1179656 | tf_op jit(solution)/shard_map/ppermute | solution.py:37
  6.4 29.8 %collective-permute-start = (bf16[24,32,256]{2,1,0:T(8,128)(2,1)}, bf16[24,32,256]{2,1,0:T(8,128)(2,1)S(1)}, u32[]{:S(2)}, u32[]{:S(2)}) collective-permute-start(bf16[24,32,256]{2,1,0:T(8,128)(2,1)} %refs_0_.1), channel_id=1, source_target_pairs={{0,16},{8,24},{16,32},{24,40},{32,48},{40,56},{48,0},{56,8},{64,80... | collective-permute-start | bytes 1179656 | tf_op jit(solution)/shard_map/ppermute | solution.py:37
  6.4 9.5 %copy-start.3 = (s32[128,1]{0,1:T(1,128)S(1)}, s32[128,1]{0,1:T(1,128)}, u32[]{:S(2)}) copy-start(s32[128,1]{0,1:T(1,128)} %param.15) | copy-start | bytes 1540
  6.4 9.6 %copy-start.4 = (s32[128]{0:T(128)S(1)}, s32[128]{0:T(128)}, u32[]{:S(2)}) copy-start(s32[128]{0:T(128)} %param.14) | copy-start | bytes 1540
  6.4 9.6 %copy-start.5 = (s32[128]{0:T(128)S(1)}, s32[128]{0:T(128)}, u32[]{:S(2)}) copy-start(s32[128]{0:T(128)} %param.16) | copy-start | bytes 1540
  8.5 27.7 %copy-start = (bf16[24,32,256]{2,1,0:T(8,128)(2,1)S(1)}, bf16[24,32,256]{2,1,0:T(8,128)(2,1)}, u32[]{:S(2)}) copy-start(bf16[24,32,256]{2,1,0:T(8,128)(2,1)} %refs_0_.1) | copy-start | bytes 1179652
  8.5 20.7 %all-to-all-start = ((bf16[8,192,256]{2,1,0:T(8,128)(2,1)}), bf16[8,192,256]{2,1,0:T(8,128)(2,1)S(1)}, u32[]{:S(2)}, u32[]{:S(2)}) async-start(bf16[8,192,256]{2,1,0:T(8,128)(2,1)} %bitcast.5), calls=%async_computation | async-start | bytes 1572864 | tf_op jit(solution)/shard_map/all_to_all | solution.py:464
  16.3 19.8 %collective-permute-start.3 = (bf16[24,32,256]{2,1,0:T(8,128)(2,1)S(1)}, bf16[24,32,256]{2,1,0:T(8,128)(2,1)S(1)}, u32[]{:S(2)}, u32[]{:S(2)}) collective-permute-start(bf16[24,32,256]{2,1,0:T(8,128)(2,1)S(1)} %collective-permute-done.1.refs_2_), channel_id=1, source_target_pairs={{0,64},{8,72},{16,80},{24,88},{32,96},{40,104},{48,112},{56,120},{... | collective-permute-start | bytes 1179656 | tf_op jit(solution)/shard_map/ppermute | solution.py:37
  16.6 19.6 %collective-permute-start.5 = (bf16[24,32,256]{2,1,0:T(8,128)(2,1)S(1)}, bf16[24,32,256]{2,1,0:T(8,128)(2,1)S(1)}, u32[]{:S(2)}, u32[]{:S(2)}) collective-permute-start(bf16[24,32,256]{2,1,0:T(8,128)(2,1)S(1)} %collective-permute-done.1.refs_2_), channel_id=1, source_target_pairs={{0,48},{8,56},{16,0},{24,8},{32,16},{40,24},{48,32},{56,40},{64,11... | collective-permute-start | bytes 1179656 | tf_op jit(solution)/shard_map/ppermute | solution.py:37
  19.8 16.4 %collective-permute-start.4 = (bf16[24,32,256]{2,1,0:T(8,128)(2,1)S(1)}, bf16[24,32,256]{2,1,0:T(8,128)(2,1)}, u32[]{:S(2)}, u32[]{:S(2)}) collective-permute-start(bf16[24,32,256]{2,1,0:T(8,128)(2,1)S(1)} %collective-permute-done.2.refs_3_), channel_id=1, source_target_pairs={{0,16},{8,24},{16,32},{24,40},{32,48},{40,56},{48,0},{56,8},{64,80... | collective-permute-start | bytes 1179656 | tf_op jit(solution)/shard_map/ppermute | solution.py:37
  36.1 5.2 %copy-start.1 = (bf16[256,256]{1,0:T(8,128)(2,1)S(1)}, bf16[256,256]{1,0:T(8,128)(2,1)}, u32[]{:S(2)}) copy-start(bf16[256,256]{1,0:T(8,128)(2,1)} %param.13) | copy-start | bytes 393220
  36.2 5.2 %copy-start.2 = (bf16[256,256]{1,0:T(8,128)(2,1)S(1)}, bf16[256,256]{1,0:T(8,128)(2,1)}, u32[]{:S(2)}) copy-start(bf16[256,256]{1,0:T(8,128)(2,1)} %param.12) | copy-start | bytes 393220
  37.5 7.4 %collective-permute-start.8 = (bf16[96,32,256]{2,1,0:T(8,128)(2,1)S(1)}, bf16[96,32,256]{2,1,0:T(8,128)(2,1)S(1)}, u32[]{:S(2)}, u32[]{:S(2)}) collective-permute-start(bf16[96,32,256]{2,1,0:T(8,128)(2,1)S(1)} %get-tuple-element.55.refs_2_), channel_id=1, source_target_pairs={{0,8},{8,0},{16,24},{24,16},{32,40},{40,32},{48,56},{56,48},{64,72... | collective-permute-start | bytes 4718600 | tf_op jit(solution)/shard_map/ppermute | solution.py:37
  37.6 10.1 %collective-permute-start.10 = (bf16[72,32,256]{2,1,0:T(8,128)(2,1)S(1)}, bf16[72,32,256]{2,1,0:T(8,128)(2,1)S(1)}, u32[]{:S(2)}, u32[]{:S(2)}) collective-permute-start(bf16[72,32,256]{2,1,0:T(8,128)(2,1)S(1)} %get-tuple-element.56.refs_4_.refs_1_), channel_id=1, source_target_pairs={{0,8},{8,0},{16,24},{24,16},{32,40},{40,32},{48,56},{56,48},{64,72... | collective-permute-start | bytes 3538952 | tf_op jit(solution)/shard_map/ppermute | solution.py:37
  38.1 9.4 %collective-permute-start.6 = (bf16[12,32,256]{2,1,0:T(8,128)(2,1)S(1)}, bf16[12,32,256]{2,1,0:T(8,128)(2,1)S(1)}, u32[]{:S(2)}, u32[]{:S(2)}) collective-permute-start(bf16[12,32,256]{2,1,0:T(8,128)(2,1)S(1)} %get-tuple-element.53), channel_id=1, source_target_pairs={{0,16},{8,24},{16,32},{24,40},{32,48},{40,56},{48,0},{56,8},{64,80... | collective-permute-start | bytes 589832 | tf_op jit(solution)/shard_map/ppermute | solution.py:37
  38.1 9.4 %collective-permute-start.7 = (bf16[12,32,256]{2,1,0:T(8,128)(2,1)S(1)}, bf16[12,32,256]{2,1,0:T(8,128)(2,1)S(1)}, u32[]{:S(2)}, u32[]{:S(2)}) collective-permute-start(bf16[12,32,256]{2,1,0:T(8,128)(2,1)S(1)} %get-tuple-element.54), channel_id=1, source_target_pairs={{0,48},{8,56},{16,0},{24,8},{32,16},{40,24},{48,32},{56,40},{64,11... | collective-permute-start | bytes 589832 | tf_op jit(solution)/shard_map/ppermute | solution.py:37
  47.6 1.9 %collective-permute-start.9 = (bf16[24,32,256]{2,1,0:T(8,128)(2,1)S(1)}, bf16[24,32,256]{2,1,0:T(8,128)(2,1)S(1)}, u32[]{:S(2)}, u32[]{:S(2)}) collective-permute-start(bf16[24,32,256]{2,1,0:T(8,128)(2,1)S(1)} %get-tuple-element.58.refs_1_), channel_id=1, source_target_pairs={{0,8},{8,0},{16,24},{24,16},{32,40},{40,32},{48,56},{56,48},{64,72... | collective-permute-start | bytes 1179656 | tf_op jit(solution)/shard_map/ppermute | solution.py:37
  92.9 1.8 %collective-permute-start.11 = (bf16[26,32,256]{2,1,0:T(8,128)(2,1)S(1)}, bf16[26,32,256]{2,1,0:T(8,128)(2,1)S(1)}, u32[]{:S(2)}, u32[]{:S(2)}) collective-permute-start(bf16[26,32,256]{2,1,0:T(8,128)(2,1)S(1)} %get-tuple-element.67), channel_id=1, source_target_pairs={{0,8},{8,0},{16,24},{24,16},{32,40},{40,32},{48,56},{56,48},{64,72... | collective-permute-start | bytes 1277960 | tf_op jit(solution)/shard_map/ppermute | solution.py:37
  96.0 9.9 %collective-permute-start.12 = (bf16[72,32,256]{2,1,0:T(8,128)(2,1)S(1)}, bf16[72,32,256]{2,1,0:T(8,128)(2,1)S(1)}, u32[]{:S(2)}, u32[]{:S(2)}) collective-permute-start(bf16[72,32,256]{2,1,0:T(8,128)(2,1)S(1)} %get-tuple-element.72), channel_id=1, source_target_pairs={{0,8},{8,0},{16,24},{24,16},{32,40},{40,32},{48,56},{56,48},{64,72... | collective-permute-start | bytes 3538952 | tf_op jit(solution)/shard_map/ppermute | solution.py:37
  96.7 9.2 %collective-permute-start.13 = (bf16[10,32,256]{2,1,0:T(8,128)(2,1)S(1)}, bf16[10,32,256]{2,1,0:T(8,128)(2,1)S(1)}, u32[]{:S(2)}, u32[]{:S(2)}) collective-permute-start(bf16[10,32,256]{2,1,0:T(8,128)(2,1)S(1)} %get-tuple-element.73), channel_id=1, source_target_pairs={{0,64},{8,72},{16,80},{24,88},{32,96},{40,104},{48,112},{56,120},{... | collective-permute-start | bytes 491528 | tf_op jit(solution)/shard_map/ppermute | solution.py:37
  98.7 5.2 %collective-permute-start.14 = (bf16[8,32,256]{2,1,0:T(8,128)(2,1)S(1)}, bf16[8,32,256]{2,1,0:T(8,128)(2,1)S(1)}, u32[]{:S(2)}, u32[]{:S(2)}) collective-permute-start(bf16[8,32,256]{2,1,0:T(8,128)(2,1)S(1)} %get-tuple-element.74), channel_id=1, source_target_pairs={{0,48},{8,56},{16,0},{24,8},{32,16},{40,24},{48,32},{56,40},{64,11... | collective-permute-start | bytes 393224 | tf_op jit(solution)/shard_map/ppermute | solution.py:37
  99.6 6.3 %collective-permute-start.15 = (bf16[8,32,256]{2,1,0:T(8,128)(2,1)S(1)}, bf16[8,32,256]{2,1,0:T(8,128)(2,1)S(1)}, u32[]{:S(2)}, u32[]{:S(2)}) collective-permute-start(bf16[8,32,256]{2,1,0:T(8,128)(2,1)S(1)} %get-tuple-element.75), channel_id=1, source_target_pairs={{0,16},{8,24},{16,32},{24,40},{32,48},{40,56},{48,0},{56,8},{64,80... | collective-permute-start | bytes 393224 | tf_op jit(solution)/shard_map/ppermute | solution.py:37
  107.8 3.9 %collective-permute-start.16 = (bf16[96,32,256]{2,1,0:T(8,128)(2,1)S(1)}, bf16[96,32,256]{2,1,0:T(8,128)(2,1)S(1)}, u32[]{:S(2)}, u32[]{:S(2)}) collective-permute-start(bf16[96,32,256]{2,1,0:T(8,128)(2,1)S(1)} %get-tuple-element.79), channel_id=1, source_target_pairs={{0,8},{8,0},{16,24},{24,16},{32,40},{40,32},{48,56},{56,48},{64,72... | collective-permute-start | bytes 4718600 | tf_op jit(solution)/shard_map/ppermute | solution.py:37
  107.9 13.0 %collective-permute-start.18 = (bf16[26,32,256]{2,1,0:T(8,128)(2,1)S(1)}, bf16[26,32,256]{2,1,0:T(8,128)(2,1)S(1)}, u32[]{:S(2)}, u32[]{:S(2)}) collective-permute-start(bf16[26,32,256]{2,1,0:T(8,128)(2,1)S(1)} %get-tuple-element.83), channel_id=1, source_target_pairs={{0,48},{8,56},{16,0},{24,8},{32,16},{40,24},{48,32},{56,40},{64,11... | collective-permute-start | bytes 1277960 | tf_op jit(solution)/shard_map/ppermute | solution.py:37
  108.3 13.1 %collective-permute-start.19 = (bf16[26,32,256]{2,1,0:T(8,128)(2,1)S(1)}, bf16[26,32,256]{2,1,0:T(8,128)(2,1)S(1)}, u32[]{:S(2)}, u32[]{:S(2)}) collective-permute-start(bf16[26,32,256]{2,1,0:T(8,128)(2,1)S(1)} %get-tuple-element.84), channel_id=1, source_target_pairs={{0,16},{8,24},{16,32},{24,40},{32,48},{40,56},{48,0},{56,8},{64,80... | collective-permute-start | bytes 1277960 | tf_op jit(solution)/shard_map/ppermute | solution.py:37
  110.0 10.9 %collective-permute-start.17 = (bf16[24,32,256]{2,1,0:T(8,128)(2,1)S(1)}, bf16[24,32,256]{2,1,0:T(8,128)(2,1)S(1)}, u32[]{:S(2)}, u32[]{:S(2)}) collective-permute-start(bf16[24,32,256]{2,1,0:T(8,128)(2,1)S(1)} %get-tuple-element.82), channel_id=1, source_target_pairs={{0,64},{8,72},{16,80},{24,88},{32,96},{40,104},{48,112},{56,120},{... | collective-permute-start | bytes 1179656 | tf_op jit(solution)/shard_map/ppermute | solution.py:37
  121.7 12.3 %collective-permute-start.21 = (bf16[26,32,256]{2,1,0:T(8,128)(2,1)S(1)}, bf16[26,32,256]{2,1,0:T(8,128)(2,1)S(1)}, u32[]{:S(2)}, u32[]{:S(2)}) collective-permute-start(bf16[26,32,256]{2,1,0:T(8,128)(2,1)S(1)} %get-tuple-element.88), channel_id=1, source_target_pairs={{0,16},{8,24},{16,32},{24,40},{32,48},{40,56},{48,0},{56,8},{64,80... | collective-permute-start | bytes 1277960 | tf_op jit(solution)/shard_map/ppermute | solution.py:37
  122.3 10.1 %collective-permute-start.22 = (bf16[24,32,256]{2,1,0:T(8,128)(2,1)S(1)}, bf16[24,32,256]{2,1,0:T(8,128)(2,1)S(1)}, u32[]{:S(2)}, u32[]{:S(2)}) collective-permute-start(bf16[24,32,256]{2,1,0:T(8,128)(2,1)S(1)} %get-tuple-element.89), channel_id=1, source_target_pairs={{0,64},{8,72},{16,80},{24,88},{32,96},{40,104},{48,112},{56,120},{... | collective-permute-start | bytes 1179656 | tf_op jit(solution)/shard_map/ppermute | solution.py:37
  124.0 10.0 %collective-permute-start.20 = (bf16[24,32,256]{2,1,0:T(8,128)(2,1)S(1)}, bf16[24,32,256]{2,1,0:T(8,128)(2,1)S(1)}, u32[]{:S(2)}, u32[]{:S(2)}) collective-permute-start(bf16[24,32,256]{2,1,0:T(8,128)(2,1)S(1)} %get-tuple-element.87), channel_id=1, source_target_pairs={{0,48},{8,56},{16,0},{24,8},{32,16},{40,24},{48,32},{56,40},{64,11... | collective-permute-start | bytes 1179656 | tf_op jit(solution)/shard_map/ppermute | solution.py:37

commit v6 on v5

--- a/solution.py
+++ b/solution.py
@@ -11,7 +11,7 @@
 UNROLL = 12
 HERE = 160
 ROWS = 168
-CUTS = (0, 11, 16)
+CUTS = (0, 12, 16)
 VMEM_BYTES = 14 * 1024 * 1024
 NT = (((1,), (1,)), ((), ()))
 WHOLE = pl.BlockSpec(memory_space=pltpu.VMEM)
@@ -229,7 +229,7 @@
 
         ranged(
             plan_ref[slots + low + 8 * core], plan_ref[slots + high + 8 * core], add,
-            16 if high - low == 4 else UNROLL,
+            UNROLL,
         )
     if final:
         mean = (sum_ref[:blocks] * inv_ref[...]).astype(jnp.bfloat16)

time: 135 us -> 135 us (level)
  Pallas kernels: 31.5 us -> 33.9 us
  starting transfers between devices: 33.6 us -> 31.9 us
    pallas_call x16, Pallas kernels: 31.5 us -> 33.9 us  [call(): pl.pallas_call(kernel, in_specs=[IDLE] * len(lead) + [WHOLE] * len(operan...]
    ppermute x23, starting transfers between devices: 26.8 us -> 25.1 us  [send(): return lax.ppermute(value, 'blk', ROUTES[route])]
  transfers between devices with their start and end apart: 24 -> 24, of which waited for: 8 -> 9; matrix products, arithmetic and copies ran while one was open for 3% -> 3% of each run, Pallas kernels for 16% -> 17%
where the time goes in v6:
time: 135 us
  blocking collectives  37.4 us (28%)
  Pallas kernels  33.9 us (25%)
  starting transfers between devices  31.9 us (24%)
  waiting for transfers between devices  25.8 us (19%)
  other arithmetic  3.76 us (3%)
  between operations  1.64 us (1%)
    all_to_all x2, blocking collectives, over_col(): moved = lax.all_to_all(a.reshape(n_col, rows * cols, width), 'col', 0, 0)  37.4 us
    pallas_call x16, Pallas kernels, call(): pl.pallas_call(kernel, in_specs=[IDLE] * len(lead) + [WHOLE] * len(operan...  33.9 us
    ppermute x23, starting transfers between devices, send(): return lax.ppermute(value, 'blk', ROUTES[route])  25.1 us
    ppermute x23, waiting for transfers between devices, send(): return lax.ppermute(value, 'blk', ROUTES[route])  17.7 us
    all_to_all x1, waiting for transfers between devices, over_col(): moved = lax.all_to_all(a.reshape(n_col, rows * cols, width), 'col', 0, 0)  8.09 us
    all_to_all x1, starting transfers between devices, over_col(): moved = lax.all_to_all(a.reshape(n_col, rows * cols, width), 'col', 0, 0)  6.77 us
  transfers between devices with their start and end apart: 24, of which 9 were waited for; matrix products, arithmetic and copies ran while one was open for 3% of the time, Pallas kernels for 17%

profile of v6, /device:TPU:0, one launch (start us, length us, event | category | flops | bytes accessed | tf_op | source)
XLA Modules:
  0.0 135.1 jit_solution(8005291215090791099)
XLA Ops:
  0.6 4.2 %collective-permute-start.1 = (bf16[24,32,256]{2,1,0:T(8,128)(2,1)}, bf16[24,32,256]{2,1,0:T(8,128)(2,1)S(1)}, u32[]{:S(2)}, u32[]{:S(2)}) collective-permute-start(bf16[24,32,256]{2,1,0:T(8,128)(2,1)} %refs_0_.1), channel_id=1, source_target_pairs={{0,48},{8,56},{16,0},{24,8},{32,16},{40,24},{48,32},{56,40},{64,11... | collective-permute-start | bytes 1179656 | tf_op jit(solution)/shard_map/ppermute | solution.py:37
  4.8 1.6 %collective-permute-start.2 = (bf16[24,32,256]{2,1,0:T(8,128)(2,1)}, bf16[24,32,256]{2,1,0:T(8,128)(2,1)S(1)}, u32[]{:S(2)}, u32[]{:S(2)}) collective-permute-start(bf16[24,32,256]{2,1,0:T(8,128)(2,1)} %refs_0_.1), channel_id=1, source_target_pairs={{0,64},{8,72},{16,80},{24,88},{32,96},{40,104},{48,112},{56,120},{... | collective-permute-start | bytes 1179656 | tf_op jit(solution)/shard_map/ppermute | solution.py:37
  6.4 0.0 collective-permute-start
  6.4 2.1 %pad_maximum_fusion = bf16[8,6,32,256]{3,2,1,0:T(8,128)(2,1)} fusion(bf16[8,3,32,256]{3,2,1,0:T(8,128)(2,1)} %bitcast.37, bf16[8,3,32,256]{3,2,1,0:T(8,128)(2,1)} %bitcast.32), kind=kLoop, calls=%fused_computation | loop fusion | flops 393216 | bytes 1572864 | tf_op jit(solution)/shard_map/concatenate | solution.py:474
  8.5 6.8 %all-to-all-start = ((bf16[8,192,256]{2,1,0:T(8,128)(2,1)}), bf16[8,192,256]{2,1,0:T(8,128)(2,1)S(1)}, u32[]{:S(2)}, u32[]{:S(2)}) async-start(bf16[8,192,256]{2,1,0:T(8,128)(2,1)} %bitcast.5), calls=%async_computation | async-start | bytes 1572864 | tf_op jit(solution)/shard_map/all_to_all | solution.py:464
  16.0 0.2 convert_reduce_fusion
  16.2 0.1 select_reduce_fusion
  16.3 0.2 collective-permute-start.3
  16.6 3.2 %collective-permute-start.5 = (bf16[24,32,256]{2,1,0:T(8,128)(2,1)S(1)}, bf16[24,32,256]{2,1,0:T(8,128)(2,1)S(1)}, u32[]{:S(2)}, u32[]{:S(2)}) collective-permute-start(bf16[24,32,256]{2,1,0:T(8,128)(2,1)S(1)} %collective-permute-done.1.refs_2_), channel_id=1, source_target_pairs={{0,48},{8,56},{16,0},{24,8},{32,16},{40,24},{48,32},{56,40},{64,11... | collective-permute-start | bytes 1179656 | tf_op jit(solution)/shard_map/ppermute | solution.py:37
  19.8 0.0 collective-permute-done.2.refs_3_
  19.8 0.1 convert_reduce_fusion.1
  19.9 0.1 pad_add_fusion.plan_ref
  20.0 1.1 shift-left_add_fusion.refs_0_
  21.1 8.1 %all-to-all-done = bf16[8,192,256]{2,1,0:T(8,128)(2,1)S(1)} async-done(((bf16[8,192,256]{2,1,0:T(8,128)(2,1)}), bf16[8,192,256]{2,1,0:T(8,128)(2,1)S(1)}, u32[]{:S(2)}, u32[]{:S(2)}) %all-to-all-start) | async-done | bytes 786464 | tf_op jit(solution)/shard_map/all_to_all | solution.py:464
  29.2 7.5 %adjacency.2 = (bf16[128,256,256]{2,1,0:T(8,128)(2,1)S(1)}, f32[25,8,256]{2,1,0:T(8,128)S(1)}) custom-call(s32[296]{0:T(512)S(1)} %pad_add_fusion.plan_ref, s32[128,640]{1,0:T(8,128)S(1)} %shift-left_add_fusion.refs_0_, bf16[8,6,32,256]{3,2,1,0:T(8,128)(2,1)S(1)} %bitcast.30), custom_call_target="tpu_custom_call" | custom-call | tf_op jit(solution)/shard_map/adjacency/pallas_call | solution.py:55
  36.7 0.0 copy-start.1
  36.7 0.0 copy-start.2
  36.8 0.0 collective-permute-done.3.refs_4_
  36.8 0.0 collective-permute-done.5.refs_6_
  36.8 1.3 join.2
  38.1 0.1 collective-permute-start.8
  38.2 0.5 collective-permute-start.10
  38.7 0.0 collective-permute-start.6
  38.7 3.2 %collective-permute-start.7 = (bf16[12,32,256]{2,1,0:T(8,128)(2,1)S(1)}, bf16[12,32,256]{2,1,0:T(8,128)(2,1)S(1)}, u32[]{:S(2)}, u32[]{:S(2)}) collective-permute-start(bf16[12,32,256]{2,1,0:T(8,128)(2,1)S(1)} %get-tuple-element.54), channel_id=1, source_target_pairs={{0,48},{8,56},{16,0},{24,8},{32,16},{40,24},{48,32},{56,40},{64,11... | collective-permute-start | bytes 589832 | tf_op jit(solution)/shard_map/ppermute | solution.py:37
  42.0 3.0 %adjacency.3 = (bf16[128,256,256]{2,1,0:T(8,128)(2,1)S(1)}, f32[25,8,256]{2,1,0:T(8,128)S(1)}, f32[24,1,256]{2,1,0:T(1,128)S(1)}) custom-call(s32[296]{0:T(512)S(1)} %pad_add_fusion.plan_ref, s32[128,640]{1,0:T(8,128)S(1)} %shift-left_add_fusion.refs_0_, ...), custom_call_target="tpu_custom_call", output_to_operand_aliasing={{0}: (2, {}), {1}: (3, {})} | custom-call | tf_op jit(solution)/shard_map/adjacency/pallas_call | solution.py:55
  44.9 0.0 collective-permute-done.8.refs_3_
  44.9 3.0 %neighbor_mean.3 = (f32[25,32,256]{2,1,0:T(8,128)S(1)}, bf16[4,256,256]{2,1,0:T(8,128)(2,1)S(1)}) custom-call(s32[296]{0:T(512)S(1)} %pad_add_fusion.plan_ref, bf16[128,256,256]{2,1,0:T(8,128)(2,1)S(1)} %get-tuple-element.52.refs_0_.refs_4_, bf16[2,256,256]{2,1,0:T(8,128)(2,1)S(1)} %pad_maximum_fusion.1.refs_1_, ...), custom_call_target="tpu_custom_call" | custom-call | tf_op jit(solution)/shard_map/neighbor_mean/pallas_call | solution.py:55
  47.9 0.0 collective-permute-done.6.one_ref
  47.9 0.0 collective-permute-done.7.two_ref
  48.0 0.1 collective-permute-start.9
  48.1 2.6 %neighbor_mean.4.refs_3_ = f32[25,32,256]{2,1,0:T(8,128)S(1)} custom-call(s32[296]{0:T(512)S(1)} %pad_add_fusion.plan_ref, bf16[128,256,256]{2,1,0:T(8,128)(2,1)S(1)} %get-tuple-element.52.refs_0_.refs_4_, bf16[72,32,256]{2,1,0:T(8,128)(2,1)S(1)} %get-tuple-element.56.refs_4_.refs_1_, ...), custom_call_target="tpu_custom_call", output_to_operand_aliasing={{}: (4, {})} | custom-call | tf_op jit(solution)/shard_map/neighbor_mean/pallas_call | solution.py:55
  50.6 1.4 %neighbor_mean.5 = (f32[25,32,256]{2,1,0:T(8,128)S(1)}, bf16[8,3,32,256]{3,2,1,0:T(8,128)(2,1)S(1)}) custom-call(s32[296]{0:T(512)S(1)} %pad_add_fusion.plan_ref, bf16[128,256,256]{2,1,0:T(8,128)(2,1)S(1)} %get-tuple-element.52.refs_0_.refs_4_, bf16[24,32,256]{2,1,0:T(8,128)(2,1)S(1)} %get-tuple-element.58.refs_1_, ...), custom_call_target="tpu_custom_call", output_to_operand_aliasing={{0}: (4, {})} | custom-call | tf_op jit(solution)/shard_map/neighbor_mean/pallas_call | solution.py:55
  52.1 13.7 %all_to_all.15 = bf16[8,96,256]{2,1,0:T(8,128)(2,1)S(1)} all-to-all(bf16[8,96,256]{2,1,0:T(8,128)(2,1)S(1)} %bitcast.35), channel_id=1, replica_groups=mesh['blk'=16,'col'=8] {'col'}, dimensions={0} | all-to-all | bytes 786432 | tf_op jit(solution)/shard_map/all_to_all | solution.py:464
  65.8 2.0 %dense.1 = (bf16[8,11,32,256]{3,2,1,0:T(8,128)(2,1)S(1)}, bf16[128,256,256]{2,1,0:T(8,128)(2,1)S(1)}) custom-call(s32[296]{0:T(512)S(1)} %pad_add_fusion.plan_ref, bf16[8,3,32,256]{3,2,1,0:T(8,128)(2,1)S(1)} %bitcast.33, bf16[8,6,32,256]{3,2,1,0:T(8,128)(2,1)S(1)} %bitcast.31, ...), custom_call_target="tpu_custom_call", output_to_operand_aliasing={{1}: (5, {})} | custom-call | tf_op jit(solution)/shard_map/dense/pallas_call | solution.py:55
  67.8 23.7 %all_to_all.16 = bf16[8,352,256]{2,1,0:T(8,128)(2,1)S(1)} all-to-all(bf16[8,352,256]{2,1,0:T(8,128)(2,1)S(1)} %bitcast.34), channel_id=1, replica_groups=mesh['blk'=16,'col'=8] {'col'}, dimensions={0} | all-to-all | bytes 2883584 | tf_op jit(solution)/shard_map/all_to_all | solution.py:464
  91.5 1.3 sums_far_swap.1
  92.7 0.1 collective-permute-start.11
  92.8 1.9 %sums_mid_swap.1 = (bf16[128,256,256]{2,1,0:T(8,128)(2,1)S(1)}, bf16[72,32,256]{2,1,0:T(8,128)(2,1)S(1)}) custom-call(s32[296]{0:T(512)S(1)} %pad_add_fusion.plan_ref, bf16[88,32,256]{2,1,0:T(8,128)(2,1)S(1)} %bitcast.23, bf16[128,256,256]{2,1,0:T(8,128)(2,1)S(1)} %get-tuple-element.65.refs_1_), custom_call_target="tpu_custom_call", output_to_operand_aliasing={{0}: (2, {})} | custom-call | tf_op jit(solution)/shard_map/sums_mid_swap/pallas_call | solution.py:55
  94.7 1.2 sums_far_own.1
  96.0 1.2 collective-permute-start.12
  97.1 0.3 collective-permute-start.13
  97.4 1.5 %collective-permute-start.14 = (bf16[8,32,256]{2,1,0:T(8,128)(2,1)S(1)}, bf16[8,32,256]{2,1,0:T(8,128)(2,1)S(1)}, u32[]{:S(2)}, u32[]{:S(2)}) collective-permute-start(bf16[8,32,256]{2,1,0:T(8,128)(2,1)S(1)} %get-tuple-element.74), channel_id=1, source_target_pairs={{0,48},{8,56},{16,0},{24,8},{32,16},{40,24},{48,32},{56,40},{64,11... | collective-permute-start | bytes 393224 | tf_op jit(solution)/shard_map/ppermute | solution.py:37
  98.9 0.6 collective-permute-start.15
  99.4 3.1 %sums_near_swap.1 = (bf16[128,256,256]{2,1,0:T(8,128)(2,1)S(1)}, bf16[96,32,256]{2,1,0:T(8,128)(2,1)S(1)}) custom-call(s32[296]{0:T(512)S(1)} %pad_add_fusion.plan_ref, bf16[88,32,256]{2,1,0:T(8,128)(2,1)S(1)} %bitcast.25, bf16[128,256,256]{2,1,0:T(8,128)(2,1)S(1)} %get-tuple-element.70.refs_1_), custom_call_target="tpu_custom_call", output_to_operand_aliasing={{0}: (2, {})} | custom-call | tf_op jit(solution)/shard_map/sums_near_swap/pallas_call | solution.py:55
  102.6 0.4 collective-permute-done.14.refs_4_
  103.0 2.4 %collective-permute-done.15.refs_5_ = bf16[8,32,256]{2,1,0:T(8,128)(2,1)S(1)} collective-permute-done((bf16[8,32,256]{2,1,0:T(8,128)(2,1)S(1)}, bf16[8,32,256]{2,1,0:T(8,128)(2,1)S(1)}, u32[]{:S(2)}, u32[]{:S(2)}) %collective-permute-start.15) | collective-permute-done | bytes 131104 | tf_op jit(solution)/shard_map/ppermute | solution.py:37
  105.3 2.5 %sums_mid_own.1 = (bf16[128,256,256]{2,1,0:T(8,128)(2,1)S(1)}, bf16[24,32,256]{2,1,0:T(8,128)(2,1)S(1)}, bf16[26,32,256]{2,1,0:T(8,128)(2,1)S(1)}, bf16[26,32,25...) custom-call(s32[296]{0:T(512)S(1)} %pad_add_fusion.plan_ref, ...), custom_call_target="tpu_custom_call", output_to_operand_aliasing={{0}: (2, {}), {5}: (9, {})} | custom-call | tf_op jit(solution)/shard_map/sums_mid_own/pallas_call | solution.py:55
  107.8 0.1 collective-permute-start.16
  107.9 0.1 collective-permute-start.18
  108.0 2.0 %collective-permute-start.19 = (bf16[26,32,256]{2,1,0:T(8,128)(2,1)S(1)}, bf16[26,32,256]{2,1,0:T(8,128)(2,1)S(1)}, u32[]{:S(2)}, u32[]{:S(2)}) collective-permute-start(bf16[26,32,256]{2,1,0:T(8,128)(2,1)S(1)} %get-tuple-element.84), channel_id=1, source_target_pairs={{0,16},{8,24},{16,32},{24,40},{32,48},{40,56},{48,0},{56,8},{64,80... | collective-permute-start | bytes 1277960 | tf_op jit(solution)/shard_map/ppermute | solution.py:37
  110.0 1.2 collective-permute-start.17
  111.2 0.1 collective-permute-done.16.refs_2_
  111.3 2.0 %sums_near_own.1 = (bf16[128,256,256]{2,1,0:T(8,128)(2,1)S(1)}, f32[24,32,256]{2,1,0:T(8,128)S(1)}, bf16[24,32,256]{2,1,0:T(8,128)(2,1)S(1)}, f32[24,32,256]{2,1,0:T(8,128)S(1)}, f32[24,32,256]{2,1,0:T(8,128)S(1)}) custom-call(s32[296]{0:T(512)S(1)} %pad_add_fusion.plan_ref, bf16[88,32,256]{2,1,0:T(8,128)(2,1)S(1)} %bitcast.27, ...), custom_call_target="tpu_custom_call", output_to_operand_aliasing={{0}: (2, {})} | custom-call | tf_op jit(solution)/shard_map/sums_near_own/pallas_call | solution.py:55
  113.3 7.6 %collective-permute-done.17.y_more_ref = bf16[24,32,256]{2,1,0:T(8,128)(2,1)S(1)} collective-permute-done((bf16[24,32,256]{2,1,0:T(8,128)(2,1)S(1)}, bf16[24,32,256]{2,1,0:T(8,128)(2,1)S(1)}, u32[]{:S(2)}, u32[]{:S(2)}) %collective-permute-start.17) | collective-permute-done | bytes 393248 | tf_op jit(solution)/shard_map/ppermute | solution.py:37
  120.9 0.4 collective-permute-done.19.z_two_ref.up_ref
  121.4 0.3 relay.1
  121.6 0.6 collective-permute-start.21
  122.3 1.3 collective-permute-start.22
  123.6 3.1 %collective-permute-start.20 = (bf16[24,32,256]{2,1,0:T(8,128)(2,1)S(1)}, bf16[24,32,256]{2,1,0:T(8,128)(2,1)S(1)}, u32[]{:S(2)}, u32[]{:S(2)}) collective-permute-start(bf16[24,32,256]{2,1,0:T(8,128)(2,1)S(1)} %get-tuple-element.87), channel_id=1, source_target_pairs={{0,48},{8,56},{16,0},{24,8},{32,16},{40,24},{48,32},{56,40},{64,11... | collective-permute-start | bytes 1179656 | tf_op jit(solution)/shard_map/ppermute | solution.py:37
  126.7 0.8 slice.4
  127.5 4.9 %collective-permute-done.22.over_ref = bf16[24,32,256]{2,1,0:T(8,128)(2,1)S(1)} collective-permute-done((bf16[24,32,256]{2,1,0:T(8,128)(2,1)S(1)}, bf16[24,32,256]{2,1,0:T(8,128)(2,1)S(1)}, u32[]{:S(2)}, u32[]{:S(2)}) %collective-permute-start.22) | collective-permute-done | bytes 393248 | tf_op jit(solution)/shard_map/ppermute | solution.py:37
  132.4 1.7 %collective-permute-done.20.less_ref = bf16[24,32,256]{2,1,0:T(8,128)(2,1)S(1)} collective-permute-done((bf16[24,32,256]{2,1,0:T(8,128)(2,1)S(1)}, bf16[24,32,256]{2,1,0:T(8,128)(2,1)S(1)}, u32[]{:S(2)}, u32[]{:S(2)}) %collective-permute-start.20) | collective-permute-done | bytes 393248 | tf_op jit(solution)/shard_map/ppermute | solution.py:37
  134.0 0.2 collective-permute-done.21.more_ref
  134.2 0.9 finish.1
  (26 shorter events, 0.1 us)
Async XLA Ops:
  0.6 15.7 %collective-permute-start.1 = (bf16[24,32,256]{2,1,0:T(8,128)(2,1)}, bf16[24,32,256]{2,1,0:T(8,128)(2,1)S(1)}, u32[]{:S(2)}, u32[]{:S(2)}) collective-permute-start(bf16[24,32,256]{2,1,0:T(8,128)(2,1)} %refs_0_.1), channel_id=1, source_target_pairs={{0,48},{8,56},{16,0},{24,8},{32,16},{40,24},{48,32},{56,40},{64,11... | collective-permute-start | bytes 1179656 | tf_op jit(solution)/shard_map/ppermute | solution.py:37
  4.8 15.0 %collective-permute-start.2 = (bf16[24,32,256]{2,1,0:T(8,128)(2,1)}, bf16[24,32,256]{2,1,0:T(8,128)(2,1)S(1)}, u32[]{:S(2)}, u32[]{:S(2)}) collective-permute-start(bf16[24,32,256]{2,1,0:T(8,128)(2,1)} %refs_0_.1), channel_id=1, source_target_pairs={{0,64},{8,72},{16,80},{24,88},{32,96},{40,104},{48,112},{56,120},{... | collective-permute-start | bytes 1179656 | tf_op jit(solution)/shard_map/ppermute | solution.py:37
  6.4 30.4 %collective-permute-start = (bf16[24,32,256]{2,1,0:T(8,128)(2,1)}, bf16[24,32,256]{2,1,0:T(8,128)(2,1)S(1)}, u32[]{:S(2)}, u32[]{:S(2)}) collective-permute-start(bf16[24,32,256]{2,1,0:T(8,128)(2,1)} %refs_0_.1), channel_id=1, source_target_pairs={{0,16},{8,24},{16,32},{24,40},{32,48},{40,56},{48,0},{56,8},{64,80... | collective-permute-start | bytes 1179656 | tf_op jit(solution)/shard_map/ppermute | solution.py:37
  6.4 9.5 %copy-start.3 = (s32[128,1]{0,1:T(1,128)S(1)}, s32[128,1]{0,1:T(1,128)}, u32[]{:S(2)}) copy-start(s32[128,1]{0,1:T(1,128)} %param.15) | copy-start | bytes 1540
  6.4 9.6 %copy-start.4 = (s32[128]{0:T(128)S(1)}, s32[128]{0:T(128)}, u32[]{:S(2)}) copy-start(s32[128]{0:T(128)} %param.14) | copy-start | bytes 1540
  6.4 9.6 %copy-start.5 = (s32[128]{0:T(128)S(1)}, s32[128]{0:T(128)}, u32[]{:S(2)}) copy-start(s32[128]{0:T(128)} %param.16) | copy-start | bytes 1540
  8.5 28.3 %copy-start = (bf16[24,32,256]{2,1,0:T(8,128)(2,1)S(1)}, bf16[24,32,256]{2,1,0:T(8,128)(2,1)}, u32[]{:S(2)}) copy-start(bf16[24,32,256]{2,1,0:T(8,128)(2,1)} %refs_0_.1) | copy-start | bytes 1179652
  8.5 20.7 %all-to-all-start = ((bf16[8,192,256]{2,1,0:T(8,128)(2,1)}), bf16[8,192,256]{2,1,0:T(8,128)(2,1)S(1)}, u32[]{:S(2)}, u32[]{:S(2)}) async-start(bf16[8,192,256]{2,1,0:T(8,128)(2,1)} %bitcast.5), calls=%async_computation | async-start | bytes 1572864 | tf_op jit(solution)/shard_map/all_to_all | solution.py:464
  16.3 20.4 %collective-permute-start.3 = (bf16[24,32,256]{2,1,0:T(8,128)(2,1)S(1)}, bf16[24,32,256]{2,1,0:T(8,128)(2,1)S(1)}, u32[]{:S(2)}, u32[]{:S(2)}) collective-permute-start(bf16[24,32,256]{2,1,0:T(8,128)(2,1)S(1)} %collective-permute-done.1.refs_2_), channel_id=1, source_target_pairs={{0,64},{8,72},{16,80},{24,88},{32,96},{40,104},{48,112},{56,120},{... | collective-permute-start | bytes 1179656 | tf_op jit(solution)/shard_map/ppermute | solution.py:37
  16.6 20.2 %collective-permute-start.5 = (bf16[24,32,256]{2,1,0:T(8,128)(2,1)S(1)}, bf16[24,32,256]{2,1,0:T(8,128)(2,1)S(1)}, u32[]{:S(2)}, u32[]{:S(2)}) collective-permute-start(bf16[24,32,256]{2,1,0:T(8,128)(2,1)S(1)} %collective-permute-done.1.refs_2_), channel_id=1, source_target_pairs={{0,48},{8,56},{16,0},{24,8},{32,16},{40,24},{48,32},{56,40},{64,11... | collective-permute-start | bytes 1179656 | tf_op jit(solution)/shard_map/ppermute | solution.py:37
  19.8 17.0 %collective-permute-start.4 = (bf16[24,32,256]{2,1,0:T(8,128)(2,1)S(1)}, bf16[24,32,256]{2,1,0:T(8,128)(2,1)}, u32[]{:S(2)}, u32[]{:S(2)}) collective-permute-start(bf16[24,32,256]{2,1,0:T(8,128)(2,1)S(1)} %collective-permute-done.2.refs_3_), channel_id=1, source_target_pairs={{0,16},{8,24},{16,32},{24,40},{32,48},{40,56},{48,0},{56,8},{64,80... | collective-permute-start | bytes 1179656 | tf_op jit(solution)/shard_map/ppermute | solution.py:37
  36.7 5.2 %copy-start.1 = (bf16[256,256]{1,0:T(8,128)(2,1)S(1)}, bf16[256,256]{1,0:T(8,128)(2,1)}, u32[]{:S(2)}) copy-start(bf16[256,256]{1,0:T(8,128)(2,1)} %param.13) | copy-start | bytes 393220
  36.7 5.2 %copy-start.2 = (bf16[256,256]{1,0:T(8,128)(2,1)S(1)}, bf16[256,256]{1,0:T(8,128)(2,1)}, u32[]{:S(2)}) copy-start(bf16[256,256]{1,0:T(8,128)(2,1)} %param.12) | copy-start | bytes 393220
  38.1 6.8 %collective-permute-start.8 = (bf16[96,32,256]{2,1,0:T(8,128)(2,1)S(1)}, bf16[96,32,256]{2,1,0:T(8,128)(2,1)S(1)}, u32[]{:S(2)}, u32[]{:S(2)}) collective-permute-start(bf16[96,32,256]{2,1,0:T(8,128)(2,1)S(1)} %get-tuple-element.55.refs_2_), channel_id=1, source_target_pairs={{0,8},{8,0},{16,24},{24,16},{32,40},{40,32},{48,56},{56,48},{64,72... | collective-permute-start | bytes 4718600 | tf_op jit(solution)/shard_map/ppermute | solution.py:37
  38.2 9.9 %collective-permute-start.10 = (bf16[72,32,256]{2,1,0:T(8,128)(2,1)S(1)}, bf16[72,32,256]{2,1,0:T(8,128)(2,1)S(1)}, u32[]{:S(2)}, u32[]{:S(2)}) collective-permute-start(bf16[72,32,256]{2,1,0:T(8,128)(2,1)S(1)} %get-tuple-element.56.refs_4_.refs_1_), channel_id=1, source_target_pairs={{0,8},{8,0},{16,24},{24,16},{32,40},{40,32},{48,56},{56,48},{64,72... | collective-permute-start | bytes 3538952 | tf_op jit(solution)/shard_map/ppermute | solution.py:37
  38.7 9.2 %collective-permute-start.6 = (bf16[12,32,256]{2,1,0:T(8,128)(2,1)S(1)}, bf16[12,32,256]{2,1,0:T(8,128)(2,1)S(1)}, u32[]{:S(2)}, u32[]{:S(2)}) collective-permute-start(bf16[12,32,256]{2,1,0:T(8,128)(2,1)S(1)} %get-tuple-element.53), channel_id=1, source_target_pairs={{0,16},{8,24},{16,32},{24,40},{32,48},{40,56},{48,0},{56,8},{64,80... | collective-permute-start | bytes 589832 | tf_op jit(solution)/shard_map/ppermute | solution.py:37
  38.7 9.2 %collective-permute-start.7 = (bf16[12,32,256]{2,1,0:T(8,128)(2,1)S(1)}, bf16[12,32,256]{2,1,0:T(8,128)(2,1)S(1)}, u32[]{:S(2)}, u32[]{:S(2)}) collective-permute-start(bf16[12,32,256]{2,1,0:T(8,128)(2,1)S(1)} %get-tuple-element.54), channel_id=1, source_target_pairs={{0,48},{8,56},{16,0},{24,8},{32,16},{40,24},{48,32},{56,40},{64,11... | collective-permute-start | bytes 589832 | tf_op jit(solution)/shard_map/ppermute | solution.py:37
  48.0 2.7 %collective-permute-start.9 = (bf16[24,32,256]{2,1,0:T(8,128)(2,1)S(1)}, bf16[24,32,256]{2,1,0:T(8,128)(2,1)S(1)}, u32[]{:S(2)}, u32[]{:S(2)}) collective-permute-start(bf16[24,32,256]{2,1,0:T(8,128)(2,1)S(1)} %get-tuple-element.58.refs_1_), channel_id=1, source_target_pairs={{0,8},{8,0},{16,24},{24,16},{32,40},{40,32},{48,56},{56,48},{64,72... | collective-permute-start | bytes 1179656 | tf_op jit(solution)/shard_map/ppermute | solution.py:37
  92.7 2.0 %collective-permute-start.11 = (bf16[26,32,256]{2,1,0:T(8,128)(2,1)S(1)}, bf16[26,32,256]{2,1,0:T(8,128)(2,1)S(1)}, u32[]{:S(2)}, u32[]{:S(2)}) collective-permute-start(bf16[26,32,256]{2,1,0:T(8,128)(2,1)S(1)} %get-tuple-element.67), channel_id=1, source_target_pairs={{0,8},{8,0},{16,24},{24,16},{32,40},{40,32},{48,56},{56,48},{64,72... | collective-permute-start | bytes 1277960 | tf_op jit(solution)/shard_map/ppermute | solution.py:37
  96.0 9.4 %collective-permute-start.12 = (bf16[72,32,256]{2,1,0:T(8,128)(2,1)S(1)}, bf16[72,32,256]{2,1,0:T(8,128)(2,1)S(1)}, u32[]{:S(2)}, u32[]{:S(2)}) collective-permute-start(bf16[72,32,256]{2,1,0:T(8,128)(2,1)S(1)} %get-tuple-element.72), channel_id=1, source_target_pairs={{0,8},{8,0},{16,24},{24,16},{32,40},{40,32},{48,56},{56,48},{64,72... | collective-permute-start | bytes 3538952 | tf_op jit(solution)/shard_map/ppermute | solution.py:37
  97.1 8.2 %collective-permute-start.13 = (bf16[10,32,256]{2,1,0:T(8,128)(2,1)S(1)}, bf16[10,32,256]{2,1,0:T(8,128)(2,1)S(1)}, u32[]{:S(2)}, u32[]{:S(2)}) collective-permute-start(bf16[10,32,256]{2,1,0:T(8,128)(2,1)S(1)} %get-tuple-element.73), channel_id=1, source_target_pairs={{0,64},{8,72},{16,80},{24,88},{32,96},{40,104},{48,112},{56,120},{... | collective-permute-start | bytes 491528 | tf_op jit(solution)/shard_map/ppermute | solution.py:37
  97.4 5.6 %collective-permute-start.14 = (bf16[8,32,256]{2,1,0:T(8,128)(2,1)S(1)}, bf16[8,32,256]{2,1,0:T(8,128)(2,1)S(1)}, u32[]{:S(2)}, u32[]{:S(2)}) collective-permute-start(bf16[8,32,256]{2,1,0:T(8,128)(2,1)S(1)} %get-tuple-element.74), channel_id=1, source_target_pairs={{0,48},{8,56},{16,0},{24,8},{32,16},{40,24},{48,32},{56,40},{64,11... | collective-permute-start | bytes 393224 | tf_op jit(solution)/shard_map/ppermute | solution.py:37
  98.9 6.4 %collective-permute-start.15 = (bf16[8,32,256]{2,1,0:T(8,128)(2,1)S(1)}, bf16[8,32,256]{2,1,0:T(8,128)(2,1)S(1)}, u32[]{:S(2)}, u32[]{:S(2)}) collective-permute-start(bf16[8,32,256]{2,1,0:T(8,128)(2,1)S(1)} %get-tuple-element.75), channel_id=1, source_target_pairs={{0,16},{8,24},{16,32},{24,40},{32,48},{40,56},{48,0},{56,8},{64,80... | collective-permute-start | bytes 393224 | tf_op jit(solution)/shard_map/ppermute | solution.py:37
  107.8 3.5 %collective-permute-start.16 = (bf16[96,32,256]{2,1,0:T(8,128)(2,1)S(1)}, bf16[96,32,256]{2,1,0:T(8,128)(2,1)S(1)}, u32[]{:S(2)}, u32[]{:S(2)}) collective-permute-start(bf16[96,32,256]{2,1,0:T(8,128)(2,1)S(1)} %get-tuple-element.79), channel_id=1, source_target_pairs={{0,8},{8,0},{16,24},{24,16},{32,40},{40,32},{48,56},{56,48},{64,72... | collective-permute-start | bytes 4718600 | tf_op jit(solution)/shard_map/ppermute | solution.py:37
  107.9 13.0 %collective-permute-start.18 = (bf16[26,32,256]{2,1,0:T(8,128)(2,1)S(1)}, bf16[26,32,256]{2,1,0:T(8,128)(2,1)S(1)}, u32[]{:S(2)}, u32[]{:S(2)}) collective-permute-start(bf16[26,32,256]{2,1,0:T(8,128)(2,1)S(1)} %get-tuple-element.83), channel_id=1, source_target_pairs={{0,48},{8,56},{16,0},{24,8},{32,16},{40,24},{48,32},{56,40},{64,11... | collective-permute-start | bytes 1277960 | tf_op jit(solution)/shard_map/ppermute | solution.py:37
  108.0 13.3 %collective-permute-start.19 = (bf16[26,32,256]{2,1,0:T(8,128)(2,1)S(1)}, bf16[26,32,256]{2,1,0:T(8,128)(2,1)S(1)}, u32[]{:S(2)}, u32[]{:S(2)}) collective-permute-start(bf16[26,32,256]{2,1,0:T(8,128)(2,1)S(1)} %get-tuple-element.84), channel_id=1, source_target_pairs={{0,16},{8,24},{16,32},{24,40},{32,48},{40,56},{48,0},{56,8},{64,80... | collective-permute-start | bytes 1277960 | tf_op jit(solution)/shard_map/ppermute | solution.py:37
  110.0 10.9 %collective-permute-start.17 = (bf16[24,32,256]{2,1,0:T(8,128)(2,1)S(1)}, bf16[24,32,256]{2,1,0:T(8,128)(2,1)S(1)}, u32[]{:S(2)}, u32[]{:S(2)}) collective-permute-start(bf16[24,32,256]{2,1,0:T(8,128)(2,1)S(1)} %get-tuple-element.82), channel_id=1, source_target_pairs={{0,64},{8,72},{16,80},{24,88},{32,96},{40,104},{48,112},{56,120},{... | collective-permute-start | bytes 1179656 | tf_op jit(solution)/shard_map/ppermute | solution.py:37
  121.6 12.5 %collective-permute-start.21 = (bf16[26,32,256]{2,1,0:T(8,128)(2,1)S(1)}, bf16[26,32,256]{2,1,0:T(8,128)(2,1)S(1)}, u32[]{:S(2)}, u32[]{:S(2)}) collective-permute-start(bf16[26,32,256]{2,1,0:T(8,128)(2,1)S(1)} %get-tuple-element.88), channel_id=1, source_target_pairs={{0,16},{8,24},{16,32},{24,40},{32,48},{40,56},{48,0},{56,8},{64,80... | collective-permute-start | bytes 1277960 | tf_op jit(solution)/shard_map/ppermute | solution.py:37
  122.3 10.1 %collective-permute-start.22 = (bf16[24,32,256]{2,1,0:T(8,128)(2,1)S(1)}, bf16[24,32,256]{2,1,0:T(8,128)(2,1)S(1)}, u32[]{:S(2)}, u32[]{:S(2)}) collective-permute-start(bf16[24,32,256]{2,1,0:T(8,128)(2,1)S(1)} %get-tuple-element.89), channel_id=1, source_target_pairs={{0,64},{8,72},{16,80},{24,88},{32,96},{40,104},{48,112},{56,120},{... | collective-permute-start | bytes 1179656 | tf_op jit(solution)/shard_map/ppermute | solution.py:37
  123.6 10.5 %collective-permute-start.20 = (bf16[24,32,256]{2,1,0:T(8,128)(2,1)S(1)}, bf16[24,32,256]{2,1,0:T(8,128)(2,1)S(1)}, u32[]{:S(2)}, u32[]{:S(2)}) collective-permute-start(bf16[24,32,256]{2,1,0:T(8,128)(2,1)S(1)} %get-tuple-element.87), channel_id=1, source_target_pairs={{0,48},{8,56},{16,0},{24,8},{32,16},{40,24},{48,32},{56,40},{64,11... | collective-permute-start | bytes 1179656 | tf_op jit(solution)/shard_map/ppermute | solution.py:37
